TPU v7x, 256 devices: a whole 4x4x8 slice. The times are simulated.
256 devices in a mesh: row: 8 (over x, y_lo), col: 32 (over z, y_hi, core).
Axes of the slice: x: 4, y: 4 (y_hi: 2, y_lo: 2; y = y_hi * 2 + y_lo), z: 8, core: 2. Of those that a mesh axis runs over, the one named last changes fastest.
Arguments:
- patterns: float32 [16, 64, 256, 256], P('row', 'col'), may hold values from 0.05 to 4
- background: float32 [256, 256], replicated, may hold values from 0.05 to 0.6
- offsets: int32 [16, 64, 2], P('row', 'col'), may hold values from 0 to 64
- probe_wave: float32 [2, 256, 256], replicated, may hold values from -21 to 21
- object_field: float32 [2, 1024, 4096], P(None, 'row', 'col'), may hold values from -15 to 15
Outputs:
- new_object: float32 [2, 1024, 4096], P(None, 'row', 'col')
- new_probe: float32 [2, 256, 256], replicated
All inputs are finite; a program needn't handle non-finite values.
Results may differ from a plain program's by a relative error of at most 0.0085.
The roundings to bfloat16 on the way count: a program that leaves them out, or rounds other values in their place, can miss the bound.
Values sent between devices are 32-bit elements; how exact they have to be, the bound alone decides.
No kernel may reach another device: no remote copies, remote signals or barrier semaphores. Data moves between devices by JAX's collectives and lax.ppermute only.
A program may use at most 64 MiB of HBM per device.

v0:
```python
import math

import jax
import jax.numpy as jnp
from jax import lax
from jax.sharding import PartitionSpec as P

STEP = 64
ITERS = 2


def extended(shard, sides, width):
    for axis, dim in sides:
        count, length = (lax.axis_size(axis), shard.shape[dim])
        up = [(i, (i + 1) % count) for i in range(count - 1)]
        down = [(j, i) for i, j in up]
        last = lax.slice_in_dim(shard, length - width, length, axis=dim)
        first = lax.slice_in_dim(shard, 0, width, axis=dim)
        before = lax.ppermute(last, axis, up)
        after = lax.ppermute(first, axis, down)
        shard = jnp.concatenate([before, shard, after], axis=dim)
    return shard


def dft_tables(side_len):
    indices = jnp.arange(side_len, dtype=jnp.int32)
    phases = indices[:, None] * indices[None, :] % side_len
    angles = phases.astype(jnp.float32) * jnp.float32(2.0 * math.pi / side_len)
    scaling = jnp.float32(1.0 / math.sqrt(side_len))
    return (
        (jnp.cos(angles) * scaling).astype(jnp.bfloat16),
        (-jnp.sin(angles) * scaling).astype(jnp.bfloat16),
    )


def block_tables(real_part, imag_part):
    left_table = jnp.stack([jnp.stack([real_part, -imag_part]), jnp.stack([imag_part, real_part])])
    right_table = jnp.stack([jnp.stack([real_part, imag_part]), jnp.stack([-imag_part, real_part])])
    return (left_table, right_table)


def product(leading, trailing):
    real_part = (
        leading[..., 0, :, :] * trailing[..., 0, :, :]
        - leading[..., 1, :, :] * trailing[..., 1, :, :]
    )
    imag_part = (
        leading[..., 0, :, :] * trailing[..., 1, :, :]
        + leading[..., 1, :, :] * trailing[..., 0, :, :]
    )
    return jnp.stack([real_part, imag_part], axis=-3)


def times_conj(leading, trailing):
    real_part = (
        leading[..., 0, :, :] * trailing[..., 0, :, :]
        + leading[..., 1, :, :] * trailing[..., 1, :, :]
    )
    imag_part = (
        leading[..., 0, :, :] * trailing[..., 1, :, :]
        - leading[..., 1, :, :] * trailing[..., 0, :, :]
    )
    return jnp.stack([real_part, imag_part], axis=-3)


def transform(wave_set, left_table, right_table):
    half_way = jnp.einsum(
        "cdkj,pdjn->pckn", left_table, wave_set, preferred_element_type=jnp.float32
    ).astype(jnp.bfloat16)
    return jnp.einsum("pckn,cdnm->pdkm", half_way, right_table, preferred_element_type=jnp.float32)


def fold_edges(intersection, margin):
    col_rims = jnp.concatenate([intersection[:, :, :margin], intersection[:, :, -margin:]], axis=2)
    col_got = extended(col_rims, (("col", 2),), margin)
    middle = intersection[:, :, margin:-margin]
    middle = middle.at[:, :, :margin].add(col_got[:, :, :margin])
    middle = middle.at[:, :, -margin:].add(col_got[:, :, -margin:])
    row_rims = jnp.concatenate([middle[:, :margin], middle[:, -margin:]], axis=1)
    row_got = extended(row_rims, (("row", 1),), margin)
    centre = middle[:, margin:-margin]
    centre = centre.at[:, :margin].add(row_got[:, :margin])
    centre = centre.at[:, -margin:].add(row_got[:, -margin:])
    return centre


def on_device(patterns, background, offsets, probe_wave, object_field):
    side_len = probe_wave.shape[-1]
    margin = side_len // 2
    pos_rows = patterns.shape[0]
    pos_cols = patterns.shape[1]
    pos_count = pos_rows * pos_cols
    channel_zero = jnp.int32(0)
    real_part, imag_part = dft_tables(side_len)
    forward = block_tables(real_part, imag_part)
    inverse = block_tables(real_part, -imag_part)
    start_rows = (jnp.arange(pos_rows, dtype=jnp.int32)[:, None] * STEP + offsets[:, :, 0]).reshape(
        pos_count
    )
    start_cols = (jnp.arange(pos_cols, dtype=jnp.int32)[None, :] * STEP + offsets[:, :, 1]).reshape(
        pos_count
    )
    amplitude = jnp.sqrt(
        jnp.maximum(patterns.reshape(pos_count, side_len, side_len) - background, 0.0)
    )
    for step_number in range(ITERS):
        widened = extended(object_field, (("row", 1), ("col", 2)), margin)

        def cut_window(row_start, col_start):
            return lax.dynamic_slice(
                widened, (channel_zero, row_start, col_start), (2, side_len, side_len)
            )

        windows = jax.vmap(cut_window)(start_rows, start_cols)
        exit_wave = product(probe_wave, windows)
        far_field = transform(exit_wave.astype(jnp.bfloat16), forward[0], forward[1])
        magnitude = jnp.sqrt(far_field[:, 0] * far_field[:, 0] + far_field[:, 1] * far_field[:, 1])
        projected = (far_field * (amplitude / jnp.maximum(magnitude, 0.5))[:, None]).astype(
            jnp.bfloat16
        )
        back_wave = transform(projected, inverse[0], inverse[1])
        difference = back_wave - exit_wave
        object_terms = times_conj(probe_wave, difference)
        probe_terms = jnp.sum(times_conj(windows, difference), axis=0)
        illumination = probe_wave[0] * probe_wave[0] + probe_wave[1] * probe_wave[1]

        def add_window(position, accumulated):
            row_start = start_rows[position]
            col_start = start_cols[position]
            current = lax.dynamic_slice(
                accumulated, (channel_zero, row_start, col_start), (3, side_len, side_len)
            )
            obj_term = jnp.concatenate([object_terms[position], illumination[None]], axis=0)
            return lax.dynamic_update_slice(
                accumulated, current + obj_term, (channel_zero, row_start, col_start)
            )

        intersection = lax.fori_loop(
            0,
            pos_count,
            add_window,
            jnp.zeros((3, widened.shape[1], widened.shape[2]), jnp.float32),
        )
        folded = fold_edges(intersection, margin)
        light_sum = folded[2]
        summed = lax.psum(probe_terms, ("row", "col"))
        spread = jnp.sqrt(jnp.mean(summed * summed) + 1e-06)
        new_probe = probe_wave + summed / spread
        object_field = object_field + folded[0:2] / (light_sum + 1.0)
        probe_wave = new_probe
    return (object_field, probe_wave)


def solution(mesh):
    placed = (P("row", "col", None, None), P(), P("row", "col", None), P(), P(None, "row", "col"))
    return jax.shard_map(
        on_device,
        mesh=mesh,
        in_specs=placed,
        out_specs=(P(None, "row", "col"), P()),
        check_vma=False,
    )
```

profile of v0, /device:TPU:3, one launch (start us, length us, event | category | flops | bytes accessed | tf_op | source)
XLA Modules:
  0.0 827.5 jit_solution(10484763632224276593)
XLA Ops:
  7.2 3.3 collective-permute-start
  10.6 3.0 collective-permute-start.1
  19.1 5.9 collective-permute-start.2
  25.1 1.9 collective-permute-start.3
  29.1 1.4 copy.48
  32.5 3.2 collective-permute-done.3
  35.7 1.1 pad_maximum_fusion.4
  37.0 14.0 %while.46 = (s32[]{:T(128)}, f32[2,384,384]{2,1,0:T(8,128)}, s32[4,3]{1,0:T(4,128)S(1)}, f32[4,2,256,256]{2,3,1,0:T(8,128)S(1)}, s32[]{:T(128)}) while((s32[]{:T(128)}, f32[2,384,384]{2,1,0:T(8,128)}, s32[4,3]{1,0:T(4,128)S(1)}, f32[4,2,256,256]{2,3,1,0:T(8,128)S(1)}, s32[]{:T(128)}) %tuple.175), condition=%wide.while_cond.8, body=%wide.while_body.8.sunk | while | flops 2 | bytes 3145845 | solution.py:110
  37.6 2.6 dynamic-slice_bitcast_fusion.4
  41.1 2.6 dynamic-slice_bitcast_fusion.4
  44.6 2.6 dynamic-slice_bitcast_fusion.4
  48.1 2.6 dynamic-slice_bitcast_fusion.4
  51.0 2.6 multiply_subtract_fusion.5
  53.6 4.5 convolution_bitcast_fusion.1
  58.1 3.4 fusion.21
  61.6 5.4 bitcast_subtract_fusion.1
  67.0 3.5 multiply_add_fusion.3
  70.6 1.5 pad_maximum_fusion.1
  72.2 71.6 %while.44 = (s32[]{:T(128)}, f32[3,384,384]{2,1,0:T(8,128)S(1)}, s32[4]{0:T(128)S(1)}, s32[4]{0:T(128)S(1)}, f32[4,2,256,256]{2,3,1,0:T(8,128)}, /*index=5*/f32[...) while((s32[]{:T(128)}, f32[3,384,384]{2,1,0:T(8,128)S(1)}, s32[4]{0:T(128)S(1)}, s32[4]{0:T(128)S(1)}, ...), condition=%wide.region_1.2_spmd, body=%wide.region_0.1_spmd.sunk | while | flops 393224 | bytes 6029513 | solution.py:138
  78.9 11.8 %dynamic_update_slice.16 = f32[3,384,384]{2,1,0:T(8,128)S(1)} dynamic-update-slice(f32[3,384,384]{2,1,0:T(8,128)S(1)} %get-tuple-element.701, f32[3,256,256]{2,1,0:T(8,128)S(1)} %maximum_add_fusion.4, s32[]{:T(128)} %constant.337.clone.1..sunk, s32[]{:T(128)S(6)} %select_n.125, s32[]{:T(128)S(6)} %select_n.126) | dynamic-update-slice | bytes 1572868 | tf_op jit(solution)/shard_map/while/body/eval_jaxpr/dynamic_update_slice | solution.py:134
  97.4 11.5 %dynamic_update_slice.16 = f32[3,384,384]{2,1,0:T(8,128)S(1)} dynamic-update-slice(f32[3,384,384]{2,1,0:T(8,128)S(1)} %get-tuple-element.701, f32[3,256,256]{2,1,0:T(8,128)S(1)} %maximum_add_fusion.4, s32[]{:T(128)} %constant.337.clone.1..sunk, s32[]{:T(128)S(6)} %select_n.125, s32[]{:T(128)S(6)} %select_n.126) | dynamic-update-slice | bytes 1572868 | tf_op jit(solution)/shard_map/while/body/eval_jaxpr/dynamic_update_slice | solution.py:134
  115.5 11.2 %dynamic_update_slice.16 = f32[3,384,384]{2,1,0:T(8,128)S(1)} dynamic-update-slice(f32[3,384,384]{2,1,0:T(8,128)S(1)} %get-tuple-element.701, f32[3,256,256]{2,1,0:T(8,128)S(1)} %maximum_add_fusion.4, s32[]{:T(128)} %constant.337.clone.1..sunk, s32[]{:T(128)S(6)} %select_n.125, s32[]{:T(128)S(6)} %select_n.126) | dynamic-update-slice | bytes 1572868 | tf_op jit(solution)/shard_map/while/body/eval_jaxpr/dynamic_update_slice | solution.py:134
  133.4 10.4 %dynamic_update_slice.16 = f32[3,384,384]{2,1,0:T(8,128)S(1)} dynamic-update-slice(f32[3,384,384]{2,1,0:T(8,128)S(1)} %get-tuple-element.701, f32[3,256,256]{2,1,0:T(8,128)S(1)} %maximum_add_fusion.4, s32[]{:T(128)} %constant.337.clone.1..sunk, s32[]{:T(128)S(6)} %select_n.125, s32[]{:T(128)S(6)} %select_n.126) | dynamic-update-slice | bytes 1572868 | tf_op jit(solution)/shard_map/while/body/eval_jaxpr/dynamic_update_slice | solution.py:134
  144.7 1.9 collective-permute-start.4
  146.6 2.4 collective-permute-start.5
  150.1 10.5 %collective-permute-done.4 = f32[3,384,128]{2,1,0:T(8,128)S(1)} collective-permute-done((f32[3,384,128]{2,1,0:T(8,128)}, f32[3,384,128]{2,1,0:T(8,128)S(1)}, u32[]{:S(2)}, u32[]{:S(2)}) %collective-permute-start.4) | collective-permute-done | bytes 589856 | tf_op jit(solution)/shard_map/ppermute | solution.py:19
  160.7 1.1 add_add_fusion.1
  161.9 2.1 collective-permute-start.6
  163.9 4.3 collective-permute-start.7
  168.4 237.1 %all-reduce.3.cloned.1.call-done = f32[2,256,256]{1,2,0:T(8,128)} async-done(((f32[2,256,256]{1,2,0:T(8,128)}), f32[2,256,256]{1,2,0:T(8,128)}) %all-reduce.3.cloned.1.call-update) | async-done | bytes 524304 | tf_op jit(solution)/shard_map/psum | solution.py:146
  405.5 1.9 multiply_reduce_fusion.1
  408.2 3.0 collective-permute-start.8
  411.2 3.2 collective-permute-start.9
  414.8 3.9 collective-permute-done.9
  418.7 6.0 collective-permute-start.10
  424.7 2.1 collective-permute-start.11
  427.9 1.5 collective-permute-done.10
  429.4 5.9 collective-permute-done.11
  435.3 1.1 pad_maximum_fusion.5
  436.6 14.1 %while.47 = (s32[]{:T(128)}, f32[2,384,384]{2,1,0:T(8,128)}, s32[4,3]{1,0:T(4,128)S(1)}, f32[4,2,256,256]{2,3,1,0:T(8,128)S(1)}, s32[]{:T(128)}) while((s32[]{:T(128)}, f32[2,384,384]{2,1,0:T(8,128)}, s32[4,3]{1,0:T(4,128)S(1)}, f32[4,2,256,256]{2,3,1,0:T(8,128)S(1)}, s32[]{:T(128)}) %tuple.191), condition=%wide.while_cond.9, body=%wide.while_body.9.sunk | while | flops 2 | bytes 3145845 | solution.py:110
  437.3 2.6 dynamic-slice_bitcast_fusion.5
  440.8 2.6 dynamic-slice_bitcast_fusion.5
  444.3 2.6 dynamic-slice_bitcast_fusion.5
  447.8 2.6 dynamic-slice_bitcast_fusion.5
  450.7 2.6 multiply_subtract_fusion.2
  453.3 4.5 convolution_bitcast_fusion
  457.8 3.4 fusion.16
  461.2 5.4 bitcast_subtract_fusion
  466.6 3.5 multiply_add_fusion
  470.2 1.5 pad_maximum_fusion.3
  471.9 69.5 %while.45 = (s32[]{:T(128)}, f32[3,384,384]{2,1,0:T(8,128)S(1)}, s32[4]{0:T(128)S(1)}, s32[4]{0:T(128)S(1)}, f32[4,2,256,256]{2,3,1,0:T(8,128)}, /*index=5*/f32[...) while((s32[]{:T(128)}, f32[3,384,384]{2,1,0:T(8,128)S(1)}, s32[4]{0:T(128)S(1)}, s32[4]{0:T(128)S(1)}, ...), condition=%wide.region_6.7_spmd, body=%wide.region_5.6_spmd.sunk | while | flops 393224 | bytes 6029513 | solution.py:138
  478.0 11.8 %dynamic_update_slice.17 = f32[3,384,384]{2,1,0:T(8,128)S(1)} dynamic-update-slice(f32[3,384,384]{2,1,0:T(8,128)S(1)} %get-tuple-element.743, f32[3,256,256]{2,1,0:T(8,128)S(1)} %maximum_add_fusion.5, s32[]{:T(128)} %constant.337.clone.1..sunk.1, s32[]{:T(128)S(6)} %select_n.127, s32[]{:T(128)S(6)} %select_n.128) | dynamic-update-slice | bytes 1572868 | tf_op jit(solution)/shard_map/while/body/eval_jaxpr/dynamic_update_slice | solution.py:134
  496.0 11.5 %dynamic_update_slice.17 = f32[3,384,384]{2,1,0:T(8,128)S(1)} dynamic-update-slice(f32[3,384,384]{2,1,0:T(8,128)S(1)} %get-tuple-element.743, f32[3,256,256]{2,1,0:T(8,128)S(1)} %maximum_add_fusion.5, s32[]{:T(128)} %constant.337.clone.1..sunk.1, s32[]{:T(128)S(6)} %select_n.127, s32[]{:T(128)S(6)} %select_n.128) | dynamic-update-slice | bytes 1572868 | tf_op jit(solution)/shard_map/while/body/eval_jaxpr/dynamic_update_slice | solution.py:134
  513.6 11.2 %dynamic_update_slice.17 = f32[3,384,384]{2,1,0:T(8,128)S(1)} dynamic-update-slice(f32[3,384,384]{2,1,0:T(8,128)S(1)} %get-tuple-element.743, f32[3,256,256]{2,1,0:T(8,128)S(1)} %maximum_add_fusion.5, s32[]{:T(128)} %constant.337.clone.1..sunk.1, s32[]{:T(128)S(6)} %select_n.127, s32[]{:T(128)S(6)} %select_n.128) | dynamic-update-slice | bytes 1572868 | tf_op jit(solution)/shard_map/while/body/eval_jaxpr/dynamic_update_slice | solution.py:134
  531.0 10.4 %dynamic_update_slice.17 = f32[3,384,384]{2,1,0:T(8,128)S(1)} dynamic-update-slice(f32[3,384,384]{2,1,0:T(8,128)S(1)} %get-tuple-element.743, f32[3,256,256]{2,1,0:T(8,128)S(1)} %maximum_add_fusion.5, s32[]{:T(128)} %constant.337.clone.1..sunk.1, s32[]{:T(128)S(6)} %select_n.127, s32[]{:T(128)S(6)} %select_n.128) | dynamic-update-slice | bytes 1572868 | tf_op jit(solution)/shard_map/while/body/eval_jaxpr/dynamic_update_slice | solution.py:134
  541.4 1.1 fusion.59
  542.5 1.9 collective-permute-start.12
  544.4 2.4 collective-permute-start.13
  547.9 254.1 %all-reduce.5.cloned.1.call-done = f32[2,256,256]{1,2,0:T(8,128)} async-done(((f32[2,256,256]{1,2,0:T(8,128)}), f32[2,256,256]{1,2,0:T(8,128)}) %all-reduce.5.cloned.1.call-update) | async-done | bytes 524304 | tf_op jit(solution)/shard_map/psum | solution.py:146
  802.0 1.9 multiply_reduce_fusion
  805.4 1.3 add_add_fusion
  806.7 3.0 collective-permute-start.14
  809.7 3.2 collective-permute-start.15
  814.1 5.9 collective-permute-done.15
  (170 shorter events, 46.5 us)
Async XLA Ops:
  7.2 22.0 %copy-start.12 = (f32[2,2,256,256]{3,2,1,0:T(8,128)S(1)}, f32[2,2,256,256]{3,2,1,0:T(8,128)}, u32[]{:S(2)}) copy-start(f32[2,2,256,256]{3,2,1,0:T(8,128)} %param.41) | copy-start | bytes 3145732
  7.2 398.4 %all-reduce.3.cloned.1.call-start = ((), (), s32[]{:S(2)}) async-start(), calls=%async_computation | async-start | bytes 1048576 | tf_op jit(solution)/shard_map/psum | solution.py:146
  7.2 10.9 %collective-permute-start = (f32[2,128,128]{2,1,0:T(8,128)}, f32[2,128,128]{2,1,0:T(8,128)S(1)}, u32[]{:S(2)}, u32[]{:S(2)}) collective-permute-start(f32[2,128,128]{2,1,0:T(8,128)} %param.45), channel_id=1, source_target_pairs={{0,32},{32,64},{64,96},{96,128},{128,160},{160,192},{192,224},{1,3... | collective-permute-start | bytes 393224 | tf_op jit(solution)/shard_map/ppermute | solution.py:19
  10.6 8.5 %collective-permute-start.1 = (f32[2,128,128]{2,1,0:T(8,128)}, f32[2,128,128]{2,1,0:T(8,128)S(1)}, u32[]{:S(2)}, u32[]{:S(2)}) collective-permute-start(f32[2,128,128]{2,1,0:T(8,128)} %param.45), channel_id=1, source_target_pairs={{32,0},{64,32},{96,64},{128,96},{160,128},{192,160},{224,192},{33,... | collective-permute-start | bytes 393224 | tf_op jit(solution)/shard_map/ppermute | solution.py:20
  17.0 13.5 %copy-start.15 = (f32[256,256]{1,0:T(8,128)S(1)}, f32[256,256]{1,0:T(8,128)}, u32[]{:S(2)}) copy-start(f32[256,256]{1,0:T(8,128)} %param.42) | copy-start | bytes 786436
  19.1 13.4 %collective-permute-start.2 = (f32[2,384,128]{2,1,0:T(8,128)S(1)}, f32[2,384,128]{2,1,0:T(8,128)S(1)}, u32[]{:S(2)}, u32[]{:S(2)}) collective-permute-start(f32[2,384,128]{2,1,0:T(8,128)S(1)} %constant_dynamic-update-slice_fusion.2), channel_id=1, source_target_pairs={{0,1},{1,2},{2,3},{3,4},{4,5},{5,6},{6,7},{7,8},{8,9},{9,10},{10,1... | collective-permute-start | bytes 1179656 | tf_op jit(solution)/shard_map/ppermute | solution.py:19
  25.1 10.6 %collective-permute-start.3 = (f32[2,384,128]{2,1,0:T(8,128)S(1)}, f32[2,384,128]{2,1,0:T(8,128)S(1)}, u32[]{:S(2)}, u32[]{:S(2)}) collective-permute-start(f32[2,384,128]{2,1,0:T(8,128)S(1)} %constant_dynamic-update-slice_fusion.2), channel_id=1, source_target_pairs={{1,0},{2,1},{3,2},{4,3},{5,4},{6,5},{7,6},{8,7},{9,8},{10,9},{11,1... | collective-permute-start | bytes 1179656 | tf_op jit(solution)/shard_map/ppermute | solution.py:20
  29.1 3.3 copy-start.4
  53.6 4.5 copy-start
  143.8 5.3 copy-start.8
  143.8 5.3 copy-start.9
  144.7 15.9 %collective-permute-start.4 = (f32[3,384,128]{2,1,0:T(8,128)}, f32[3,384,128]{2,1,0:T(8,128)S(1)}, u32[]{:S(2)}, u32[]{:S(2)}) collective-permute-start(f32[3,384,128]{2,1,0:T(8,128)} %get-tuple-element.524), channel_id=1, source_target_pairs={{0,1},{1,2},{2,3},{3,4},{4,5},{5,6},{6,7},{7,8},{8,9},{9,10},{10,1... | collective-permute-start | bytes 1769480 | tf_op jit(solution)/shard_map/ppermute | solution.py:19
  146.6 14.0 %collective-permute-start.5 = (f32[3,384,128]{2,1,0:T(8,128)S(1)}, f32[3,384,128]{2,1,0:T(8,128)}, u32[]{:S(2)}, u32[]{:S(2)}) collective-permute-start(f32[3,384,128]{2,1,0:T(8,128)S(1)} %get-tuple-element.525), channel_id=1, source_target_pairs={{1,0},{2,1},{3,2},{4,3},{5,4},{6,5},{7,6},{8,7},{9,8},{10,9},{11,1... | collective-permute-start | bytes 1769480 | tf_op jit(solution)/shard_map/ppermute | solution.py:20
  150.0 18.1 %copy-start.5 = (f32[2,256,256]{2,1,0:T(8,128)S(1)}, f32[2,256,256]{2,1,0:T(8,128)}, u32[]{:S(2)}) copy-start(f32[2,256,256]{2,1,0:T(8,128)} %param.44) | copy-start | bytes 1572868
  150.1 651.9 %all-reduce.5.cloned.1.call-start = ((), (), s32[]{:S(2)}) async-start(), calls=%async_computation.1 | async-start | bytes 1048576 | tf_op jit(solution)/shard_map/psum | solution.py:146
  161.8 246.4 %copy-start.14 = (f32[2,128,128]{2,1,0:T(8,128)S(1)}, f32[2,128,128]{2,1,0:T(8,128)}, u32[]{:S(2)}) copy-start(f32[2,128,128]{2,1,0:T(8,128)} %param.45) | copy-start | bytes 393220
  161.9 246.2 %collective-permute-start.6 = (f32[3,128,128]{2,1,0:T(8,128)S(1)}, f32[3,128,128]{2,1,0:T(8,128)S(1)}, u32[]{:S(2)}, u32[]{:S(2)}) collective-permute-start(f32[3,128,128]{2,1,0:T(8,128)S(1)} %get-tuple-element.528), channel_id=1, source_target_pairs={{0,32},{32,64},{64,96},{96,128},{128,160},{160,192},{192,224},{1,3... | collective-permute-start | bytes 589832 | tf_op jit(solution)/shard_map/ppermute | solution.py:19
  163.9 244.2 %collective-permute-start.7 = (f32[3,128,128]{2,1,0:T(8,128)S(1)}, f32[3,128,128]{2,1,0:T(8,128)S(1)}, u32[]{:S(2)}, u32[]{:S(2)}) collective-permute-start(f32[3,128,128]{2,1,0:T(8,128)S(1)} %get-tuple-element.529), channel_id=1, source_target_pairs={{32,0},{64,32},{96,64},{128,96},{160,128},{192,160},{224,192},{33,... | collective-permute-start | bytes 589832 | tf_op jit(solution)/shard_map/ppermute | solution.py:20
  405.5 8.9 %copy-start.10 = (f32[2,256,256]{1,2,0:T(8,128)S(1)}, f32[2,256,256]{1,2,0:T(8,128)}, u32[]{:S(2)}) copy-start(f32[2,256,256]{1,2,0:T(8,128)} %all-reduce.3.cloned.1.call-done) | copy-start | bytes 1572868
  408.2 6.6 collective-permute-start.8
  411.2 7.5 collective-permute-start.9
  414.5 20.8 %copy-start.2 = (f32[2,256,256]{1,2,0:T(8,128)}, f32[2,256,256]{1,2,0:T(8,128)S(1)}, u32[]{:S(2)}) copy-start(f32[2,256,256]{1,2,0:T(8,128)S(1)} %divide_add_fusion.1) | copy-start | bytes 1572868
  418.7 10.7 %collective-permute-start.10 = (f32[2,384,128]{2,1,0:T(8,128)S(1)}, f32[2,384,128]{2,1,0:T(8,128)S(1)}, u32[]{:S(2)}, u32[]{:S(2)}) collective-permute-start(f32[2,384,128]{2,1,0:T(8,128)S(1)} %pad_maximum_fusion.6), channel_id=1, source_target_pairs={{0,1},{1,2},{2,3},{3,4},{4,5},{5,6},{6,7},{7,8},{8,9},{9,10},{10,1... | collective-permute-start | bytes 1179656 | tf_op jit(solution)/shard_map/ppermute | solution.py:19
  424.7 10.6 %collective-permute-start.11 = (f32[2,384,128]{2,1,0:T(8,128)S(1)}, f32[2,384,128]{2,1,0:T(8,128)S(1)}, u32[]{:S(2)}, u32[]{:S(2)}) collective-permute-start(f32[2,384,128]{2,1,0:T(8,128)S(1)} %pad_maximum_fusion.6), channel_id=1, source_target_pairs={{1,0},{2,1},{3,2},{4,3},{5,4},{6,5},{7,6},{8,7},{9,8},{10,9},{11,1... | collective-permute-start | bytes 1179656 | tf_op jit(solution)/shard_map/ppermute | solution.py:20
  453.3 4.5 copy-start.1
  541.4 5.5 copy-start.6
  541.4 5.5 copy-start.7
  542.5 262.0 %collective-permute-start.12 = (f32[3,384,128]{2,1,0:T(8,128)}, f32[3,384,128]{2,1,0:T(8,128)S(1)}, u32[]{:S(2)}, u32[]{:S(2)}) collective-permute-start(f32[3,384,128]{2,1,0:T(8,128)} %get-tuple-element.522), channel_id=1, source_target_pairs={{0,1},{1,2},{2,3},{3,4},{4,5},{5,6},{6,7},{7,8},{8,9},{9,10},{10,1... | collective-permute-start | bytes 1769480 | tf_op jit(solution)/shard_map/ppermute | solution.py:19
  544.4 261.0 %collective-permute-start.13 = (f32[3,384,128]{2,1,0:T(8,128)}, f32[3,384,128]{2,1,0:T(8,128)}, u32[]{:S(2)}, u32[]{:S(2)}) collective-permute-start(f32[3,384,128]{2,1,0:T(8,128)} %get-tuple-element.523), channel_id=1, source_target_pairs={{1,0},{2,1},{3,2},{4,3},{5,4},{6,5},{7,6},{8,7},{9,8},{10,9},{11,1... | collective-permute-start | bytes 1769480 | tf_op jit(solution)/shard_map/ppermute | solution.py:20
  547.8 265.1 %copy-start.3 = (f32[2,256,256]{1,2,0:T(8,128)S(1)}, f32[2,256,256]{1,2,0:T(8,128)}, u32[]{:S(2)}) copy-start(f32[2,256,256]{1,2,0:T(8,128)} %copy-done.2) | copy-start | bytes 1572868
  802.0 11.0 %copy-start.11 = (f32[2,256,256]{1,2,0:T(8,128)S(1)}, f32[2,256,256]{1,2,0:T(8,128)}, u32[]{:S(2)}) copy-start(f32[2,256,256]{1,2,0:T(8,128)} %all-reduce.5.cloned.1.call-done) | copy-start | bytes 1572868
  804.6 0.8 copy-start.13
  806.7 7.3 collective-permute-start.14
  809.7 10.2 %collective-permute-start.15 = (f32[3,128,128]{2,1,0:T(8,128)S(1)}, f32[3,128,128]{2,1,0:T(8,128)S(1)}, u32[]{:S(2)}, u32[]{:S(2)}) collective-permute-start(f32[3,128,128]{2,1,0:T(8,128)S(1)} %get-tuple-element.527), channel_id=1, source_target_pairs={{32,0},{64,32},{96,64},{128,96},{160,128},{192,160},{224,192},{33,... | collective-permute-start | bytes 589832 | tf_op jit(solution)/shard_map/ppermute | solution.py:20
Sparse Core Ops, SparseCore 0:
  150.2 255.3 all-reduce.2
  548.0 253.9 all-reduce.4
where the time goes:
time: 831 us; the launch traced here: 828 us
  waiting for transfers between devices  523 us (63%)
  local copies, waits for them, and re-layouts  151 us (18%)
  starting transfers between devices  49.7 us (6%)
  other arithmetic  39 us (5%)
  loops' own time  29.7 us (4%)
  matrix products  19.9 us (2%)
  between operations  16 us (2%)
    psum x2, waiting for transfers between devices, on_device(): summed = lax.psum(probe_terms, ('row', 'col'))  491 us
    dynamic_update_slice x8, local copies, waits for them, and re-layouts, add_window(): lax.dynamic_update_slice(accumulated, current + obj_term, (channel_zero,...  89.8 us
    another operation x2, loops' own time, on_device(): lax.fori_loop(0, pos_count, add_window, jnp.zeros((3, widened.shape[1], w...  29.4 us
    gather x40, local copies, waits for them, and re-layouts  27.8 us
    ppermute x8, starting transfers between devices, extended(): before = lax.ppermute(last, axis, up)  27.1 us
    ppermute x8, starting transfers between devices, extended(): after = lax.ppermute(first, axis, down)  22.5 us
    dot_general x4, matrix products, transform(): jnp.einsum('pckn,cdnm->pdkm', half_way, right_table, preferred_element_ty...  19.9 us
    ppermute x8, waiting for transfers between devices, extended(): after = lax.ppermute(first, axis, down)  18.9 us
  transfers between devices with their start and end apart: 18, of which 9 were waited for; matrix products, arithmetic and copies ran while one was open for 2% of the time, Pallas kernels for 0%

commit v1 on v0

v1 whole, which is shorter than its diff:
```python
import math

import jax
import jax.numpy as jnp
import numpy as np
from jax import lax
from jax.experimental import pallas as pl
from jax.experimental.pallas import tpu as pltpu
from jax.sharding import Mesh, PartitionSpec as P

STEP = 64
ITERS = 2
ROW = ("x", "yl")
COL = ("z", "yh", "core")
NEAR = ("x", "yl", "yh", "core")
CHUNK = 32
f32 = jnp.float32
bf16 = jnp.bfloat16


def dft_tables(side_len):
    index = np.arange(side_len)
    angles = (np.outer(index, index) % side_len).astype(np.float32) * np.float32(
        2.0 * math.pi / side_len
    )
    scaling = np.float32(1.0 / math.sqrt(side_len))
    real = np.cos(angles) * scaling
    imag = -np.sin(angles) * scaling
    first = np.block([[real, -imag], [imag, real]]).astype(bf16)
    second = np.block([[real, imag], [-imag, real]]).astype(bf16)
    return first, second


def shift_from(value, axis, step):
    count = lax.axis_size(axis)
    if step > 0:
        pairs = [(i, i + step) for i in range(count - step)]
    else:
        pairs = [(i, i + step) for i in range(-step, count)]
    return lax.ppermute(value, axis, pairs)


def update_kernel(renew, starts, left, mid, right, amplitude, probe_in, summed, first, second,
                  acc_l, acc_m, acc_r, grad, probe, window, wave, field, bent):
    side = probe.shape[-1]
    count = amplitude.shape[0]
    chunks = side // CHUNK
    if renew:
        square = jnp.zeros((8, side), f32)
        for c in range(2):
            part = summed[c] * summed[c]
            square = square + jnp.sum(part.reshape(side // 8, 8, side), axis=0)
        spread = jnp.sqrt(jnp.sum(square) / (2.0 * side * side) + 1e-06)
        probe[...] = probe_in[...] + summed[...] / spread
    else:
        probe[...] = probe_in[...]
    for ref in (acc_l, acc_m, acc_r):
        ref[...] = jnp.zeros_like(ref)
    for p in range(count):
        row_start = starts[p, 0]
        col_start = starts[p, 1]

        def load(i, _):
            here = pl.ds(pl.multiple_of(i * CHUNK, CHUNK), CHUNK)
            there = pl.ds(row_start + i * CHUNK, CHUNK)
            cut = []
            for c in range(2):
                wide = jnp.concatenate([left[c, there, :], mid[c, there, :], right[c, there, :]], axis=1)
                part = pltpu.roll(wide, 3 * 128 - col_start, 1)[:, :side]
                window[c, here, :] = part
                cut.append(part)
            pr, pi = probe[0, here, :], probe[1, here, :]
            er = pr * cut[0] - pi * cut[1]
            ei = pr * cut[1] + pi * cut[0]
            wave[0, here, :] = er
            wave[1, here, :] = ei
            bent[here, :] = er.astype(bf16)
            bent[pl.ds(pl.multiple_of(side + i * CHUNK, CHUNK), CHUNK), :] = ei.astype(bf16)
            return 0

        lax.fori_loop(0, chunks, load, 0)
        half = jnp.dot(first[...], bent[...], preferred_element_type=f32).astype(bf16)
        half = jnp.concatenate([half[:side], half[side:]], axis=1)
        field[...] = jnp.dot(half, second[...], preferred_element_type=f32)

        def project(i, _):
            here = pl.ds(pl.multiple_of(i * CHUNK, CHUNK), CHUNK)
            fr, fi = field[here, :side], field[here, side:]
            scale = amplitude[p, here, :] * lax.rsqrt(jnp.maximum(fr * fr + fi * fi, 0.25))
            bent[here, :] = (fr * scale).astype(bf16)
            bent[pl.ds(pl.multiple_of(side + i * CHUNK, CHUNK), CHUNK), :] = (fi * scale).astype(bf16)
            return 0

        lax.fori_loop(0, chunks, project, 0)
        half = jnp.dot(second[...], bent[...], preferred_element_type=f32).astype(bf16)
        half = jnp.concatenate([half[:side], half[side:]], axis=1)
        field[...] = jnp.dot(half, first[...], preferred_element_type=f32)

        def spread_out(i, _):
            here = pl.ds(pl.multiple_of(i * CHUNK, CHUNK), CHUNK)
            there = pl.ds(row_start + i * CHUNK, CHUNK)
            dr = field[here, :side] - wave[0, here, :]
            di = field[here, side:] - wave[1, here, :]
            pr, pi = probe[0, here, :], probe[1, here, :]
            wr, wi = window[0, here, :], window[1, here, :]
            gr = wr * dr + wi * di
            gi = wr * di - wi * dr
            if p == 0:
                grad[0, here, :] = gr
                grad[1, here, :] = gi
            else:
                grad[0, here, :] += gr
                grad[1, here, :] += gi
            terms = (pr * dr + pi * di, pr * di - pi * dr, pr * pr + pi * pi)
            for c, term in enumerate(terms):
                wide = jnp.concatenate([term, jnp.zeros((CHUNK, 128), f32)], axis=1)
                moved = pltpu.roll(wide, col_start, 1)
                acc_l[c, there, :] += moved[:, :128]
                acc_m[c, there, :] += moved[:, 128:256]
                acc_r[c, there, :] += moved[:, 256:]
            return 0

        lax.fori_loop(0, chunks, spread_out, 0)


def update(renew, starts, strips, amplitude, probe, summed, tables):
    side = probe.shape[-1]
    strip = jax.ShapeDtypeStruct((3,) + strips[0].shape[1:], f32)
    wave = jax.ShapeDtypeStruct(probe.shape, f32)
    vmem = pl.BlockSpec(memory_space=pltpu.VMEM)
    return pl.pallas_call(
        lambda *refs: update_kernel(renew, *refs),
        out_shape=(strip, strip, strip, wave, wave),
        in_specs=[pl.BlockSpec(memory_space=pltpu.SMEM)] + [vmem] * 8,
        out_specs=(vmem,) * 5,
        scratch_shapes=[
            pltpu.VMEM((2, side, side), f32),
            pltpu.VMEM((2, side, side), f32),
            pltpu.VMEM((side, 2 * side), f32),
            pltpu.VMEM((2 * side, side), bf16),
        ],
        compiler_params=pltpu.CompilerParams(vmem_limit_bytes=40 * 1024 * 1024),
        cost_estimate=pl.CostEstimate(
            flops=amplitude.shape[0] * 32 * side**3, bytes_accessed=8 * 2**20, transcendentals=0
        ),
        name="update",
    )(starts, *strips, amplitude, probe, summed, *tables)


def finish_kernel(probe, summed, out):
    side = probe.shape[-1]
    square = jnp.zeros((8, side), f32)
    for c in range(2):
        part = summed[c] * summed[c]
        square = square + jnp.sum(part.reshape(side // 8, 8, side), axis=0)
    spread = jnp.sqrt(jnp.sum(square) / (2.0 * side * side) + 1e-06)
    out[...] = probe[...] + summed[...] / spread


def finish(probe, summed):
    vmem = pl.BlockSpec(memory_space=pltpu.VMEM)
    return pl.pallas_call(
        finish_kernel,
        out_shape=jax.ShapeDtypeStruct(probe.shape, f32),
        in_specs=[vmem, vmem],
        out_specs=vmem,
        name="finish",
    )(probe, summed)


def total(value):
    near = math.prod(lax.axis_size(a) for a in NEAR)
    flat = value.reshape(near, -1, value.shape[-1])
    part = jnp.sum(lax.all_to_all(flat, NEAR, 0, 0), axis=0)
    deep = lax.axis_size("z")
    part = jnp.sum(lax.all_to_all(jnp.broadcast_to(part, (deep,) + part.shape), "z", 0, 0), axis=0)
    full = lax.all_to_all(jnp.broadcast_to(part, (near,) + part.shape), NEAR, 0, 0)
    return full.reshape(value.shape)


def widen(tile):
    above = shift_from(tile, ROW, 1)
    below = shift_from(tile, ROW, -1)
    tall = jnp.concatenate([above, tile, below], axis=1)
    return (shift_from(tall, COL, 1), tall, shift_from(tall, COL, -1))


def fold(acc_l, acc_m, acc_r):
    length = acc_m.shape[1] // 3
    tall = acc_m + shift_from(acc_r, COL, 1) + shift_from(acc_l, COL, -1)
    top, centre, bottom = (tall[:, i * length : (i + 1) * length] for i in range(3))
    return centre + shift_from(bottom, ROW, 1) + shift_from(top, ROW, -1)


def on_device(patterns, background, offsets, probe, tile):
    side = probe.shape[-1]
    rows, cols = patterns.shape[:2]
    steps = jnp.stack(jnp.meshgrid(jnp.arange(rows), jnp.arange(cols), indexing="ij"), axis=-1)
    starts = (offsets + steps.astype(jnp.int32) * STEP).reshape(rows * cols, 2)
    amplitude = jnp.sqrt(jnp.maximum(patterns.reshape(rows * cols, side, side) - background, 0.0))
    tables = tuple(jnp.asarray(t) for t in dft_tables(side))
    summed = probe
    for step in range(ITERS):
        strips = widen(tile)
        acc_l, acc_m, acc_r, grad, probe = update(
            step > 0, starts, strips, amplitude, probe, summed, tables
        )
        folded = fold(acc_l, acc_m, acc_r)
        tile = tile + folded[0:2] / (folded[2] + 1.0)
        summed = total(grad)
    return tile, finish(probe, summed)


def solution(mesh):
    fine = Mesh(mesh.devices.reshape(4, 2, 8, 2, 2), ROW + COL)
    return jax.shard_map(
        on_device,
        mesh=fine,
        in_specs=(P(ROW, COL, None, None), P(), P(ROW, COL, None), P(), P(None, ROW, COL)),
        out_specs=(P(None, ROW, COL), P()),
        check_vma=False,
    )
```

time: 831 us -> 205 us (0.25)
  waiting for transfers between devices: 523 us -> 39.3 us
  local copies, waits for them, and re-layouts: 151 us -> 12.2 us
  starting transfers between devices: 49.7 us -> 94.1 us
  other arithmetic: 39 us -> 5.13 us
  Pallas kernels: 0 us -> 31.6 us
  loops' own time: 29.7 us -> 0 us
  matrix products: 19.9 us -> 0 us
  blocking collectives: 0 us -> 18.4 us
  between operations: 16 us -> 1.05 us
    psum x2 -> x0, waiting for transfers between devices: 491 us -> none  [on_device(): summed = lax.psum(probe_terms, ('row', 'col'))]
    dynamic_update_slice x8 -> x0, local copies, waits for them, and re-layouts: 89.8 us -> none  [add_window(): lax.dynamic_update_slice(accumulated, current + obj_term, (channel_zero,...]
    all_to_all x0 -> x5, starting transfers between devices: none -> 39.5 us  [the longest x2 18.3 us: total(): lax.all_to_all(jnp.broadcast_to(part, (deep,) + part.shape), 'z', 0, 0)]
    pallas_call x0 -> x3, Pallas kernels: none -> 31.6 us  [the longest x2 29.3 us: update(): pl.pallas_call(lambda *refs: update_kernel(renew, *refs), out_shape=(stri...]
    another operation x4 -> x0, loops' own time: 29.7 us -> none  [the longest x2 29.4 us: on_device(): lax.fori_loop(0, pos_count, add_window, jnp.zeros((3, widened.shape[1], w...]
    gather x40 -> x0, local copies, waits for them, and re-layouts: 27.8 us -> none
    dot_general x4 -> x0, matrix products: 19.9 us -> none  [transform(): jnp.einsum('pckn,cdnm->pdkm', half_way, right_table, preferred_element_ty...]
    dynamic_slice x32 -> x0, local copies, waits for them, and re-layouts: 19.6 us -> none  [the longest x16 10.2 us: add_window(): object_terms[position]]
  transfers between devices with their start and end apart: 18 -> 21, of which waited for: 9 -> 11; matrix products, arithmetic and copies ran while one was open for 2% -> 4% of each run, Pallas kernels for 0% -> 0%
where the time goes in v1:
time: 205 us; the launch traced here: 202 us
  starting transfers between devices  94.1 us (46%)
  waiting for transfers between devices  39.3 us (19%)
  Pallas kernels  31.6 us (15%)
  blocking collectives  18.4 us (9%)
  local copies, waits for them, and re-layouts  12.2 us (6%)
  other arithmetic  5.13 us (3%)
    ppermute x16, starting transfers between devices, shift_from(): return lax.ppermute(value, axis, pairs)  54.6 us
    pallas_call x2, Pallas kernels, update(): pl.pallas_call(lambda *refs: update_kernel(renew, *refs), out_shape=(stri...  29.3 us
    ppermute x16, waiting for transfers between devices, shift_from(): return lax.ppermute(value, axis, pairs)  24.7 us
    all_to_all x1, blocking collectives, total(): part = jnp.sum(lax.all_to_all(flat, NEAR, 0, 0), axis=0)  18.4 us
    all_to_all x2, starting transfers between devices, total(): lax.all_to_all(jnp.broadcast_to(part, (deep,) + part.shape), 'z', 0, 0)  18.3 us
    all_to_all x2, starting transfers between devices, total(): lax.all_to_all(jnp.broadcast_to(part, (near,) + part.shape), NEAR, 0, 0)  13.4 us
    all_to_all x2, waiting for transfers between devices, total(): lax.all_to_all(jnp.broadcast_to(part, (near,) + part.shape), NEAR, 0, 0)  10.5 us
    unnamed x36, local copies, waits for them, and re-layouts  9.04 us
  transfers between devices with their start and end apart: 21, of which 11 were waited for; matrix products, arithmetic and copies ran while one was open for 4% of the time, Pallas kernels for 0%

profile of v1, /device:TPU:3, one launch (start us, length us, event | category | flops | bytes accessed | tf_op | source)
XLA Modules:
  0.0 201.7 jit_solution(16966111857116916707)
XLA Ops:
  0.6 3.3 %collective-permute-start = (f32[2,128,128]{2,1,0:T(8,128)}, f32[2,128,128]{2,1,0:T(8,128)S(1)}, u32[]{:S(2)}, u32[]{:S(2)}) collective-permute-start(f32[2,128,128]{2,1,0:T(8,128)} %param.11), channel_id=1, source_target_pairs={{0,32},{32,64},{64,96},{96,128},{128,160},{160,192},{192,224},{1,3... | collective-permute-start | bytes 393224 | tf_op jit(solution)/shard_map/ppermute | solution.py:40
  4.0 3.0 %collective-permute-start.1 = (f32[2,128,128]{2,1,0:T(8,128)}, f32[2,128,128]{2,1,0:T(8,128)S(1)}, u32[]{:S(2)}, u32[]{:S(2)}) collective-permute-start(f32[2,128,128]{2,1,0:T(8,128)} %param.11), channel_id=1, source_target_pairs={{32,0},{64,32},{96,64},{128,96},{160,128},{192,160},{224,192},{33,... | collective-permute-start | bytes 393224 | tf_op jit(solution)/shard_map/ppermute | solution.py:40
  7.0 1.2 collective-permute-done
  8.2 0.0 copy-start.15
  8.2 2.9 %collective-permute-done.1 = f32[2,128,128]{2,1,0:T(8,128)S(1)} collective-permute-done((f32[2,128,128]{2,1,0:T(8,128)}, f32[2,128,128]{2,1,0:T(8,128)S(1)}, u32[]{:S(2)}, u32[]{:S(2)}) %collective-permute-start.1) | collective-permute-done | bytes 131104 | tf_op jit(solution)/shard_map/ppermute | solution.py:40
  11.1 0.0 copy-start.16
  11.1 3.3 %collective-permute-start.3 = (f32[2,384,128]{2,1,0:T(8,128)S(1)}, f32[2,384,128]{2,1,0:T(8,128)S(1)}, u32[]{:S(2)}, u32[]{:S(2)}) collective-permute-start(f32[2,384,128]{2,1,0:T(8,128)S(1)} %constant_dynamic-update-slice_fusion.refs_2_), channel_id=1, source_target_pairs={{1,0},{2,1},{3,2},{4,3},{5,4},{6,5},{7,6},{8,7},{9,8},{10,9},{11,1... | collective-permute-start | bytes 1179656 | tf_op jit(solution)/shard_map/ppermute | solution.py:40
  14.4 4.7 %collective-permute-start.2 = (f32[2,384,128]{2,1,0:T(8,128)S(1)}, f32[2,384,128]{2,1,0:T(8,128)S(1)}, u32[]{:S(2)}, u32[]{:S(2)}) collective-permute-start(f32[2,384,128]{2,1,0:T(8,128)S(1)} %constant_dynamic-update-slice_fusion.refs_2_), channel_id=1, source_target_pairs={{0,1},{1,2},{2,3},{3,4},{4,5},{5,6},{6,7},{7,8},{8,9},{9,10},{10,1... | collective-permute-start | bytes 1179656 | tf_op jit(solution)/shard_map/ppermute | solution.py:40
  19.2 0.1 fusion.8
  19.3 0.0 copy-start.6
  19.3 1.7 fusion.1.refs_4_
  21.0 1.7 collective-permute-done.3.refs_3_
  22.7 4.0 %collective-permute-done.2.refs_1_ = f32[2,384,128]{2,1,0:T(8,128)S(1)} collective-permute-done((f32[2,384,128]{2,1,0:T(8,128)S(1)}, f32[2,384,128]{2,1,0:T(8,128)S(1)}, u32[]{:S(2)}, u32[]{:S(2)}) %collective-permute-start.2) | collective-permute-done | bytes 393248 | tf_op jit(solution)/shard_map/ppermute | solution.py:40
  26.7 14.5 %update.2 = (f32[3,384,128]{2,1,0:T(8,128)S(1)}, f32[3,384,128]{2,1,0:T(8,128)S(1)}, f32[3,384,128]{2,1,0:T(8,128)S(1)}, f32[2,256,256]{2,1,0:T(8,128)}, f32[2,256,256]{2,1,0:T(8,128)S(1)}) custom-call(s32[4,2]{1,0:T(4,128)S(1)} %bitcast.17, f32[2,384,128]{2,1,0:T(8,128)S(1)} %collective-permute-done.2.refs_1_, ...), custom_call_target="tpu_custom_call" | custom-call | flops 2147483648 | bytes 8388608 | tf_op jit(solution)/shard_map/update/pallas_call | solution.py:131
  41.2 0.8 copy-done.8
  42.0 5.9 %collective-permute-start.4 = (f32[3,384,128]{2,1,0:T(8,128)S(1)}, f32[3,384,128]{2,1,0:T(8,128)S(1)}, u32[]{:S(2)}, u32[]{:S(2)}) collective-permute-start(f32[3,384,128]{2,1,0:T(8,128)S(1)} %get-tuple-element.13), channel_id=1, source_target_pairs={{0,1},{1,2},{2,3},{3,4},{4,5},{5,6},{6,7},{7,8},{8,9},{9,10},{10,1... | collective-permute-start | bytes 1769480 | tf_op jit(solution)/shard_map/ppermute | solution.py:40
  47.9 1.9 collective-permute-start.5
  49.8 7.8 %all-to-all-start = ((f32[32,16,256]{2,1,0:T(8,128)}), f32[32,16,256]{2,1,0:T(8,128)}, u32[]{:S(2)}, u32[]{:S(2)}) async-start(f32[32,16,256]{2,1,0:T(8,128)} %bitcast.3), calls=%async_computation | async-start | bytes 1048576 | tf_op jit(solution)/shard_map/all_to_all | solution.py:174
  57.6 9.2 %collective-permute-done.4 = f32[3,384,128]{2,1,0:T(8,128)S(1)} collective-permute-done((f32[3,384,128]{2,1,0:T(8,128)S(1)}, f32[3,384,128]{2,1,0:T(8,128)S(1)}, u32[]{:S(2)}, u32[]{:S(2)}) %collective-permute-start.4) | collective-permute-done | bytes 589856 | tf_op jit(solution)/shard_map/ppermute | solution.py:40
  66.8 0.0 collective-permute-done.5
  66.8 0.8 copy-done.13
  67.6 1.4 add_add_fusion.1
  69.0 3.3 %collective-permute-start.6 = (f32[3,128,128]{2,1,0:T(8,128)S(1)}, f32[3,128,128]{2,1,0:T(8,128)S(1)}, u32[]{:S(2)}, u32[]{:S(2)}) collective-permute-start(f32[3,128,128]{2,1,0:T(8,128)S(1)} %get-tuple-element.24), channel_id=1, source_target_pairs={{0,32},{32,64},{64,96},{96,128},{128,160},{160,192},{192,224},{1,3... | collective-permute-start | bytes 589832 | tf_op jit(solution)/shard_map/ppermute | solution.py:40
  72.3 2.9 %collective-permute-start.7 = (f32[3,128,128]{2,1,0:T(8,128)S(1)}, f32[3,128,128]{2,1,0:T(8,128)S(1)}, u32[]{:S(2)}, u32[]{:S(2)}) collective-permute-start(f32[3,128,128]{2,1,0:T(8,128)S(1)} %get-tuple-element.25), channel_id=1, source_target_pairs={{32,0},{64,32},{96,64},{128,96},{160,128},{192,160},{224,192},{33,... | collective-permute-start | bytes 589832 | tf_op jit(solution)/shard_map/ppermute | solution.py:40
  75.2 0.0 all-to-all-done
  75.2 1.1 reduce_sum.36
  76.3 0.7 broadcast_in_dim.15
  77.0 11.7 %all-to-all-start.1 = ((f32[8,16,256]{2,1,0:T(8,128)}), f32[8,16,256]{2,1,0:T(8,128)S(1)}, u32[]{:S(2)}, u32[]{:S(2)}) async-start(f32[8,16,256]{2,1,0:T(8,128)} %broadcast_in_dim.15), calls=%async_computation.1 | async-start | bytes 262144 | tf_op jit(solution)/shard_map/all_to_all | solution.py:176
  88.6 0.0 collective-permute-done.6
  88.7 0.0 copy-start.11
  88.7 1.9 collective-permute-start.9
  90.7 3.4 %collective-permute-start.8 = (f32[2,128,128]{2,1,0:T(8,128)S(1)}, f32[2,128,128]{2,1,0:T(8,128)S(1)}, u32[]{:S(2)}, u32[]{:S(2)}) collective-permute-start(f32[2,128,128]{2,1,0:T(8,128)S(1)} %fusion.5), channel_id=1, source_target_pairs={{0,32},{32,64},{64,96},{96,128},{128,160},{160,192},{192,224},{1,3... | collective-permute-start | bytes 393224 | tf_op jit(solution)/shard_map/ppermute | solution.py:40
  94.0 2.5 %all-to-all-done.1 = f32[8,16,256]{2,1,0:T(8,128)S(1)} async-done(((f32[8,16,256]{2,1,0:T(8,128)}), f32[8,16,256]{2,1,0:T(8,128)S(1)}, u32[]{:S(2)}, u32[]{:S(2)}) %all-to-all-start.1) | async-done | bytes 131104 | tf_op jit(solution)/shard_map/all_to_all | solution.py:176
  96.6 0.9 broadcast_in_dim.16
  97.4 6.4 %all-to-all-start.2 = ((f32[32,16,256]{2,1,0:T(8,128)}), f32[32,16,256]{2,1,0:T(8,128)S(1)}, u32[]{:S(2)}, u32[]{:S(2)}) async-start(f32[32,16,256]{2,1,0:T(8,128)} %broadcast_in_dim.16), calls=%async_computation.2 | async-start | bytes 1048576 | tf_op jit(solution)/shard_map/all_to_all | solution.py:177
  103.9 2.3 %collective-permute-start.11 = (f32[2,384,128]{2,1,0:T(8,128)S(1)}, f32[2,384,128]{2,1,0:T(8,128)S(1)}, u32[]{:S(2)}, u32[]{:S(2)}) collective-permute-start(f32[2,384,128]{2,1,0:T(8,128)S(1)} %pad_maximum_fusion.refs_2_), channel_id=1, source_target_pairs={{1,0},{2,1},{3,2},{4,3},{5,4},{6,5},{7,6},{8,7},{9,8},{10,9},{11,1... | collective-permute-start | bytes 1179656 | tf_op jit(solution)/shard_map/ppermute | solution.py:40
  106.2 4.8 %collective-permute-start.10 = (f32[2,384,128]{2,1,0:T(8,128)S(1)}, f32[2,384,128]{2,1,0:T(8,128)S(1)}, u32[]{:S(2)}, u32[]{:S(2)}) collective-permute-start(f32[2,384,128]{2,1,0:T(8,128)S(1)} %pad_maximum_fusion.refs_2_), channel_id=1, source_target_pairs={{0,1},{1,2},{2,3},{3,4},{4,5},{5,6},{6,7},{7,8},{8,9},{9,10},{10,1... | collective-permute-start | bytes 1179656 | tf_op jit(solution)/shard_map/ppermute | solution.py:40
  111.0 2.5 %all-to-all-done.2 = f32[32,16,256]{2,1,0:T(8,128)S(1)} async-done(((f32[32,16,256]{2,1,0:T(8,128)}), f32[32,16,256]{2,1,0:T(8,128)S(1)}, u32[]{:S(2)}, u32[]{:S(2)}) %all-to-all-start.2) | async-done | bytes 524320 | tf_op jit(solution)/shard_map/all_to_all | solution.py:177
  113.5 4.1 %collective-permute-done.11.refs_3_ = f32[2,384,128]{2,1,0:T(8,128)S(1)} collective-permute-done((f32[2,384,128]{2,1,0:T(8,128)S(1)}, f32[2,384,128]{2,1,0:T(8,128)S(1)}, u32[]{:S(2)}, u32[]{:S(2)}) %collective-permute-start.11) | collective-permute-done | bytes 393248 | tf_op jit(solution)/shard_map/ppermute | solution.py:40
  117.6 1.6 collective-permute-done.10.refs_1_
  119.2 0.7 copy-done.2
  120.0 1.0 copy-done.3
  121.0 1.0 copy-done.5
  122.0 1.0 copy-done.7
  123.0 1.0 copy-done.9
  124.1 14.8 %update.3 = (f32[3,384,128]{2,1,0:T(8,128)S(1)}, f32[3,384,128]{2,1,0:T(8,128)S(1)}, f32[3,384,128]{2,1,0:T(8,128)}, f32[2,256,256]{2,1,0:T(8,128)S(1)}, f32[2,256,256]{2,1,0:T(8,128)S(1)}) custom-call(s32[4,2]{1,0:T(4,128)S(1)} %bitcast.18, f32[2,384,128]{2,1,0:T(8,128)S(1)} %copy-done.3, f32[2,384,128]{2,1,0:T(8,128)S(1)} %pad_maximum_fusion.refs_2_, ...), custom_call_target="tpu_custom_call" | custom-call | flops 2147483648 | bytes 8388608 | tf_op jit(solution)/shard_map/update/pallas_call | solution.py:131
  138.8 0.8 copy-done
  139.7 5.9 %collective-permute-start.12 = (f32[3,384,128]{2,1,0:T(8,128)}, f32[3,384,128]{2,1,0:T(8,128)S(1)}, u32[]{:S(2)}, u32[]{:S(2)}) collective-permute-start(f32[3,384,128]{2,1,0:T(8,128)} %get-tuple-element.18), channel_id=1, source_target_pairs={{0,1},{1,2},{2,3},{3,4},{4,5},{5,6},{6,7},{7,8},{8,9},{9,10},{10,1... | collective-permute-start | bytes 1769480 | tf_op jit(solution)/shard_map/ppermute | solution.py:40
  145.5 1.9 collective-permute-start.13
  147.5 18.4 %all_to_all.30 = f32[32,16,256]{2,1,0:T(8,128)S(1)} all-to-all(f32[32,16,256]{2,1,0:T(8,128)S(1)} %bitcast.16), channel_id=1, replica_groups=mesh['x'=4,'yl'=2,'z'=8,'yh'=2,'core'=2] {'x','yl','yh','core'}, dimensions={0} | all-to-all | bytes 1048576 | tf_op jit(solution)/shard_map/all_to_all | solution.py:174
  165.9 0.7 broadcast_in_dim.17
  166.6 6.6 %all-to-all-start.4 = ((f32[8,16,256]{2,1,0:T(8,128)}), f32[8,16,256]{2,1,0:T(8,128)S(1)}, u32[]{:S(2)}, u32[]{:S(2)}) async-start(f32[8,16,256]{2,1,0:T(8,128)} %broadcast_in_dim.17), calls=%async_computation.4 | async-start | bytes 262144 | tf_op jit(solution)/shard_map/all_to_all | solution.py:176
  173.2 0.1 add_add_fusion
  173.3 2.0 collective-permute-start.14
  175.3 4.2 %collective-permute-start.15 = (f32[3,128,128]{2,1,0:T(8,128)S(1)}, f32[3,128,128]{2,1,0:T(8,128)S(1)}, u32[]{:S(2)}, u32[]{:S(2)}) collective-permute-start(f32[3,128,128]{2,1,0:T(8,128)S(1)} %get-tuple-element.23), channel_id=1, source_target_pairs={{32,0},{64,32},{96,64},{128,96},{160,128},{192,160},{224,192},{33,... | collective-permute-start | bytes 589832 | tf_op jit(solution)/shard_map/ppermute | solution.py:40
  179.5 1.6 all-to-all-done.4
  181.1 0.9 broadcast_in_dim.18
  182.0 7.0 %all-to-all-start.5 = ((f32[32,16,256]{2,1,0:T(8,128)}), f32[32,16,256]{2,1,0:T(8,128)S(1)}, u32[]{:S(2)}, u32[]{:S(2)}) async-start(f32[32,16,256]{2,1,0:T(8,128)} %broadcast_in_dim.18), calls=%async_computation.5 | async-start | bytes 1048576 | tf_op jit(solution)/shard_map/all_to_all | solution.py:177
  189.0 0.0 copy-start.12
  189.1 0.9 copy-done.12
  190.0 0.7 fusion.4
  190.6 8.0 %all-to-all-done.5 = f32[32,16,256]{2,1,0:T(8,128)S(1)} async-done(((f32[32,16,256]{2,1,0:T(8,128)}), f32[32,16,256]{2,1,0:T(8,128)S(1)}, u32[]{:S(2)}, u32[]{:S(2)}) %all-to-all-start.5) | async-done | bytes 524320 | tf_op jit(solution)/shard_map/all_to_all | solution.py:177
  198.6 0.8 copy-done.10
  199.4 2.3 %finish.1 = f32[2,256,256]{2,1,0:T(8,128)} custom-call(f32[2,256,256]{2,1,0:T(8,128)} %copy-done, f32[2,256,256]{2,1,0:T(8,128)} %bitcast.19), custom_call_target="tpu_custom_call" | custom-call | tf_op jit(solution)/shard_map/finish/pallas_call | solution.py:162
  (42 shorter events, 0.3 us)
Async XLA Ops:
  0.6 7.5 %copy-start.14 = (f32[2,128,128]{2,1,0:T(8,128)S(1)}, f32[2,128,128]{2,1,0:T(8,128)}, u32[]{:S(2)}) copy-start(f32[2,128,128]{2,1,0:T(8,128)} %param.11) | copy-start | bytes 393220
  0.6 7.5 %collective-permute-start = (f32[2,128,128]{2,1,0:T(8,128)}, f32[2,128,128]{2,1,0:T(8,128)S(1)}, u32[]{:S(2)}, u32[]{:S(2)}) collective-permute-start(f32[2,128,128]{2,1,0:T(8,128)} %param.11), channel_id=1, source_target_pairs={{0,32},{32,64},{64,96},{96,128},{128,160},{160,192},{192,224},{1,3... | collective-permute-start | bytes 393224 | tf_op jit(solution)/shard_map/ppermute | solution.py:40
  4.0 7.1 %collective-permute-start.1 = (f32[2,128,128]{2,1,0:T(8,128)}, f32[2,128,128]{2,1,0:T(8,128)S(1)}, u32[]{:S(2)}, u32[]{:S(2)}) collective-permute-start(f32[2,128,128]{2,1,0:T(8,128)} %param.11), channel_id=1, source_target_pairs={{32,0},{64,32},{96,64},{128,96},{160,128},{192,160},{224,192},{33,... | collective-permute-start | bytes 393224 | tf_op jit(solution)/shard_map/ppermute | solution.py:40
  8.2 11.1 %copy-start.15 = (f32[256,256]{1,0:T(8,128)S(1)}, f32[256,256]{1,0:T(8,128)}, u32[]{:S(2)}) copy-start(f32[256,256]{1,0:T(8,128)} %param.8) | copy-start | bytes 786436
  11.1 8.1 %copy-start.16 = (s32[2,2,2]{2,1,0:T(2,128)S(1)}, s32[2,2,2]{2,1,0:T(2,128)}, u32[]{:S(2)}) copy-start(s32[2,2,2]{2,1,0:T(2,128)} %param.9) | copy-start | bytes 100
  11.1 11.5 %collective-permute-start.3 = (f32[2,384,128]{2,1,0:T(8,128)S(1)}, f32[2,384,128]{2,1,0:T(8,128)S(1)}, u32[]{:S(2)}, u32[]{:S(2)}) collective-permute-start(f32[2,384,128]{2,1,0:T(8,128)S(1)} %constant_dynamic-update-slice_fusion.refs_2_), channel_id=1, source_target_pairs={{1,0},{2,1},{3,2},{4,3},{5,4},{6,5},{7,6},{8,7},{9,8},{10,9},{11,1... | collective-permute-start | bytes 1179656 | tf_op jit(solution)/shard_map/ppermute | solution.py:40
  14.4 12.2 %collective-permute-start.2 = (f32[2,384,128]{2,1,0:T(8,128)S(1)}, f32[2,384,128]{2,1,0:T(8,128)S(1)}, u32[]{:S(2)}, u32[]{:S(2)}) collective-permute-start(f32[2,384,128]{2,1,0:T(8,128)S(1)} %constant_dynamic-update-slice_fusion.refs_2_), channel_id=1, source_target_pairs={{0,1},{1,2},{2,3},{3,4},{4,5},{5,6},{6,7},{7,8},{8,9},{9,10},{10,1... | collective-permute-start | bytes 1179656 | tf_op jit(solution)/shard_map/ppermute | solution.py:40
  19.3 7.4 %copy-start.1 = (f32[2,256,256]{2,1,0:T(8,128)S(1)}, f32[2,256,256]{2,1,0:T(8,128)}, u32[]{:S(2)}) copy-start(f32[2,256,256]{2,1,0:T(8,128)} %refs_6_.1) | copy-start | bytes 1572868
  19.3 7.4 %copy-start.4 = (bf16[512,512]{1,0:T(8,128)(2,1)S(1)}, bf16[512,512]{1,0:T(8,128)(2,1)}, u32[]{:S(2)}) copy-start(bf16[512,512]{1,0:T(8,128)(2,1)} %constant.12.clone.refs_8_) | copy-start | bytes 1572868
  19.3 7.4 %copy-start.6 = (bf16[512,512]{1,0:T(8,128)(2,1)S(1)}, bf16[512,512]{1,0:T(8,128)(2,1)}, u32[]{:S(2)}) copy-start(bf16[512,512]{1,0:T(8,128)(2,1)} %constant.4.clone.refs_7_) | copy-start | bytes 1572868
  41.2 0.8 copy-start.8
  42.0 24.8 %collective-permute-start.4 = (f32[3,384,128]{2,1,0:T(8,128)S(1)}, f32[3,384,128]{2,1,0:T(8,128)S(1)}, u32[]{:S(2)}, u32[]{:S(2)}) collective-permute-start(f32[3,384,128]{2,1,0:T(8,128)S(1)} %get-tuple-element.13), channel_id=1, source_target_pairs={{0,1},{1,2},{2,3},{3,4},{4,5},{5,6},{6,7},{7,8},{8,9},{9,10},{10,1... | collective-permute-start | bytes 1769480 | tf_op jit(solution)/shard_map/ppermute | solution.py:40
  47.9 18.9 %collective-permute-start.5 = (f32[3,384,128]{2,1,0:T(8,128)S(1)}, f32[3,384,128]{2,1,0:T(8,128)}, u32[]{:S(2)}, u32[]{:S(2)}) collective-permute-start(f32[3,384,128]{2,1,0:T(8,128)S(1)} %get-tuple-element.14), channel_id=1, source_target_pairs={{1,0},{2,1},{3,2},{4,3},{5,4},{6,5},{7,6},{8,7},{9,8},{10,9},{11,1... | collective-permute-start | bytes 1769480 | tf_op jit(solution)/shard_map/ppermute | solution.py:40
  49.8 25.4 %all-to-all-start = ((f32[32,16,256]{2,1,0:T(8,128)}), f32[32,16,256]{2,1,0:T(8,128)}, u32[]{:S(2)}, u32[]{:S(2)}) async-start(f32[32,16,256]{2,1,0:T(8,128)} %bitcast.3), calls=%async_computation | async-start | bytes 1048576 | tf_op jit(solution)/shard_map/all_to_all | solution.py:174
  66.8 0.8 copy-start.13
  69.0 19.6 %collective-permute-start.6 = (f32[3,128,128]{2,1,0:T(8,128)S(1)}, f32[3,128,128]{2,1,0:T(8,128)S(1)}, u32[]{:S(2)}, u32[]{:S(2)}) collective-permute-start(f32[3,128,128]{2,1,0:T(8,128)S(1)} %get-tuple-element.24), channel_id=1, source_target_pairs={{0,32},{32,64},{64,96},{96,128},{128,160},{160,192},{192,224},{1,3... | collective-permute-start | bytes 589832 | tf_op jit(solution)/shard_map/ppermute | solution.py:40
  72.3 16.4 %collective-permute-start.7 = (f32[3,128,128]{2,1,0:T(8,128)S(1)}, f32[3,128,128]{2,1,0:T(8,128)S(1)}, u32[]{:S(2)}, u32[]{:S(2)}) collective-permute-start(f32[3,128,128]{2,1,0:T(8,128)S(1)} %get-tuple-element.25), channel_id=1, source_target_pairs={{32,0},{64,32},{96,64},{128,96},{160,128},{192,160},{224,192},{33,... | collective-permute-start | bytes 589832 | tf_op jit(solution)/shard_map/ppermute | solution.py:40
  77.0 19.6 %all-to-all-start.1 = ((f32[8,16,256]{2,1,0:T(8,128)}), f32[8,16,256]{2,1,0:T(8,128)S(1)}, u32[]{:S(2)}, u32[]{:S(2)}) async-start(f32[8,16,256]{2,1,0:T(8,128)} %broadcast_in_dim.15), calls=%async_computation.1 | async-start | bytes 262144 | tf_op jit(solution)/shard_map/all_to_all | solution.py:176
  88.7 15.2 %copy-start.11 = (f32[2,128,128]{2,1,0:T(8,128)}, f32[2,128,128]{2,1,0:T(8,128)S(1)}, u32[]{:S(2)}) copy-start(f32[2,128,128]{2,1,0:T(8,128)S(1)} %fusion.5) | copy-start | bytes 393220
  88.7 15.1 %collective-permute-start.9 = (f32[2,128,128]{2,1,0:T(8,128)S(1)}, f32[2,128,128]{2,1,0:T(8,128)S(1)}, u32[]{:S(2)}, u32[]{:S(2)}) collective-permute-start(f32[2,128,128]{2,1,0:T(8,128)S(1)} %fusion.5), channel_id=1, source_target_pairs={{32,0},{64,32},{96,64},{128,96},{160,128},{192,160},{224,192},{33,... | collective-permute-start | bytes 393224 | tf_op jit(solution)/shard_map/ppermute | solution.py:40
  90.7 13.2 %collective-permute-start.8 = (f32[2,128,128]{2,1,0:T(8,128)S(1)}, f32[2,128,128]{2,1,0:T(8,128)S(1)}, u32[]{:S(2)}, u32[]{:S(2)}) collective-permute-start(f32[2,128,128]{2,1,0:T(8,128)S(1)} %fusion.5), channel_id=1, source_target_pairs={{0,32},{32,64},{64,96},{96,128},{128,160},{160,192},{192,224},{1,3... | collective-permute-start | bytes 393224 | tf_op jit(solution)/shard_map/ppermute | solution.py:40
  97.4 16.1 %all-to-all-start.2 = ((f32[32,16,256]{2,1,0:T(8,128)}), f32[32,16,256]{2,1,0:T(8,128)S(1)}, u32[]{:S(2)}, u32[]{:S(2)}) async-start(f32[32,16,256]{2,1,0:T(8,128)} %broadcast_in_dim.16), calls=%async_computation.2 | async-start | bytes 1048576 | tf_op jit(solution)/shard_map/all_to_all | solution.py:177
  103.9 13.7 %collective-permute-start.11 = (f32[2,384,128]{2,1,0:T(8,128)S(1)}, f32[2,384,128]{2,1,0:T(8,128)S(1)}, u32[]{:S(2)}, u32[]{:S(2)}) collective-permute-start(f32[2,384,128]{2,1,0:T(8,128)S(1)} %pad_maximum_fusion.refs_2_), channel_id=1, source_target_pairs={{1,0},{2,1},{3,2},{4,3},{5,4},{6,5},{7,6},{8,7},{9,8},{10,9},{11,1... | collective-permute-start | bytes 1179656 | tf_op jit(solution)/shard_map/ppermute | solution.py:40
  106.2 13.0 %collective-permute-start.10 = (f32[2,384,128]{2,1,0:T(8,128)S(1)}, f32[2,384,128]{2,1,0:T(8,128)S(1)}, u32[]{:S(2)}, u32[]{:S(2)}) collective-permute-start(f32[2,384,128]{2,1,0:T(8,128)S(1)} %pad_maximum_fusion.refs_2_), channel_id=1, source_target_pairs={{0,1},{1,2},{2,3},{3,4},{4,5},{5,6},{6,7},{7,8},{8,9},{9,10},{10,1... | collective-permute-start | bytes 1179656 | tf_op jit(solution)/shard_map/ppermute | solution.py:40
  119.2 0.7 copy-start.2
  120.0 1.0 copy-start.3
  121.0 1.0 copy-start.5
  122.0 1.0 copy-start.7
  123.0 1.0 copy-start.9
  138.8 0.8 copy-start
  139.7 33.5 %collective-permute-start.12 = (f32[3,384,128]{2,1,0:T(8,128)}, f32[3,384,128]{2,1,0:T(8,128)S(1)}, u32[]{:S(2)}, u32[]{:S(2)}) collective-permute-start(f32[3,384,128]{2,1,0:T(8,128)} %get-tuple-element.18), channel_id=1, source_target_pairs={{0,1},{1,2},{2,3},{3,4},{4,5},{5,6},{6,7},{7,8},{8,9},{9,10},{10,1... | collective-permute-start | bytes 1769480 | tf_op jit(solution)/shard_map/ppermute | solution.py:40
  145.5 27.6 %collective-permute-start.13 = (f32[3,384,128]{2,1,0:T(8,128)S(1)}, f32[3,384,128]{2,1,0:T(8,128)S(1)}, u32[]{:S(2)}, u32[]{:S(2)}) collective-permute-start(f32[3,384,128]{2,1,0:T(8,128)S(1)} %get-tuple-element.19), channel_id=1, source_target_pairs={{1,0},{2,1},{3,2},{4,3},{5,4},{6,5},{7,6},{8,7},{9,8},{10,9},{11,1... | collective-permute-start | bytes 1769480 | tf_op jit(solution)/shard_map/ppermute | solution.py:40
  166.6 14.5 %all-to-all-start.4 = ((f32[8,16,256]{2,1,0:T(8,128)}), f32[8,16,256]{2,1,0:T(8,128)S(1)}, u32[]{:S(2)}, u32[]{:S(2)}) async-start(f32[8,16,256]{2,1,0:T(8,128)} %broadcast_in_dim.17), calls=%async_computation.4 | async-start | bytes 262144 | tf_op jit(solution)/shard_map/all_to_all | solution.py:176
  173.3 15.7 %collective-permute-start.14 = (f32[3,128,128]{2,1,0:T(8,128)S(1)}, f32[3,128,128]{2,1,0:T(8,128)S(1)}, u32[]{:S(2)}, u32[]{:S(2)}) collective-permute-start(f32[3,128,128]{2,1,0:T(8,128)S(1)} %get-tuple-element.22), channel_id=1, source_target_pairs={{0,32},{32,64},{64,96},{96,128},{128,160},{160,192},{192,224},{1,3... | collective-permute-start | bytes 589832 | tf_op jit(solution)/shard_map/ppermute | solution.py:40
  175.3 13.6 %collective-permute-start.15 = (f32[3,128,128]{2,1,0:T(8,128)S(1)}, f32[3,128,128]{2,1,0:T(8,128)S(1)}, u32[]{:S(2)}, u32[]{:S(2)}) collective-permute-start(f32[3,128,128]{2,1,0:T(8,128)S(1)} %get-tuple-element.23), channel_id=1, source_target_pairs={{32,0},{64,32},{96,64},{128,96},{160,128},{192,160},{224,192},{33,... | collective-permute-start | bytes 589832 | tf_op jit(solution)/shard_map/ppermute | solution.py:40
  182.0 16.7 %all-to-all-start.5 = ((f32[32,16,256]{2,1,0:T(8,128)}), f32[32,16,256]{2,1,0:T(8,128)S(1)}, u32[]{:S(2)}, u32[]{:S(2)}) async-start(f32[32,16,256]{2,1,0:T(8,128)} %broadcast_in_dim.18), calls=%async_computation.5 | async-start | bytes 1048576 | tf_op jit(solution)/shard_map/all_to_all | solution.py:177
  189.0 0.9 copy-start.12
  198.6 0.8 copy-start.10

commit v2 on v1

v2 whole, which is shorter than its diff:
```python
import math

import jax
import jax.numpy as jnp
import numpy as np
from jax import lax
from jax.experimental import pallas as pl
from jax.experimental.pallas import tpu as pltpu
from jax.sharding import Mesh, PartitionSpec as P

STEP = 64
ITERS = 2
ROW = ("x", "yl")
COL = ("z", "yh", "core")
PLANE = ("x", "yl", "yh")
CHUNK = 256
UNROLL = 1
VMEM_LIMIT = 14 * 1024 * 1024
SMALL = 8 * 1024 * 1024
f32 = jnp.float32
bf16 = jnp.bfloat16
VMEM = pl.BlockSpec(memory_space=pltpu.VMEM)
HBM = pl.BlockSpec(memory_space=pltpu.HBM)
ANY = pl.BlockSpec(memory_space=pl.ANY)
SMEM = pl.BlockSpec(memory_space=pltpu.SMEM)


def dft_table(side_len):
    index = np.arange(side_len)
    angles = (np.outer(index, index) % side_len).astype(np.float32) * np.float32(
        2.0 * math.pi / side_len
    )
    scaling = np.float32(1.0 / math.sqrt(side_len))
    real = np.cos(angles) * scaling
    imag = -np.sin(angles) * scaling
    return np.concatenate([real, imag], axis=1).astype(bf16)


def call(kernel, out_shape, operands, name, scratch=(), scalars=1, flops=0, limit=SMALL, after=()):
    many = isinstance(out_shape, (tuple, list))
    moved = sum(math.prod(o.shape) * o.dtype.itemsize for o in operands)
    waits = len(after)

    def body(*refs):
        kernel(*refs[waits:])

    operands = (*after, *operands)
    return pl.pallas_call(
        body,
        out_shape=out_shape,
        in_specs=[ANY] * waits
        + [SMEM] * scalars
        + [VMEM] * (len(operands) - scalars - waits),
        out_specs=[VMEM] * len(out_shape) if many else VMEM,
        scratch_shapes=list(scratch),
        compiler_params=pltpu.CompilerParams(vmem_limit_bytes=limit),
        cost_estimate=pl.CostEstimate(flops=flops, bytes_accessed=moved, transcendentals=0),
        name=name,
    )(*operands)


def shape(*dims):
    return jax.ShapeDtypeStruct(dims, f32)


def pair_swap(value, axis, first):
    count = lax.axis_size(axis)
    pairs = []
    for i in range(first, count - 1, 2):
        pairs += [(i, i + 1), (i + 1, i)]
    return lax.ppermute(value, axis, pairs)


def renewed(probe, own, other, core, out):
    side = probe.shape[-1]
    square = jnp.zeros((8, side), f32)
    for part in (own, other):
        part = part[...]
        square = square + jnp.sum((part * part).reshape(side // 8, 8, side), axis=0)
    spread = jnp.sqrt(jnp.sum(square) / (2.0 * side * side) + 1e-06)
    scale = jnp.full((8, side), 1.0, f32) / spread
    scale = jnp.broadcast_to(scale[None], (side // 8, 8, side)).reshape(side, side)
    out[core] = probe[core] + own[...] * scale
    out[1 - core] = probe[1 - core] + other[...] * scale


def update_kernel(renew, ids, starts, own, other, sib, mid, cross, amplitude_in, probe_in, table_in,
                  mid_out, keep, give, probe_out, sib_out, cross_out,
                  strips, amplitude, probe, table, first, second, acc, grad, window, wave, field, bent, sems):
    side = probe.shape[-1]
    count = amplitude.shape[0]
    chunks = side // CHUNK
    core = ids[0]
    near, far = 2 * (1 - core), 2 * core
    tall = pl.ds(0, side + side // 2)
    moves = [
        pltpu.make_async_copy(a, b, sems.at[n])
        for n, (a, b) in enumerate((
            (probe_in, probe),
            (mid.at[:, tall], strips.at[1]),
            (sib.at[:, tall], strips.at[near]),
            (cross.at[:, tall], strips.at[far]),
            (table_in, table),
            (amplitude_in, amplitude),
            (acc.at[near], sib_out),
            (acc.at[far], cross_out),
        ))
    ]
    for move in moves[:6]:
        move.start()
    acc[...] = jnp.zeros_like(acc)
    moves[0].wait()
    if renew:
        renewed(probe, own, other, core, probe)
    probe_out[...] = probe[...]
    for move in moves[1:4]:
        move.wait()
    for p in range(count):
        row_start = starts[p, 0]
        col_start = starts[p, 1]

        def load(i, _):
            here = pl.ds(pl.multiple_of(i * CHUNK, CHUNK), CHUNK)
            there = pl.ds(row_start + i * CHUNK, CHUNK)
            cut = []
            for c in range(2):
                wide = jnp.concatenate([strips[k, c, there, :] for k in range(3)], axis=1)
                part = pltpu.roll(wide, 3 * 128 - col_start, 1)[:, :side]
                window[c, here, :] = part
                cut.append(part)
            pr, pi = probe[0, here, :], probe[1, here, :]
            er = pr * cut[0] - pi * cut[1]
            ei = pr * cut[1] + pi * cut[0]
            wave[0, here, :] = er
            wave[1, here, :] = ei
            bent[here, :] = er.astype(bf16)
            bent[pl.ds(pl.multiple_of(side + i * CHUNK, CHUNK), CHUNK), :] = ei.astype(bf16)
            return 0

        lax.fori_loop(0, chunks, load, 0, unroll=UNROLL)
        if p == 0:
            for move in moves[4:6]:
                move.wait()
            real, imag = table[:, :side], table[:, side:]
            first[:side, :side] = real
            first[:side, side:] = -imag
            first[side:, :side] = imag
            first[side:, side:] = real
            second[:side, :side] = real
            second[:side, side:] = imag
            second[side:, :side] = -imag
            second[side:, side:] = real
        half = jnp.dot(first[...], bent[...], preferred_element_type=f32).astype(bf16)
        half = jnp.concatenate([half[:side], half[side:]], axis=1)
        field[...] = jnp.dot(half, second[...], preferred_element_type=f32)

        def project(i, _):
            here = pl.ds(pl.multiple_of(i * CHUNK, CHUNK), CHUNK)
            fr, fi = field[here, :side], field[here, side:]
            scale = amplitude[p, here, :] * lax.rsqrt(jnp.maximum(fr * fr + fi * fi, 0.25))
            bent[here, :] = (fr * scale).astype(bf16)
            bent[pl.ds(pl.multiple_of(side + i * CHUNK, CHUNK), CHUNK), :] = (fi * scale).astype(bf16)
            return 0

        lax.fori_loop(0, chunks, project, 0, unroll=UNROLL)
        half = jnp.dot(second[...], bent[...], preferred_element_type=f32).astype(bf16)
        half = jnp.concatenate([half[:side], half[side:]], axis=1)
        field[...] = jnp.dot(half, first[...], preferred_element_type=f32)

        def spread_out(i, _):
            here = pl.ds(pl.multiple_of(i * CHUNK, CHUNK), CHUNK)
            there = pl.ds(row_start + i * CHUNK, CHUNK)
            dr = field[here, :side] - wave[0, here, :]
            di = field[here, side:] - wave[1, here, :]
            pr, pi = probe[0, here, :], probe[1, here, :]
            wr, wi = window[0, here, :], window[1, here, :]
            gr = wr * dr + wi * di
            gi = wr * di - wi * dr
            if p > 0:
                gr = gr + grad[0, here, :]
                gi = gi + grad[1, here, :]
            if p < count - 1:
                grad[0, here, :] = gr
                grad[1, here, :] = gi
            else:
                keep[here, :] = jnp.where(core == 0, gr, gi)
                give[here, :] = jnp.where(core == 0, gi, gr)
            terms = (pr * dr + pi * di, pr * di - pi * dr)
            for c, term in enumerate(terms):
                wide = jnp.concatenate([term, jnp.zeros((CHUNK, 128), f32)], axis=1)
                moved = pltpu.roll(wide, col_start, 1)
                for k in range(3):
                    acc[k, c, there, :] += moved[:, 128 * k : 128 * (k + 1)]
            return 0

        lax.fori_loop(0, chunks, spread_out, 0, unroll=UNROLL)
    moves[6].start()
    moves[7].start()
    mid_out[...] = acc[1]
    for move in moves[6:]:
        move.wait()


def update(renew, ids, starts, parts, amplitude, probe, own, other, table):
    side = probe.shape[-1]
    rows, cols = side + side // 2, parts[0].shape[2]
    strip, square, wave = shape(2, rows, cols), shape(side, side), shape(2, side, side)
    count = amplitude.shape[0]
    return pl.pallas_call(
        lambda *refs: update_kernel(renew, *refs),
        out_shape=(strip, square, square, wave, strip, strip),
        in_specs=[SMEM] * 2 + [VMEM] * 2 + [HBM] * 6,
        out_specs=[VMEM] * 4 + [HBM] * 2,
        scratch_shapes=(
            pltpu.VMEM((3, 2, rows, cols), f32),
            pltpu.VMEM((count, side, side), f32),
            pltpu.VMEM((2, side, side), f32),
            pltpu.VMEM((side, 2 * side), bf16),
            pltpu.VMEM((2 * side, 2 * side), bf16),
            pltpu.VMEM((2 * side, 2 * side), bf16),
            pltpu.VMEM((3, 2, rows, cols), f32),
            pltpu.VMEM((2, side, side), f32),
            pltpu.VMEM((2, side, side), f32),
            pltpu.VMEM((2, side, side), f32),
            pltpu.VMEM((side, 2 * side), f32),
            pltpu.VMEM((2 * side, side), bf16),
            pltpu.SemaphoreType.DMA((8,)),
        ),
        compiler_params=pltpu.CompilerParams(vmem_limit_bytes=VMEM_LIMIT),
        cost_estimate=pl.CostEstimate(
            flops=count * 64 * side**3, bytes_accessed=0, transcendentals=0
        ),
        name="update",
    )(ids, starts, own, other, *parts, amplitude, probe, table)


def hold(value, after):
    return pl.pallas_call(
        lambda *refs: None,
        out_shape=jax.ShapeDtypeStruct(value.shape, value.dtype),
        in_specs=[ANY, ANY],
        out_specs=ANY,
        input_output_aliases={0: 0},
        name="hold",
    )(value, after)


def finish(ids, probe, own, other):
    def kernel(ids, probe, own, other, out):
        renewed(probe, own, other, ids[0], out)

    return call(kernel, shape(*probe.shape), (ids, probe, own, other), "finish")


def sum_and_repeat(value, copies, after):
    def kernel(value, out):
        added = value[0]
        for i in range(1, value.shape[0]):
            added = added + value[i]
        for i in range(copies):
            out[i] = added

    return call(kernel, shape(copies, *value.shape[1:]), (value,), "sum_repeat", scalars=0, after=after)


def add_into_ways(a, b, ways):
    return (a + b).reshape(ways, -1, a.shape[-1])


def scatter(keep, give):
    plane = math.prod(lax.axis_size(a) for a in PLANE)
    return lax.all_to_all(add_into_ways(keep, pair_swap(give, "core", 0), plane), PLANE, 0, 0)


def gather(part, first, second, third=None):
    plane = part.shape[0]
    part = sum_and_repeat(part, lax.axis_size("z"), first)
    part = sum_and_repeat(lax.all_to_all(part, "z", 0, 0), plane, second)
    own = lax.all_to_all(part, PLANE, 0, 0).reshape(-1, part.shape[-1])
    if third is not None:
        own = hold(own, third)
    return own, pair_swap(own, "core", 0)


def widen(ids, tile):
    channels, rows, cols = tile.shape
    side = cols
    tags = rows - side

    def kernel(ids, near, tile, far, out):
        flip = ids[1]
        for ref, place in ((near, 2 * (1 - flip)), (tile, 1), (far, 2 * flip)):
            out[:, pl.ds(pl.multiple_of(side * place, side), side), :] = ref[:, :side, :]
            if tags:
                there = pl.ds(pl.multiple_of(3 * side + tags * place, tags), tags)
                out[:, there, :] = ref[:, side:, :]

    far = pair_swap(tile, ROW, 1)
    near = pair_swap(tile, ROW, 0)
    tall = call(kernel, shape(channels, 3 * rows, cols), (ids, near, tile, far), "stack")
    return pair_swap(tall, COL, 0), tall, pair_swap(tall, COL, 1)


def light(ids, spots, probe):
    side = probe.shape[-1]
    half = side // 2

    def kernel(ids, spots, probe, out, pad):
        core = ids[0]
        bright = probe[0] * probe[0] + probe[1] * probe[1]
        pad[...] = jnp.zeros_like(pad)
        pad[1, half : half + side, :] = bright[:, :half]
        pad[2, half : half + side, :] = bright[:, half:]
        added = jnp.zeros((half, half), f32)
        for k, beside in enumerate((1 - 2 * core, 0, 2 * core - 1)):
            for r in range(3):
                for p in range(spots.shape[2] // 2):
                    tag = spots[k, r, 2 * p]
                    u = jnp.where(tag > 0, side + 1 - tag - (r - 1) * half, 0)
                    v = side + 1 - spots[k, r, 2 * p + 1] - beside * half
                    v = jnp.where(tag > 0, v, 0)
                    lane = jnp.bitwise_and(v, half - 1)
                    block = lax.div(v, half)
                    here = pl.ds(u, half)
                    wide = jnp.concatenate([pad[block, here, :], pad[block + 1, here, :]], axis=1)
                    moved = pltpu.roll(wide, jnp.bitwise_and(side - lane, side - 1), 1)
                    added = added + moved[:, :half]
        out[...] = added

    return call(
        kernel,
        shape(half, half),
        (ids, spots, probe),
        "light",
        scratch=(pltpu.VMEM((5, 2 * side, half), f32),),
        scalars=2,
        flops=2 * 10**9,
    )


def fold(ids, tile, bright, sib, mid, cross):
    channels, tall, cols = mid.shape
    rows = tall // 3

    def split(ids, mid, sib, cross, near, own, far):
        flip = ids[1]

        def part(start):
            here = pl.ds(start, rows)
            return mid[:, here, :] + sib[:, here, :] + cross[:, here, :]

        near[...] = part(pl.multiple_of(2 * rows * (1 - flip), rows))
        own[...] = part(rows)
        far[...] = part(pl.multiple_of(2 * rows * flip, rows))

    def renew(tile, bright, near, own, far, out):
        part = near[...] + own[...] + far[...]
        out[...] = tile[...] + part / (bright[...] + 1.0)

    cross = pair_swap(cross, COL, 1)
    sib = pair_swap(sib, COL, 0)
    near, own, far = call(split, [shape(channels, rows, cols)] * 3, (ids, mid, sib, cross), "split")
    far = pair_swap(far, ROW, 1)
    near = pair_swap(near, ROW, 0)
    return own, call(renew, shape(*tile.shape), (tile, bright, near, own, far), "renew", scalars=0)


def on_device(patterns, background, offsets, probe, tile):
    side = probe.shape[-1]
    rows, cols = patterns.shape[:2]
    steps = jnp.stack(jnp.meshgrid(jnp.arange(rows), jnp.arange(cols), indexing="ij"), axis=-1)
    starts = (offsets + steps.astype(jnp.int32) * STEP).reshape(rows * cols, 2)
    ids = jnp.stack([lax.axis_index("core"), lax.axis_index("yl")]).astype(jnp.int32)
    amplitude = jnp.sqrt(jnp.maximum(patterns.reshape(rows * cols, side, side) - background, 0.0))
    table = jnp.asarray(dft_table(side))
    own = other = background
    tags = starts.reshape(1, 1, 2 * rows * cols).astype(f32) + 1.0
    tags = jnp.pad(tags, ((0, 0), (0, 7), (0, tile.shape[2] - tags.shape[2])))
    tags = jnp.broadcast_to(tags, (2,) + tags.shape[1:])
    parts = widen(ids, jnp.concatenate([tile, tags], axis=1))
    tall = side + side // 2
    spots = jnp.stack([v[0, tall::8, : 2 * rows * cols] for v in parts]).astype(jnp.int32)
    for step in range(ITERS):
        mid, keep, give, new_probe, sib, cross = update(
            step > 0, ids, starts, parts, amplitude, probe, own, other, table
        )
        if step > 0:
            probe = new_probe
        bright = light(ids, spots, probe)
        part = scatter(keep, give)
        last = step == ITERS - 1
        if last:
            cross = hold(cross, part)
        centre, tile = fold(ids, tile, bright, sib, mid, cross)
        if last:
            own, other = gather(part, (), (centre,), tile)
        else:
            parts = widen(ids, tile)
            own, other = gather(part, (tile,), (parts[1],))
    return tile, finish(ids, probe, own, other)


def solution(mesh):
    fine = Mesh(mesh.devices.reshape(4, 2, 8, 2, 2), ROW + COL)
    return jax.shard_map(
        on_device,
        mesh=fine,
        in_specs=(P(ROW, COL, None, None), P(), P(ROW, COL, None), P(), P(None, ROW, COL)),
        out_specs=(P(None, ROW, COL), P()),
        check_vma=False,
    )
```

time: 205 us -> 179 us (0.87); the launches traced: 202 us -> 178 us
  blocking collectives: 18.4 us -> 0 us
  waiting for transfers between devices: 39.3 us -> 55.7 us
  starting transfers between devices: 94.1 us -> 80.9 us
  Pallas kernels: 31.6 us -> 27.2 us
  local copies, waits for them, and re-layouts: 12.2 us -> 8.36 us
    all_to_all x1 -> x0, blocking collectives: 18.4 us -> none  [total(): part = jnp.sum(lax.all_to_all(flat, NEAR, 0, 0), axis=0)]
    ppermute x16 -> x20, waiting for transfers between devices: 24.7 us -> 42.4 us  [pair_swap(): return lax.ppermute(value, axis, pairs)]
    pallas_call x2, Pallas kernels: 29.3 us -> 15.6 us  [update(): pl.pallas_call(lambda *refs: update_kernel(renew, *refs), out_shape=(stri...]
    ppermute x16 -> x20, starting transfers between devices: 54.6 us -> 42.1 us  [pair_swap(): return lax.ppermute(value, axis, pairs)]
    pallas_call x1 -> x15, Pallas kernels: 2.28 us -> 11.6 us  [the longest x13 11.6 us: call(): pl.pallas_call(body, out_shape=out_shape, in_specs=[ANY] * waits + [SMEM]...]
    broadcast_in_dim x4 -> x2, local copies, waits for them, and re-layouts: 3.04 us -> 0.01 us  [on_device(): tags = jnp.broadcast_to(tags, (2,) + tags.shape[1:])]
    unnamed x36 -> x38, local copies, waits for them, and re-layouts: 9.04 us -> 7.5 us
    all_to_all x5 -> x6, waiting for transfers between devices: 14.6 us -> 13.3 us  [the longest x2 7.74 us: gather(): part = sum_and_repeat(lax.all_to_all(part, 'z', 0, 0), plane, second)]
  transfers between devices with their start and end apart: 21 -> 26, of which waited for: 11 -> 15; matrix products, arithmetic and copies ran while one was open for 4% -> 2% of each run, Pallas kernels for 0% -> 4%
where the time goes in v2:
time: 179 us; the launch traced here: 178 us
  starting transfers between devices  80.9 us (45%)
  waiting for transfers between devices  55.7 us (31%)
  Pallas kernels  27.2 us (15%)
  local copies, waits for them, and re-layouts  8.36 us (5%)
  other arithmetic  5.05 us (3%)
    ppermute x20, waiting for transfers between devices, pair_swap(): return lax.ppermute(value, axis, pairs)  42.4 us
    ppermute x20, starting transfers between devices, pair_swap(): return lax.ppermute(value, axis, pairs)  42.1 us
    pallas_call x2, Pallas kernels, update(): pl.pallas_call(lambda *refs: update_kernel(renew, *refs), out_shape=(stri...  15.6 us
    all_to_all x2, starting transfers between devices, scatter(): lax.all_to_all(add_into_ways(keep, pair_swap(give, 'core', 0), plane), PL...  14 us
    all_to_all x2, starting transfers between devices, gather(): part = sum_and_repeat(lax.all_to_all(part, 'z', 0, 0), plane, second)  13.7 us
    pallas_call x13, Pallas kernels, call(): pl.pallas_call(body, out_shape=out_shape, in_specs=[ANY] * waits + [SMEM]...  11.6 us
    all_to_all x2, starting transfers between devices, gather(): own = lax.all_to_all(part, PLANE, 0, 0).reshape(-1, part.shape[-1])  11.2 us
    all_to_all x2, waiting for transfers between devices, gather(): part = sum_and_repeat(lax.all_to_all(part, 'z', 0, 0), plane, second)  7.74 us
  transfers between devices with their start and end apart: 26, of which 15 were waited for; matrix products, arithmetic and copies ran while one was open for 2% of the time, Pallas kernels for 4%

profile of v2, /device:TPU:3, one launch (start us, length us, event | category | flops | bytes accessed | tf_op | source)
XLA Modules:
  0.0 178.1 jit_solution(6898968936857102403)
XLA Ops:
  0.7 0.7 copy-done.18
  1.5 0.9 pad_maximum_fusion.refs_2_
  2.4 3.2 %collective-permute-start.1 = (f32[2,136,128]{2,1,0:T(8,128)S(1)}, f32[2,136,128]{2,1,0:T(8,128)S(1)}, u32[]{:S(2)}, u32[]{:S(2)}) collective-permute-start(f32[2,136,128]{2,1,0:T(8,128)S(1)} %pad_maximum_fusion.refs_2_), channel_id=1, source_target_pairs={{32,64},{64,32},{96,128},{128,96},{160,192},{192,160},{33,65},{65,... | collective-permute-start | bytes 417800 | tf_op jit(solution)/shard_map/ppermute | solution.py:71
  5.6 1.2 collective-permute-start
  6.9 2.9 %collective-permute-done.1.refs_3_ = f32[2,136,128]{2,1,0:T(8,128)S(1)} collective-permute-done((f32[2,136,128]{2,1,0:T(8,128)S(1)}, f32[2,136,128]{2,1,0:T(8,128)S(1)}, u32[]{:S(2)}, u32[]{:S(2)}) %collective-permute-start.1) | collective-permute-done | bytes 139296 | tf_op jit(solution)/shard_map/ppermute | solution.py:71
  9.7 4.0 %collective-permute-done.refs_1_ = f32[2,136,128]{2,1,0:T(8,128)S(1)} collective-permute-done((f32[2,136,128]{2,1,0:T(8,128)S(1)}, f32[2,136,128]{2,1,0:T(8,128)S(1)}, u32[]{:S(2)}, u32[]{:S(2)}) %collective-permute-start) | collective-permute-done | bytes 139296 | tf_op jit(solution)/shard_map/ppermute | solution.py:71
  13.8 0.6 stack.22.refs_5_
  14.4 5.3 %collective-permute-start.3 = (f32[2,408,128]{2,1,0:T(8,128)S(1)}, f32[2,408,128]{2,1,0:T(8,128)S(1)}, u32[]{:S(2)}, u32[]{:S(2)}) collective-permute-start(f32[2,408,128]{2,1,0:T(8,128)S(1)} %stack.22.refs_5_), channel_id=1, source_target_pairs={{1,2},{2,1},{3,4},{4,3},{5,6},{6,5},{7,8},{8,7},{9,10},{10,9},{11,... | collective-permute-start | bytes 1253384 | tf_op jit(solution)/shard_map/ppermute | solution.py:71
  19.8 1.5 fusion.1.refs_7_
  21.4 7.8 %collective-permute-done.3.refs_6_ = f32[2,408,128]{2,1,0:T(8,128)S(1)} collective-permute-done((f32[2,408,128]{2,1,0:T(8,128)S(1)}, f32[2,408,128]{2,1,0:T(8,128)S(1)}, u32[]{:S(2)}, u32[]{:S(2)}) %collective-permute-start.3) | collective-permute-done | bytes 417824 | tf_op jit(solution)/shard_map/ppermute | solution.py:71
  29.2 8.2 %update.2 = (f32[2,384,128]{2,1,0:T(8,128)S(1)}, f32[256,256]{1,0:T(8,128)S(1)}, f32[256,256]{1,0:T(8,128)}, f32[2,256,256]{2,1,0:T(8,128)}, f32[2,384,128]{2,1,0:T(8,128)}, /*index=5*/f32[2,384,128]{2,1,0:T(8,128)}) custom-call(s32[2]{0:T(128)S(1)} %pad_add_fusion.refs_0_, s32[4,2]{1,0:T(4,128)S(1)} %bitcast.18, f32[256,256]{1,0:T(8,128)S(1)} %copy-done.6, ...), custom_call_target="tpu_custom_call" | custom-call | flops 4294967296 | tf_op jit(solution)/shard_map/update/pallas_call | solution.py:209
  37.5 5.9 %collective-permute-start.5 = (f32[2,384,128]{2,1,0:T(8,128)}, f32[2,384,128]{2,1,0:T(8,128)S(1)}, u32[]{:S(2)}, u32[]{:S(2)}) collective-permute-start(f32[2,384,128]{2,1,0:T(8,128)} %get-tuple-element.21), channel_id=1, source_target_pairs={{1,2},{2,1},{3,4},{4,3},{5,6},{6,5},{7,8},{8,7},{9,10},{10,9},{11,... | collective-permute-start | bytes 1179656 | tf_op jit(solution)/shard_map/ppermute | solution.py:71
  43.6 0.7 slice.9
  44.3 1.1 collective-permute-done.10
  45.4 1.7 add.28
  47.1 6.1 %all-to-all-start = ((f32[16,16,256]{2,1,0:T(8,128)}), f32[16,16,256]{2,1,0:T(8,128)S(1)}, u32[]{:S(2)}, u32[]{:S(2)}) async-start(f32[16,16,256]{2,1,0:T(8,128)} %bitcast.5), calls=%async_computation | async-start | bytes 524288 | tf_op jit(solution)/shard_map/all_to_all | solution.py:272
  53.3 0.6 split.2
  53.9 1.3 collective-permute-start.6
  55.1 2.1 %collective-permute-start.7 = (f32[2,128,128]{2,1,0:T(8,128)S(1)}, f32[2,128,128]{2,1,0:T(8,128)S(1)}, u32[]{:S(2)}, u32[]{:S(2)}) collective-permute-start(f32[2,128,128]{2,1,0:T(8,128)S(1)} %get-tuple-element.24), channel_id=1, source_target_pairs={{32,64},{64,32},{96,128},{128,96},{160,192},{192,160},{33,65},{65,... | collective-permute-start | bytes 393224 | tf_op jit(solution)/shard_map/ppermute | solution.py:71
  57.3 2.0 %light.2.refs_1_ = f32[128,128]{1,0:T(8,128)S(1)} custom-call(s32[2]{0:T(128)S(1)} %pad_add_fusion.refs_0_, s32[3,3,8]{2,1,0:T(4,128)S(1)} %maximum_convert_fusion.refs_1_, f32[2,256,256]{2,1,0:T(8,128)S(1)} %copy-done.9), custom_call_target="tpu_custom_call" | custom-call | flops 2000000000 | bytes 524584 | tf_op jit(solution)/shard_map/light/pallas_call | solution.py:48
  59.3 4.9 %collective-permute-done.6.refs_2_ = f32[2,128,128]{2,1,0:T(8,128)S(1)} collective-permute-done((f32[2,128,128]{2,1,0:T(8,128)S(1)}, f32[2,128,128]{2,1,0:T(8,128)S(1)}, u32[]{:S(2)}, u32[]{:S(2)}) %collective-permute-start.6) | collective-permute-done | bytes 131104 | tf_op jit(solution)/shard_map/ppermute | solution.py:71
  64.3 0.7 sum_repeat.4
  65.0 7.3 %all-to-all-start.1 = ((f32[8,16,256]{2,1,0:T(8,128)}), f32[8,16,256]{2,1,0:T(8,128)S(1)}, u32[]{:S(2)}, u32[]{:S(2)}) async-start(f32[8,16,256]{2,1,0:T(8,128)} %sum_repeat.4), calls=%async_computation.1 | async-start | bytes 262144 | tf_op jit(solution)/shard_map/all_to_all | solution.py:278
  72.2 3.5 %collective-permute-start.9 = (f32[2,128,128]{2,1,0:T(8,128)S(1)}, f32[2,128,128]{2,1,0:T(8,128)S(1)}, u32[]{:S(2)}, u32[]{:S(2)}) collective-permute-start(f32[2,128,128]{2,1,0:T(8,128)S(1)} %renew.2.refs_2_.refs_0_), channel_id=1, source_target_pairs={{32,64},{64,32},{96,128},{128,96},{160,192},{192,160},{33,65},{65,... | collective-permute-start | bytes 393224 | tf_op jit(solution)/shard_map/ppermute | solution.py:71
  75.7 0.9 collective-permute-start.8
  76.7 2.5 %collective-permute-done.9.refs_3_ = f32[2,128,128]{2,1,0:T(8,128)S(1)} collective-permute-done((f32[2,128,128]{2,1,0:T(8,128)S(1)}, f32[2,128,128]{2,1,0:T(8,128)S(1)}, u32[]{:S(2)}, u32[]{:S(2)}) %collective-permute-start.9) | collective-permute-done | bytes 131104 | tf_op jit(solution)/shard_map/ppermute | solution.py:71
  79.1 4.0 %collective-permute-done.8.refs_1_ = f32[2,128,128]{2,1,0:T(8,128)S(1)} collective-permute-done((f32[2,128,128]{2,1,0:T(8,128)S(1)}, f32[2,128,128]{2,1,0:T(8,128)S(1)}, u32[]{:S(2)}, u32[]{:S(2)}) %collective-permute-start.8) | collective-permute-done | bytes 131104 | tf_op jit(solution)/shard_map/ppermute | solution.py:71
  83.1 0.6 stack.23.refs_0_.refs_5_
  83.7 0.7 sum_repeat.5
  84.5 5.6 %all-to-all-start.2 = ((f32[16,16,256]{2,1,0:T(8,128)}), f32[16,16,256]{2,1,0:T(8,128)S(1)}, u32[]{:S(2)}, u32[]{:S(2)}) async-start(f32[16,16,256]{2,1,0:T(8,128)} %sum_repeat.5), calls=%async_computation.2 | async-start | bytes 524288 | tf_op jit(solution)/shard_map/all_to_all | solution.py:279
  90.1 6.0 %collective-permute-start.13 = (f32[2,384,128]{2,1,0:T(8,128)S(1)}, f32[2,384,128]{2,1,0:T(8,128)S(1)}, u32[]{:S(2)}, u32[]{:S(2)}) collective-permute-start(f32[2,384,128]{2,1,0:T(8,128)S(1)} %stack.23.refs_0_.refs_5_), channel_id=1, source_target_pairs={{1,2},{2,1},{3,4},{4,3},{5,6},{6,5},{7,8},{8,7},{9,10},{10,9},{11,... | collective-permute-start | bytes 1179656 | tf_op jit(solution)/shard_map/ppermute | solution.py:71
  96.2 0.2 all-to-all-done.2
  96.5 2.4 %collective-permute-start.11 = (f32[256,256]{1,0:T(8,128)S(1)}, f32[256,256]{1,0:T(8,128)S(1)}, u32[]{:S(2)}, u32[]{:S(2)}) collective-permute-start(f32[256,256]{1,0:T(8,128)S(1)} %bitcast.16), channel_id=1, source_target_pairs={{0,1},{1,0},{2,3},{3,2},{4,5},{5,4},{6,7},{7,6},{8,9},{9,8},{10,11... | collective-permute-start | bytes 786440 | tf_op jit(solution)/shard_map/ppermute | solution.py:71
  98.9 6.2 %collective-permute-done.13.refs_6_ = f32[2,384,128]{2,1,0:T(8,128)S(1)} collective-permute-done((f32[2,384,128]{2,1,0:T(8,128)S(1)}, f32[2,384,128]{2,1,0:T(8,128)S(1)}, u32[]{:S(2)}, u32[]{:S(2)}) %collective-permute-start.13) | collective-permute-done | bytes 393248 | tf_op jit(solution)/shard_map/ppermute | solution.py:71
  105.1 0.8 copy-done.12
  105.8 0.7 copy-done.14
  106.6 1.0 copy-done.13
  107.6 1.0 copy-done.15
  108.6 7.4 %update.3 = (f32[2,384,128]{2,1,0:T(8,128)S(1)}, f32[256,256]{1,0:T(8,128)S(1)}, f32[256,256]{1,0:T(8,128)S(1)}, f32[2,256,256]{2,1,0:T(8,128)S(1)}, f32[2,384,1...) custom-call(s32[2]{0:T(128)S(1)} %pad_add_fusion.refs_0_, s32[4,2]{1,0:T(4,128)S(1)} %bitcast.19, f32[256,256]{1,0:T(8,128)S(1)} %bitcast.17, ...), custom_call_target="tpu_custom_call" | custom-call | flops 4294967296 | tf_op jit(solution)/shard_map/update/pallas_call | solution.py:209
  116.0 1.5 collective-permute-done.15
  117.6 0.8 add.29
  118.3 7.8 %all-to-all-start.3 = ((f32[16,16,256]{2,1,0:T(8,128)}), f32[16,16,256]{2,1,0:T(8,128)S(1)}, u32[]{:S(2)}, u32[]{:S(2)}) async-start(f32[16,16,256]{2,1,0:T(8,128)} %bitcast.7), calls=%async_computation.3 | async-start | bytes 524288 | tf_op jit(solution)/shard_map/all_to_all | solution.py:272
  126.2 1.0 collective-permute-start.14
  127.2 5.3 %all-to-all-done.3.refs_1_.refs_0_ = f32[16,16,256]{2,1,0:T(8,128)S(1)} async-done(((f32[16,16,256]{2,1,0:T(8,128)}), f32[16,16,256]{2,1,0:T(8,128)S(1)}, u32[]{:S(2)}, u32[]{:S(2)}) %all-to-all-start.3) | async-done | bytes 262176 | tf_op jit(solution)/shard_map/all_to_all | solution.py:272
  132.5 0.7 copy-done.2
  133.2 4.2 %collective-permute-start.16 = (f32[2,384,128]{2,1,0:T(8,128)}, f32[2,384,128]{2,1,0:T(8,128)S(1)}, u32[]{:S(2)}, u32[]{:S(2)}) collective-permute-start(f32[2,384,128]{2,1,0:T(8,128)} %hold.2), channel_id=1, source_target_pairs={{1,2},{2,1},{3,4},{4,3},{5,6},{6,5},{7,8},{8,7},{9,10},{10,9},{11,... | collective-permute-start | bytes 1179656 | tf_op jit(solution)/shard_map/ppermute | solution.py:71
  137.5 0.9 copy-done.3
  138.4 0.7 sum_repeat.6
  139.1 6.4 %all-to-all-start.4 = ((f32[8,16,256]{2,1,0:T(8,128)}), f32[8,16,256]{2,1,0:T(8,128)S(1)}, u32[]{:S(2)}, u32[]{:S(2)}) async-start(f32[8,16,256]{2,1,0:T(8,128)} %sum_repeat.6), calls=%async_computation.4 | async-start | bytes 262144 | tf_op jit(solution)/shard_map/all_to_all | solution.py:278
  145.5 1.2 collective-permute-done.16.refs_3_
  146.7 0.6 split.3
  147.3 7.7 %all-to-all-done.4.refs_1_ = f32[8,16,256]{2,1,0:T(8,128)S(1)} async-done(((f32[8,16,256]{2,1,0:T(8,128)}), f32[8,16,256]{2,1,0:T(8,128)S(1)}, u32[]{:S(2)}, u32[]{:S(2)}) %all-to-all-start.4) | async-done | bytes 131104 | tf_op jit(solution)/shard_map/all_to_all | solution.py:278
  155.0 0.7 sum_repeat.7
  155.8 5.5 %all-to-all-start.5 = ((f32[16,16,256]{2,1,0:T(8,128)}), f32[16,16,256]{2,1,0:T(8,128)S(1)}, u32[]{:S(2)}, u32[]{:S(2)}) async-start(f32[16,16,256]{2,1,0:T(8,128)} %sum_repeat.7), calls=%async_computation.5 | async-start | bytes 524288 | tf_op jit(solution)/shard_map/all_to_all | solution.py:279
  161.3 1.2 collective-permute-start.17
  162.5 2.1 %collective-permute-start.18 = (f32[2,128,128]{2,1,0:T(8,128)S(1)}, f32[2,128,128]{2,1,0:T(8,128)S(1)}, u32[]{:S(2)}, u32[]{:S(2)}) collective-permute-start(f32[2,128,128]{2,1,0:T(8,128)S(1)} %get-tuple-element.35), channel_id=1, source_target_pairs={{32,64},{64,32},{96,128},{128,96},{160,192},{192,160},{33,65},{65,... | collective-permute-start | bytes 393224 | tf_op jit(solution)/shard_map/ppermute | solution.py:71
  164.6 2.0 %light.3.refs_1_ = f32[128,128]{1,0:T(8,128)S(1)} custom-call(s32[2]{0:T(128)S(1)} %pad_add_fusion.refs_0_, s32[3,3,8]{2,1,0:T(4,128)S(1)} %maximum_convert_fusion.refs_1_, f32[2,256,256]{2,1,0:T(8,128)S(1)} %get-tuple-element.27.refs_2_.refs_1_), custom_call_target="tpu_custom_call" | custom-call | flops 2000000000 | bytes 524584 | tf_op jit(solution)/shard_map/light/pallas_call | solution.py:48
  166.6 4.9 %collective-permute-done.17.refs_2_ = f32[2,128,128]{2,1,0:T(8,128)S(1)} collective-permute-done((f32[2,128,128]{2,1,0:T(8,128)S(1)}, f32[2,128,128]{2,1,0:T(8,128)S(1)}, u32[]{:S(2)}, u32[]{:S(2)}) %collective-permute-start.17) | collective-permute-done | bytes 131104 | tf_op jit(solution)/shard_map/ppermute | solution.py:71
  171.5 0.7 renew.3.refs_1_
  172.2 0.7 copy-done
  172.9 1.2 collective-permute-start.19
  174.1 1.4 collective-permute-done.19.refs_3_
  175.5 0.9 copy-done.1
  176.5 1.6 finish.1
  (58 shorter events, 0.9 us)
Async XLA Ops:
  0.6 0.7 copy-start.18
  2.4 7.3 %collective-permute-start.1 = (f32[2,136,128]{2,1,0:T(8,128)S(1)}, f32[2,136,128]{2,1,0:T(8,128)S(1)}, u32[]{:S(2)}, u32[]{:S(2)}) collective-permute-start(f32[2,136,128]{2,1,0:T(8,128)S(1)} %pad_maximum_fusion.refs_2_), channel_id=1, source_target_pairs={{32,64},{64,32},{96,128},{128,96},{160,192},{192,160},{33,65},{65,... | collective-permute-start | bytes 417800 | tf_op jit(solution)/shard_map/ppermute | solution.py:71
  5.6 8.2 %collective-permute-start = (f32[2,136,128]{2,1,0:T(8,128)S(1)}, f32[2,136,128]{2,1,0:T(8,128)S(1)}, u32[]{:S(2)}, u32[]{:S(2)}) collective-permute-start(f32[2,136,128]{2,1,0:T(8,128)S(1)} %pad_maximum_fusion.refs_2_), channel_id=1, source_target_pairs={{0,32},{32,0},{64,96},{96,64},{128,160},{160,128},{192,224},{224,1... | collective-permute-start | bytes 417800 | tf_op jit(solution)/shard_map/ppermute | solution.py:71
  6.9 12.9 %copy-start.6 = (f32[256,256]{1,0:T(8,128)S(1)}, f32[256,256]{1,0:T(8,128)}, u32[]{:S(2)}) copy-start(f32[256,256]{1,0:T(8,128)} %refs_3_.1) | copy-start | bytes 786436
  14.4 14.8 %copy-start.8 = (f32[2,256,256]{2,1,0:T(8,128)S(1)}, f32[2,256,256]{2,1,0:T(8,128)}, u32[]{:S(2)}) copy-start(f32[2,256,256]{2,1,0:T(8,128)} %refs_8_.3) | copy-start | bytes 1572868
  14.4 14.8 %copy-start.16 = (bf16[256,512]{1,0:T(8,128)(2,1)S(1)}, bf16[256,512]{1,0:T(8,128)(2,1)}, u32[]{:S(2)}) copy-start(bf16[256,512]{1,0:T(8,128)(2,1)} %constant.18.clone.refs_9_) | copy-start | bytes 786436
  14.4 14.8 %collective-permute-start.3 = (f32[2,408,128]{2,1,0:T(8,128)S(1)}, f32[2,408,128]{2,1,0:T(8,128)S(1)}, u32[]{:S(2)}, u32[]{:S(2)}) collective-permute-start(f32[2,408,128]{2,1,0:T(8,128)S(1)} %stack.22.refs_5_), channel_id=1, source_target_pairs={{1,2},{2,1},{3,4},{4,3},{5,6},{6,5},{7,8},{8,7},{9,10},{10,9},{11,... | collective-permute-start | bytes 1253384 | tf_op jit(solution)/shard_map/ppermute | solution.py:71
  19.7 9.4 %collective-permute-start.2 = (f32[2,408,128]{2,1,0:T(8,128)S(1)}, f32[2,408,128]{2,1,0:T(8,128)S(1)}, u32[]{:S(2)}, u32[]{:S(2)}) collective-permute-start(f32[2,408,128]{2,1,0:T(8,128)S(1)} %stack.22.refs_5_), channel_id=1, source_target_pairs={{0,1},{1,0},{2,3},{3,2},{4,5},{5,4},{6,7},{7,6},{8,9},{9,8},{10,11... | collective-permute-start | bytes 1253384 | tf_op jit(solution)/shard_map/ppermute | solution.py:71
  29.2 8.3 %copy-start.7 = (f32[2,408,128]{2,1,0:T(8,128)}, f32[2,408,128]{2,1,0:T(8,128)S(1)}, u32[]{:S(2)}) copy-start(f32[2,408,128]{2,1,0:T(8,128)S(1)} %collective-permute-done.2.refs_4_) | copy-start | bytes 1253380
  37.4 15.8 %collective-permute-start.4 = (f32[2,384,128]{2,1,0:T(8,128)}, f32[2,384,128]{2,1,0:T(8,128)S(1)}, u32[]{:S(2)}, u32[]{:S(2)}) collective-permute-start(f32[2,384,128]{2,1,0:T(8,128)} %get-tuple-element.20), channel_id=1, source_target_pairs={{0,1},{1,0},{2,3},{3,2},{4,5},{5,4},{6,7},{7,6},{8,9},{9,8},{10,11... | collective-permute-start | bytes 1179656 | tf_op jit(solution)/shard_map/ppermute | solution.py:71
  37.5 15.7 %collective-permute-start.5 = (f32[2,384,128]{2,1,0:T(8,128)}, f32[2,384,128]{2,1,0:T(8,128)S(1)}, u32[]{:S(2)}, u32[]{:S(2)}) collective-permute-start(f32[2,384,128]{2,1,0:T(8,128)} %get-tuple-element.21), channel_id=1, source_target_pairs={{1,2},{2,1},{3,4},{4,3},{5,6},{6,5},{7,8},{8,7},{9,10},{10,9},{11,... | collective-permute-start | bytes 1179656 | tf_op jit(solution)/shard_map/ppermute | solution.py:71
  43.4 2.0 %collective-permute-start.10 = (f32[256,256]{1,0:T(8,128)}, f32[256,256]{1,0:T(8,128)}, u32[]{:S(2)}, u32[]{:S(2)}) collective-permute-start(f32[256,256]{1,0:T(8,128)} %get-tuple-element.26), channel_id=1, source_target_pairs={{0,1},{1,0},{2,3},{3,2},{4,5},{5,4},{6,7},{7,6},{8,9},{9,8},{10,11... | collective-permute-start | bytes 786440 | tf_op jit(solution)/shard_map/ppermute | solution.py:71
  47.1 17.2 %all-to-all-start = ((f32[16,16,256]{2,1,0:T(8,128)}), f32[16,16,256]{2,1,0:T(8,128)S(1)}, u32[]{:S(2)}, u32[]{:S(2)}) async-start(f32[16,16,256]{2,1,0:T(8,128)} %bitcast.5), calls=%async_computation | async-start | bytes 524288 | tf_op jit(solution)/shard_map/all_to_all | solution.py:272
  53.3 4.0 %copy-start.9 = (f32[2,256,256]{2,1,0:T(8,128)S(1)}, f32[2,256,256]{2,1,0:T(8,128)}, u32[]{:S(2)}) copy-start(f32[2,256,256]{2,1,0:T(8,128)} %refs_8_.3) | copy-start | bytes 1572868
  53.9 10.4 %collective-permute-start.6 = (f32[2,128,128]{2,1,0:T(8,128)S(1)}, f32[2,128,128]{2,1,0:T(8,128)S(1)}, u32[]{:S(2)}, u32[]{:S(2)}) collective-permute-start(f32[2,128,128]{2,1,0:T(8,128)S(1)} %get-tuple-element.22), channel_id=1, source_target_pairs={{0,32},{32,0},{64,96},{96,64},{128,160},{160,128},{192,224},{224,1... | collective-permute-start | bytes 393224 | tf_op jit(solution)/shard_map/ppermute | solution.py:71
  55.1 9.1 %copy-start.4 = (f32[2,128,128]{2,1,0:T(8,128)S(1)}, f32[2,128,128]{2,1,0:T(8,128)}, u32[]{:S(2)}) copy-start(f32[2,128,128]{2,1,0:T(8,128)} %refs_0_.1) | copy-start | bytes 393220
  55.1 9.1 %collective-permute-start.7 = (f32[2,128,128]{2,1,0:T(8,128)S(1)}, f32[2,128,128]{2,1,0:T(8,128)S(1)}, u32[]{:S(2)}, u32[]{:S(2)}) collective-permute-start(f32[2,128,128]{2,1,0:T(8,128)S(1)} %get-tuple-element.24), channel_id=1, source_target_pairs={{32,64},{64,32},{96,128},{128,96},{160,192},{192,160},{33,65},{65,... | collective-permute-start | bytes 393224 | tf_op jit(solution)/shard_map/ppermute | solution.py:71
  65.0 18.7 %all-to-all-start.1 = ((f32[8,16,256]{2,1,0:T(8,128)}), f32[8,16,256]{2,1,0:T(8,128)S(1)}, u32[]{:S(2)}, u32[]{:S(2)}) async-start(f32[8,16,256]{2,1,0:T(8,128)} %sum_repeat.4), calls=%async_computation.1 | async-start | bytes 262144 | tf_op jit(solution)/shard_map/all_to_all | solution.py:278
  72.2 6.9 %collective-permute-start.9 = (f32[2,128,128]{2,1,0:T(8,128)S(1)}, f32[2,128,128]{2,1,0:T(8,128)S(1)}, u32[]{:S(2)}, u32[]{:S(2)}) collective-permute-start(f32[2,128,128]{2,1,0:T(8,128)S(1)} %renew.2.refs_2_.refs_0_), channel_id=1, source_target_pairs={{32,64},{64,32},{96,128},{128,96},{160,192},{192,160},{33,65},{65,... | collective-permute-start | bytes 393224 | tf_op jit(solution)/shard_map/ppermute | solution.py:71
  75.7 7.4 %collective-permute-start.8 = (f32[2,128,128]{2,1,0:T(8,128)S(1)}, f32[2,128,128]{2,1,0:T(8,128)S(1)}, u32[]{:S(2)}, u32[]{:S(2)}) collective-permute-start(f32[2,128,128]{2,1,0:T(8,128)S(1)} %renew.2.refs_2_.refs_0_), channel_id=1, source_target_pairs={{0,32},{32,0},{64,96},{96,64},{128,160},{160,128},{192,224},{224,1... | collective-permute-start | bytes 393224 | tf_op jit(solution)/shard_map/ppermute | solution.py:71
  84.5 22.1 %copy-start.17 = (bf16[256,512]{1,0:T(8,128)(2,1)S(1)}, bf16[256,512]{1,0:T(8,128)(2,1)}, u32[]{:S(2)}) copy-start(bf16[256,512]{1,0:T(8,128)(2,1)} %constant.18.clone.refs_9_) | copy-start | bytes 786436
  84.5 12.0 %all-to-all-start.2 = ((f32[16,16,256]{2,1,0:T(8,128)}), f32[16,16,256]{2,1,0:T(8,128)S(1)}, u32[]{:S(2)}, u32[]{:S(2)}) async-start(f32[16,16,256]{2,1,0:T(8,128)} %sum_repeat.5), calls=%async_computation.2 | async-start | bytes 524288 | tf_op jit(solution)/shard_map/all_to_all | solution.py:279
  90.1 14.9 %collective-permute-start.13 = (f32[2,384,128]{2,1,0:T(8,128)S(1)}, f32[2,384,128]{2,1,0:T(8,128)S(1)}, u32[]{:S(2)}, u32[]{:S(2)}) collective-permute-start(f32[2,384,128]{2,1,0:T(8,128)S(1)} %stack.23.refs_0_.refs_5_), channel_id=1, source_target_pairs={{1,2},{2,1},{3,4},{4,3},{5,6},{6,5},{7,8},{8,7},{9,10},{10,9},{11,... | collective-permute-start | bytes 1179656 | tf_op jit(solution)/shard_map/ppermute | solution.py:71
  96.1 9.7 %collective-permute-start.12 = (f32[2,384,128]{2,1,0:T(8,128)S(1)}, f32[2,384,128]{2,1,0:T(8,128)S(1)}, u32[]{:S(2)}, u32[]{:S(2)}) collective-permute-start(f32[2,384,128]{2,1,0:T(8,128)S(1)} %stack.23.refs_0_.refs_5_), channel_id=1, source_target_pairs={{0,1},{1,0},{2,3},{3,2},{4,5},{5,4},{6,7},{7,6},{8,9},{9,8},{10,11... | collective-permute-start | bytes 1179656 | tf_op jit(solution)/shard_map/ppermute | solution.py:71
  96.5 10.1 %collective-permute-start.11 = (f32[256,256]{1,0:T(8,128)S(1)}, f32[256,256]{1,0:T(8,128)S(1)}, u32[]{:S(2)}, u32[]{:S(2)}) collective-permute-start(f32[256,256]{1,0:T(8,128)S(1)} %bitcast.16), channel_id=1, source_target_pairs={{0,1},{1,0},{2,3},{3,2},{4,5},{5,4},{6,7},{7,6},{8,9},{9,8},{10,11... | collective-permute-start | bytes 786440 | tf_op jit(solution)/shard_map/ppermute | solution.py:71
  105.1 0.8 copy-start.12
  105.8 0.7 copy-start.14
  106.6 1.0 copy-start.13
  107.6 1.0 copy-start.15
  115.9 2.4 %copy-start.5 = (f32[2,384,128]{2,1,0:T(8,128)}, f32[2,384,128]{2,1,0:T(8,128)S(1)}, u32[]{:S(2)}) copy-start(f32[2,384,128]{2,1,0:T(8,128)S(1)} %get-tuple-element.30.refs_0_) | copy-start | bytes 1179652
  115.9 2.4 %copy-start.10 = (f32[2,384,128]{2,1,0:T(8,128)}, f32[2,384,128]{2,1,0:T(8,128)S(1)}, u32[]{:S(2)}) copy-start(f32[2,384,128]{2,1,0:T(8,128)S(1)} %get-tuple-element.29) | copy-start | bytes 1179652
  115.9 1.6 collective-permute-start.15
  118.3 7.8 %copy-start.11 = (f32[2,384,128]{2,1,0:T(8,128)S(1)}, f32[2,384,128]{2,1,0:T(8,128)}, u32[]{:S(2)}) copy-start(f32[2,384,128]{2,1,0:T(8,128)} %copy-done.10) | copy-start | bytes 1179652
  118.3 14.2 %all-to-all-start.3 = ((f32[16,16,256]{2,1,0:T(8,128)}), f32[16,16,256]{2,1,0:T(8,128)S(1)}, u32[]{:S(2)}, u32[]{:S(2)}) async-start(f32[16,16,256]{2,1,0:T(8,128)} %bitcast.7), calls=%async_computation.3 | async-start | bytes 524288 | tf_op jit(solution)/shard_map/all_to_all | solution.py:272
  126.2 19.3 %collective-permute-start.14 = (f32[2,384,128]{2,1,0:T(8,128)S(1)}, f32[2,384,128]{2,1,0:T(8,128)S(1)}, u32[]{:S(2)}, u32[]{:S(2)}) collective-permute-start(f32[2,384,128]{2,1,0:T(8,128)S(1)} %copy-done.11), channel_id=1, source_target_pairs={{0,1},{1,0},{2,3},{3,2},{4,5},{5,4},{6,7},{7,6},{8,9},{9,8},{10,11... | collective-permute-start | bytes 1179656 | tf_op jit(solution)/shard_map/ppermute | solution.py:71
  132.5 0.7 copy-start.2
  133.2 13.5 %collective-permute-start.16 = (f32[2,384,128]{2,1,0:T(8,128)}, f32[2,384,128]{2,1,0:T(8,128)S(1)}, u32[]{:S(2)}, u32[]{:S(2)}) collective-permute-start(f32[2,384,128]{2,1,0:T(8,128)} %hold.2), channel_id=1, source_target_pairs={{1,2},{2,1},{3,4},{4,3},{5,6},{6,5},{7,8},{8,7},{9,10},{10,9},{11,... | collective-permute-start | bytes 1179656 | tf_op jit(solution)/shard_map/ppermute | solution.py:71
  137.4 1.0 copy-start.3
  139.1 15.9 %all-to-all-start.4 = ((f32[8,16,256]{2,1,0:T(8,128)}), f32[8,16,256]{2,1,0:T(8,128)S(1)}, u32[]{:S(2)}, u32[]{:S(2)}) async-start(f32[8,16,256]{2,1,0:T(8,128)} %sum_repeat.6), calls=%async_computation.4 | async-start | bytes 262144 | tf_op jit(solution)/shard_map/all_to_all | solution.py:278
  155.8 16.5 %all-to-all-start.5 = ((f32[16,16,256]{2,1,0:T(8,128)}), f32[16,16,256]{2,1,0:T(8,128)S(1)}, u32[]{:S(2)}, u32[]{:S(2)}) async-start(f32[16,16,256]{2,1,0:T(8,128)} %sum_repeat.7), calls=%async_computation.5 | async-start | bytes 524288 | tf_op jit(solution)/shard_map/all_to_all | solution.py:279
  161.3 10.2 %collective-permute-start.17 = (f32[2,128,128]{2,1,0:T(8,128)S(1)}, f32[2,128,128]{2,1,0:T(8,128)S(1)}, u32[]{:S(2)}, u32[]{:S(2)}) collective-permute-start(f32[2,128,128]{2,1,0:T(8,128)S(1)} %get-tuple-element.33), channel_id=1, source_target_pairs={{0,32},{32,0},{64,96},{96,64},{128,160},{160,128},{192,224},{224,1... | collective-permute-start | bytes 393224 | tf_op jit(solution)/shard_map/ppermute | solution.py:71
  162.5 9.1 %collective-permute-start.18 = (f32[2,128,128]{2,1,0:T(8,128)S(1)}, f32[2,128,128]{2,1,0:T(8,128)S(1)}, u32[]{:S(2)}, u32[]{:S(2)}) collective-permute-start(f32[2,128,128]{2,1,0:T(8,128)S(1)} %get-tuple-element.35), channel_id=1, source_target_pairs={{32,64},{64,32},{96,128},{128,96},{160,192},{192,160},{33,65},{65,... | collective-permute-start | bytes 393224 | tf_op jit(solution)/shard_map/ppermute | solution.py:71
  172.2 0.7 copy-start
  172.9 2.6 %collective-permute-start.19 = (f32[256,256]{1,0:T(8,128)}, f32[256,256]{1,0:T(8,128)S(1)}, u32[]{:S(2)}, u32[]{:S(2)}) collective-permute-start(f32[256,256]{1,0:T(8,128)} %hold.3.refs_2_), channel_id=1, source_target_pairs={{0,1},{1,0},{2,3},{3,2},{4,5},{5,4},{6,7},{7,6},{8,9},{9,8},{10,11... | collective-permute-start | bytes 786440 | tf_op jit(solution)/shard_map/ppermute | solution.py:71
  175.5 0.9 copy-start.1

commit v3 on v2

--- a/solution.py
+++ b/solution.py
@@ -267,22 +267,12 @@
     return (a + b).reshape(ways, -1, a.shape[-1])
 
 
-def scatter(keep, give):
+def spread_over(keep, give):
     plane = math.prod(lax.axis_size(a) for a in PLANE)
-    return lax.all_to_all(add_into_ways(keep, pair_swap(give, "core", 0), plane), PLANE, 0, 0)
-
-
-def gather(part, first, second, third=None):
-    plane = part.shape[0]
-    part = sum_and_repeat(part, lax.axis_size("z"), first)
-    part = sum_and_repeat(lax.all_to_all(part, "z", 0, 0), plane, second)
-    own = lax.all_to_all(part, PLANE, 0, 0).reshape(-1, part.shape[-1])
-    if third is not None:
-        own = hold(own, third)
-    return own, pair_swap(own, "core", 0)
-
-
-def widen(ids, tile):
+    return add_into_ways(keep, pair_swap(give, "core", 0), plane)
+
+
+def widen(ids, tile, after=()):
     channels, rows, cols = tile.shape
     side = cols
     tags = rows - side
@@ -297,7 +287,7 @@
 
     far = pair_swap(tile, ROW, 1)
     near = pair_swap(tile, ROW, 0)
-    tall = call(kernel, shape(channels, 3 * rows, cols), (ids, near, tile, far), "stack")
+    tall = call(kernel, shape(channels, 3 * rows, cols), (ids, near, tile, far), "stack", after=after)
     return pair_swap(tall, COL, 0), tall, pair_swap(tall, COL, 1)
 
 
@@ -338,11 +328,11 @@
     )
 
 
-def fold(ids, tile, bright, sib, mid, cross):
+def split(ids, sib, mid, cross):
     channels, tall, cols = mid.shape
     rows = tall // 3
 
-    def split(ids, mid, sib, cross, near, own, far):
+    def kernel(ids, mid, sib, cross, near, own, far):
         flip = ids[1]
 
         def part(start):
@@ -353,16 +343,19 @@
         own[...] = part(rows)
         far[...] = part(pl.multiple_of(2 * rows * flip, rows))
 
-    def renew(tile, bright, near, own, far, out):
+    cross = pair_swap(cross, COL, 1)
+    sib = pair_swap(sib, COL, 0)
+    near, own, far = call(kernel, [shape(channels, rows, cols)] * 3, (ids, mid, sib, cross), "split")
+    return pair_swap(near, ROW, 0), own, pair_swap(far, ROW, 1)
+
+
+def renew(tile, bright, near, own, far, after):
+    def kernel(tile, bright, near, own, far, out):
         part = near[...] + own[...] + far[...]
         out[...] = tile[...] + part / (bright[...] + 1.0)
 
-    cross = pair_swap(cross, COL, 1)
-    sib = pair_swap(sib, COL, 0)
-    near, own, far = call(split, [shape(channels, rows, cols)] * 3, (ids, mid, sib, cross), "split")
-    far = pair_swap(far, ROW, 1)
-    near = pair_swap(near, ROW, 0)
-    return own, call(renew, shape(*tile.shape), (tile, bright, near, own, far), "renew", scalars=0)
+    operands = (tile, bright, near, own, far)
+    return call(kernel, shape(*tile.shape), operands, "renew", scalars=0, after=after)
 
 
 def on_device(patterns, background, offsets, probe, tile):
@@ -387,16 +380,24 @@
         if step > 0:
             probe = new_probe
         bright = light(ids, spots, probe)
-        part = scatter(keep, give)
         last = step == ITERS - 1
+        part = spread_over(keep, give)
+        ways, deep = part.shape[0], lax.axis_size("z")
         if last:
             cross = hold(cross, part)
-        centre, tile = fold(ids, tile, bright, sib, mid, cross)
+        near, centre, far = split(ids, sib, mid, cross)
+        part = lax.all_to_all(part, PLANE, 0, 0)
+        part = sum_and_repeat(part, deep, () if last else (centre,))
+        if not last:
+            tile = renew(tile, bright, near, centre, far, (part,))
+        part = lax.all_to_all(part, "z", 0, 0)
+        part = sum_and_repeat(part, ways, (centre,) if last else (tile,))
         if last:
-            own, other = gather(part, (), (centre,), tile)
+            tile = renew(tile, bright, near, centre, far, ())
         else:
-            parts = widen(ids, tile)
-            own, other = gather(part, (tile,), (parts[1],))
+            parts = widen(ids, tile, (part,))
+        own = lax.all_to_all(part, PLANE, 0, 0).reshape(side, side)
+        other = pair_swap(hold(own, tile) if last else own, "core", 0)
     return tile, finish(ids, probe, own, other)
 
 

time: 179 us -> 168 us (0.939)
  waiting for transfers between devices: 55.7 us -> 45.9 us
  local copies, waits for them, and re-layouts: 8.36 us -> 6.42 us
    all_to_all x6, waiting for transfers between devices: 13.3 us -> 6.04 us  [the longest x2 5.17 us: on_device(): part = lax.all_to_all(part, 'z', 0, 0)]
    ppermute x20, starting transfers between devices: 42.1 us -> 45.7 us  [pair_swap(): return lax.ppermute(value, axis, pairs)]
    ppermute x20, waiting for transfers between devices: 42.4 us -> 39.9 us  [pair_swap(): return lax.ppermute(value, axis, pairs)]
    all_to_all x6, starting transfers between devices: 38.8 us -> 36.5 us  [the longest x2 14.2 us: on_device(): part = lax.all_to_all(part, PLANE, 0, 0)]
    unnamed x38 -> x37, local copies, waits for them, and re-layouts: 7.5 us -> 5.56 us
  transfers between devices with their start and end apart: 26 -> 26, of which waited for: 15 -> 14; matrix products, arithmetic and copies ran while one was open for 2% -> 2% of each run, Pallas kernels for 4% -> 5%
where the time goes in v3:
time: 168 us; the launch traced here: 167 us
  starting transfers between devices  82.2 us (49%)
  waiting for transfers between devices  45.9 us (27%)
  Pallas kernels  27.1 us (16%)
  local copies, waits for them, and re-layouts  6.42 us (4%)
  other arithmetic  4.13 us (2%)
    ppermute x20, starting transfers between devices, pair_swap(): return lax.ppermute(value, axis, pairs)  45.7 us
    ppermute x20, waiting for transfers between devices, pair_swap(): return lax.ppermute(value, axis, pairs)  39.9 us
    pallas_call x2, Pallas kernels, update(): pl.pallas_call(lambda *refs: update_kernel(renew, *refs), out_shape=(stri...  15.5 us
    all_to_all x2, starting transfers between devices, on_device(): part = lax.all_to_all(part, PLANE, 0, 0)  14.2 us
    all_to_all x2, starting transfers between devices, on_device(): part = lax.all_to_all(part, 'z', 0, 0)  13.7 us
    pallas_call x13, Pallas kernels, call(): pl.pallas_call(body, out_shape=out_shape, in_specs=[ANY] * waits + [SMEM]...  11.6 us
    all_to_all x2, starting transfers between devices, on_device(): own = lax.all_to_all(part, PLANE, 0, 0).reshape(side, side)  8.5 us
    unnamed x37, local copies, waits for them, and re-layouts  5.56 us
  transfers between devices with their start and end apart: 26, of which 14 were waited for; matrix products, arithmetic and copies ran while one was open for 2% of the time, Pallas kernels for 5%

profile of v3, /device:TPU:3, one launch (start us, length us, event | category | flops | bytes accessed | tf_op | source)
XLA Modules:
  0.0 166.8 jit_solution(8986446456759157324)
XLA Ops:
  0.7 0.7 copy-done.17
  1.5 0.9 pad_maximum_fusion.refs_2_
  2.4 3.2 %collective-permute-start.1 = (f32[2,136,128]{2,1,0:T(8,128)S(1)}, f32[2,136,128]{2,1,0:T(8,128)S(1)}, u32[]{:S(2)}, u32[]{:S(2)}) collective-permute-start(f32[2,136,128]{2,1,0:T(8,128)S(1)} %pad_maximum_fusion.refs_2_), channel_id=1, source_target_pairs={{32,64},{64,32},{96,128},{128,96},{160,192},{192,160},{33,65},{65,... | collective-permute-start | bytes 417800 | tf_op jit(solution)/shard_map/ppermute | solution.py:71
  5.6 1.2 collective-permute-start
  6.9 2.9 %collective-permute-done.1.refs_3_ = f32[2,136,128]{2,1,0:T(8,128)S(1)} collective-permute-done((f32[2,136,128]{2,1,0:T(8,128)S(1)}, f32[2,136,128]{2,1,0:T(8,128)S(1)}, u32[]{:S(2)}, u32[]{:S(2)}) %collective-permute-start.1) | collective-permute-done | bytes 139296 | tf_op jit(solution)/shard_map/ppermute | solution.py:71
  9.7 4.0 %collective-permute-done.refs_1_ = f32[2,136,128]{2,1,0:T(8,128)S(1)} collective-permute-done((f32[2,136,128]{2,1,0:T(8,128)S(1)}, f32[2,136,128]{2,1,0:T(8,128)S(1)}, u32[]{:S(2)}, u32[]{:S(2)}) %collective-permute-start) | collective-permute-done | bytes 139296 | tf_op jit(solution)/shard_map/ppermute | solution.py:71
  13.8 0.6 stack.22.refs_5_
  14.4 5.3 %collective-permute-start.3 = (f32[2,408,128]{2,1,0:T(8,128)S(1)}, f32[2,408,128]{2,1,0:T(8,128)S(1)}, u32[]{:S(2)}, u32[]{:S(2)}) collective-permute-start(f32[2,408,128]{2,1,0:T(8,128)S(1)} %stack.22.refs_5_), channel_id=1, source_target_pairs={{1,2},{2,1},{3,4},{4,3},{5,6},{6,5},{7,8},{8,7},{9,10},{10,9},{11,... | collective-permute-start | bytes 1253384 | tf_op jit(solution)/shard_map/ppermute | solution.py:71
  19.7 0.1 collective-permute-start.2
  19.8 1.6 fusion.1.refs_7_
  21.4 7.8 %collective-permute-done.3.refs_6_ = f32[2,408,128]{2,1,0:T(8,128)S(1)} collective-permute-done((f32[2,408,128]{2,1,0:T(8,128)S(1)}, f32[2,408,128]{2,1,0:T(8,128)S(1)}, u32[]{:S(2)}, u32[]{:S(2)}) %collective-permute-start.3) | collective-permute-done | bytes 417824 | tf_op jit(solution)/shard_map/ppermute | solution.py:71
  29.2 8.2 %update.2 = (f32[2,384,128]{2,1,0:T(8,128)S(1)}, f32[256,256]{1,0:T(8,128)S(1)}, f32[256,256]{1,0:T(8,128)S(1)}, f32[2,256,256]{2,1,0:T(8,128)}, f32[2,384,128]{2,1,0:T(8,128)}, /*index=5*/f32[2,384,128]{2,1,0:T(8,128)}) custom-call(s32[2]{0:T(128)S(1)} %pad_add_fusion.refs_0_.refs_1_, s32[4,2]{1,0:T(4,128)S(1)} %bitcast.19, f32[256,256]{1,0:T(8,128)S(1)} %copy-done.2, ...), custom_call_target="tpu_custom_call" | custom-call | flops 4294967296 | tf_op jit(solution)/shard_map/update/pallas_call | solution.py:209
  37.4 0.1 collective-permute-start.6
  37.5 0.5 collective-permute-start.4
  38.0 5.9 %collective-permute-start.5 = (f32[2,384,128]{2,1,0:T(8,128)}, f32[2,384,128]{2,1,0:T(8,128)S(1)}, u32[]{:S(2)}, u32[]{:S(2)}) collective-permute-start(f32[2,384,128]{2,1,0:T(8,128)} %get-tuple-element.21), channel_id=1, source_target_pairs={{1,2},{2,1},{3,4},{4,3},{5,6},{6,5},{7,8},{8,7},{9,10},{10,9},{11,... | collective-permute-start | bytes 1179656 | tf_op jit(solution)/shard_map/ppermute | solution.py:71
  43.9 0.7 add.28
  44.6 5.8 %all-to-all-start = ((f32[16,16,256]{2,1,0:T(8,128)}), f32[16,16,256]{2,1,0:T(8,128)S(1)}, u32[]{:S(2)}, u32[]{:S(2)}) async-start(f32[16,16,256]{2,1,0:T(8,128)} %bitcast.21), calls=%async_computation | async-start | bytes 524288 | tf_op jit(solution)/shard_map/all_to_all | solution.py:389
  50.4 0.7 slice.9
  51.1 4.6 %collective-permute-done.5.refs_3_ = f32[2,384,128]{2,1,0:T(8,128)S(1)} collective-permute-done((f32[2,384,128]{2,1,0:T(8,128)}, f32[2,384,128]{2,1,0:T(8,128)S(1)}, u32[]{:S(2)}, u32[]{:S(2)}) %collective-permute-start.5) | collective-permute-done | bytes 393248 | tf_op jit(solution)/shard_map/ppermute | solution.py:71
  55.8 0.6 split.2
  56.4 0.6 copy-done.13
  57.1 0.7 sum_repeat.4.refs_0_
  57.8 8.3 %all-to-all-start.1 = ((f32[8,16,256]{2,1,0:T(8,128)}), f32[8,16,256]{2,1,0:T(8,128)S(1)}, u32[]{:S(2)}, u32[]{:S(2)}) async-start(f32[8,16,256]{2,1,0:T(8,128)} %sum_repeat.4.refs_0_), calls=%async_computation.1 | async-start | bytes 262144 | tf_op jit(solution)/shard_map/all_to_all | solution.py:393
  66.1 1.8 %collective-permute-start.7 = (f32[2,128,128]{2,1,0:T(8,128)S(1)}, f32[2,128,128]{2,1,0:T(8,128)S(1)}, u32[]{:S(2)}, u32[]{:S(2)}) collective-permute-start(f32[2,128,128]{2,1,0:T(8,128)S(1)} %copy-done.14), channel_id=1, source_target_pairs={{0,32},{32,0},{64,96},{96,64},{128,160},{160,128},{192,224},{224,1... | collective-permute-start | bytes 393224 | tf_op jit(solution)/shard_map/ppermute | solution.py:71
  67.9 2.3 %collective-permute-start.8 = (f32[2,128,128]{2,1,0:T(8,128)S(1)}, f32[2,128,128]{2,1,0:T(8,128)S(1)}, u32[]{:S(2)}, u32[]{:S(2)}) collective-permute-start(f32[2,128,128]{2,1,0:T(8,128)S(1)} %get-tuple-element.26), channel_id=1, source_target_pairs={{32,64},{64,32},{96,128},{128,96},{160,192},{192,160},{33,65},{65,... | collective-permute-start | bytes 393224 | tf_op jit(solution)/shard_map/ppermute | solution.py:71
  70.2 2.0 %light.2.refs_2_ = f32[128,128]{1,0:T(8,128)S(1)} custom-call(s32[2]{0:T(128)S(1)} %pad_add_fusion.refs_0_.refs_1_, s32[3,3,8]{2,1,0:T(4,128)S(1)} %maximum_convert_fusion.refs_1_, f32[2,256,256]{2,1,0:T(8,128)S(1)} %copy-done.5), custom_call_target="tpu_custom_call" | custom-call | flops 2000000000 | bytes 524584 | tf_op jit(solution)/shard_map/light/pallas_call | solution.py:48
  72.2 3.5 %collective-permute-done.8.refs_5_ = f32[2,128,128]{2,1,0:T(8,128)S(1)} collective-permute-done((f32[2,128,128]{2,1,0:T(8,128)S(1)}, f32[2,128,128]{2,1,0:T(8,128)S(1)}, u32[]{:S(2)}, u32[]{:S(2)}) %collective-permute-start.8) | collective-permute-done | bytes 131104 | tf_op jit(solution)/shard_map/ppermute | solution.py:71
  75.8 1.9 %collective-permute-start.11 = (f32[2,128,128]{2,1,0:T(8,128)S(1)}, f32[2,128,128]{2,1,0:T(8,128)S(1)}, u32[]{:S(2)}, u32[]{:S(2)}) collective-permute-start(f32[2,128,128]{2,1,0:T(8,128)S(1)} %renew.2.refs_0_.refs_3_), channel_id=1, source_target_pairs={{32,64},{64,32},{96,128},{128,96},{160,192},{192,160},{33,65},{65,... | collective-permute-start | bytes 393224 | tf_op jit(solution)/shard_map/ppermute | solution.py:71
  77.7 2.8 %collective-permute-start.10 = (f32[2,128,128]{2,1,0:T(8,128)S(1)}, f32[2,128,128]{2,1,0:T(8,128)S(1)}, u32[]{:S(2)}, u32[]{:S(2)}) collective-permute-start(f32[2,128,128]{2,1,0:T(8,128)S(1)} %renew.2.refs_0_.refs_3_), channel_id=1, source_target_pairs={{0,32},{32,0},{64,96},{96,64},{128,160},{160,128},{192,224},{224,1... | collective-permute-start | bytes 393224 | tf_op jit(solution)/shard_map/ppermute | solution.py:71
  80.5 0.7 sum_repeat.5.refs_0_
  81.2 3.4 %all-to-all-start.2 = ((f32[16,16,256]{2,1,0:T(8,128)}), f32[16,16,256]{2,1,0:T(8,128)S(1)}, u32[]{:S(2)}, u32[]{:S(2)}) async-start(f32[16,16,256]{2,1,0:T(8,128)} %sum_repeat.5.refs_0_), calls=%async_computation.2 | async-start | bytes 524288 | tf_op jit(solution)/shard_map/all_to_all | solution.py:399
  84.7 2.1 %collective-permute-done.10.refs_2_ = f32[2,128,128]{2,1,0:T(8,128)S(1)} collective-permute-done((f32[2,128,128]{2,1,0:T(8,128)S(1)}, f32[2,128,128]{2,1,0:T(8,128)S(1)}, u32[]{:S(2)}, u32[]{:S(2)}) %collective-permute-start.10) | collective-permute-done | bytes 131104 | tf_op jit(solution)/shard_map/ppermute | solution.py:71
  86.7 0.6 stack.23.refs_5_
  87.3 6.1 %collective-permute-start.13 = (f32[2,384,128]{2,1,0:T(8,128)S(1)}, f32[2,384,128]{2,1,0:T(8,128)S(1)}, u32[]{:S(2)}, u32[]{:S(2)}) collective-permute-start(f32[2,384,128]{2,1,0:T(8,128)S(1)} %stack.23.refs_5_), channel_id=1, source_target_pairs={{1,2},{2,1},{3,4},{4,3},{5,6},{6,5},{7,8},{8,7},{9,10},{10,9},{11,... | collective-permute-start | bytes 1179656 | tf_op jit(solution)/shard_map/ppermute | solution.py:71
  93.4 0.1 collective-permute-start.12
  93.6 1.9 %collective-permute-start.9 = (f32[256,256]{1,0:T(8,128)S(1)}, f32[256,256]{1,0:T(8,128)S(1)}, u32[]{:S(2)}, u32[]{:S(2)}) collective-permute-start(f32[256,256]{1,0:T(8,128)S(1)} %bitcast.17), channel_id=1, source_target_pairs={{0,1},{1,0},{2,3},{3,2},{4,5},{5,4},{6,7},{7,6},{8,9},{9,8},{10,11... | collective-permute-start | bytes 786440 | tf_op jit(solution)/shard_map/ppermute | solution.py:71
  95.4 6.0 %collective-permute-done.13.refs_6_ = f32[2,384,128]{2,1,0:T(8,128)S(1)} collective-permute-done((f32[2,384,128]{2,1,0:T(8,128)S(1)}, f32[2,384,128]{2,1,0:T(8,128)S(1)}, u32[]{:S(2)}, u32[]{:S(2)}) %collective-permute-start.13) | collective-permute-done | bytes 393248 | tf_op jit(solution)/shard_map/ppermute | solution.py:71
  101.4 0.8 copy-done.9
  102.2 0.7 copy-done.11
  103.0 1.0 copy-done.10
  104.0 1.0 copy-done.12
  105.0 7.4 %update.3 = (f32[2,384,128]{2,1,0:T(8,128)S(1)}, f32[256,256]{1,0:T(8,128)S(1)}, f32[256,256]{1,0:T(8,128)S(1)}, f32[2,256,256]{2,1,0:T(8,128)S(1)}, f32[2,384,1...) custom-call(s32[2]{0:T(128)S(1)} %pad_add_fusion.refs_0_.refs_1_, s32[4,2]{1,0:T(4,128)S(1)} %bitcast.20, ...), custom_call_target="tpu_custom_call" | custom-call | flops 4294967296 | tf_op jit(solution)/shard_map/update/pallas_call | solution.py:209
  112.5 1.5 collective-permute-done.15
  114.0 0.8 add.29
  114.7 8.5 %all-to-all-start.3 = ((f32[16,16,256]{2,1,0:T(8,128)}), f32[16,16,256]{2,1,0:T(8,128)S(1)}, u32[]{:S(2)}, u32[]{:S(2)}) async-start(f32[16,16,256]{2,1,0:T(8,128)} %bitcast.7.refs_1_), calls=%async_computation.3 | async-start | bytes 524288 | tf_op jit(solution)/shard_map/all_to_all | solution.py:389
  123.2 1.0 collective-permute-start.14
  124.2 4.5 %collective-permute-start.16 = (f32[2,384,128]{2,1,0:T(8,128)}, f32[2,384,128]{2,1,0:T(8,128)S(1)}, u32[]{:S(2)}, u32[]{:S(2)}) collective-permute-start(f32[2,384,128]{2,1,0:T(8,128)} %hold.2), channel_id=1, source_target_pairs={{1,2},{2,1},{3,4},{4,3},{5,6},{6,5},{7,8},{8,7},{9,10},{10,9},{11,... | collective-permute-start | bytes 1179656 | tf_op jit(solution)/shard_map/ppermute | solution.py:71
  128.7 0.8 all-to-all-done.3.refs_0_
  129.5 0.7 sum_repeat.6
  130.2 5.5 %all-to-all-start.4 = ((f32[8,16,256]{2,1,0:T(8,128)}), f32[8,16,256]{2,1,0:T(8,128)S(1)}, u32[]{:S(2)}, u32[]{:S(2)}) async-start(f32[8,16,256]{2,1,0:T(8,128)} %sum_repeat.6), calls=%async_computation.4 | async-start | bytes 262144 | tf_op jit(solution)/shard_map/all_to_all | solution.py:393
  135.7 2.3 %collective-permute-done.16.refs_3_ = f32[2,384,128]{2,1,0:T(8,128)S(1)} collective-permute-done((f32[2,384,128]{2,1,0:T(8,128)}, f32[2,384,128]{2,1,0:T(8,128)S(1)}, u32[]{:S(2)}, u32[]{:S(2)}) %collective-permute-start.16) | collective-permute-done | bytes 393248 | tf_op jit(solution)/shard_map/ppermute | solution.py:71
  138.0 0.6 split.3
  138.6 5.2 %all-to-all-done.4.refs_1_ = f32[8,16,256]{2,1,0:T(8,128)S(1)} async-done(((f32[8,16,256]{2,1,0:T(8,128)}), f32[8,16,256]{2,1,0:T(8,128)S(1)}, u32[]{:S(2)}, u32[]{:S(2)}) %all-to-all-start.4) | async-done | bytes 131104 | tf_op jit(solution)/shard_map/all_to_all | solution.py:393
  143.7 0.7 sum_repeat.7
  144.5 5.1 %all-to-all-start.5 = ((f32[16,16,256]{2,1,0:T(8,128)}), f32[16,16,256]{2,1,0:T(8,128)S(1)}, u32[]{:S(2)}, u32[]{:S(2)}) async-start(f32[16,16,256]{2,1,0:T(8,128)} %sum_repeat.7), calls=%async_computation.5 | async-start | bytes 524288 | tf_op jit(solution)/shard_map/all_to_all | solution.py:399
  149.5 1.2 collective-permute-start.17
  150.7 2.2 %collective-permute-start.18 = (f32[2,128,128]{2,1,0:T(8,128)S(1)}, f32[2,128,128]{2,1,0:T(8,128)S(1)}, u32[]{:S(2)}, u32[]{:S(2)}) collective-permute-start(f32[2,128,128]{2,1,0:T(8,128)S(1)} %get-tuple-element.35), channel_id=1, source_target_pairs={{32,64},{64,32},{96,128},{128,96},{160,192},{192,160},{33,65},{65,... | collective-permute-start | bytes 393224 | tf_op jit(solution)/shard_map/ppermute | solution.py:71
  152.9 2.0 %light.3.refs_1_ = f32[128,128]{1,0:T(8,128)S(1)} custom-call(s32[2]{0:T(128)S(1)} %pad_add_fusion.refs_0_.refs_1_, s32[3,3,8]{2,1,0:T(4,128)S(1)} %maximum_convert_fusion.refs_1_, f32[2,256,256]{2,1,0:T(8,128)S(1)} %get-tuple-element.27.refs_2_.refs_1_), custom_call_target="tpu_custom_call" | custom-call | flops 2000000000 | bytes 524584 | tf_op jit(solution)/shard_map/light/pallas_call | solution.py:48
  155.0 3.9 %collective-permute-done.18.refs_4_ = f32[2,128,128]{2,1,0:T(8,128)S(1)} collective-permute-done((f32[2,128,128]{2,1,0:T(8,128)S(1)}, f32[2,128,128]{2,1,0:T(8,128)S(1)}, u32[]{:S(2)}, u32[]{:S(2)}) %collective-permute-start.18) | collective-permute-done | bytes 131104 | tf_op jit(solution)/shard_map/ppermute | solution.py:71
  158.8 0.7 renew.3.refs_1_
  159.5 0.7 copy.15.refs_0_
  160.2 3.5 %collective-permute-start.19 = (f32[256,256]{1,0:T(8,128)}, f32[256,256]{1,0:T(8,128)S(1)}, u32[]{:S(2)}, u32[]{:S(2)}) collective-permute-start(f32[256,256]{1,0:T(8,128)} %hold.3), channel_id=1, source_target_pairs={{0,1},{1,0},{2,3},{3,2},{4,5},{5,4},{6,7},{7,6},{8,9},{9,8},{10,11... | collective-permute-start | bytes 786440 | tf_op jit(solution)/shard_map/ppermute | solution.py:71
  163.8 1.4 collective-permute-done.19.refs_3_
  165.2 1.6 finish.1
  (57 shorter events, 0.6 us)
Async XLA Ops:
  0.6 0.7 copy-start.17
  2.4 7.3 %collective-permute-start.1 = (f32[2,136,128]{2,1,0:T(8,128)S(1)}, f32[2,136,128]{2,1,0:T(8,128)S(1)}, u32[]{:S(2)}, u32[]{:S(2)}) collective-permute-start(f32[2,136,128]{2,1,0:T(8,128)S(1)} %pad_maximum_fusion.refs_2_), channel_id=1, source_target_pairs={{32,64},{64,32},{96,128},{128,96},{160,192},{192,160},{33,65},{65,... | collective-permute-start | bytes 417800 | tf_op jit(solution)/shard_map/ppermute | solution.py:71
  5.6 8.2 %collective-permute-start = (f32[2,136,128]{2,1,0:T(8,128)S(1)}, f32[2,136,128]{2,1,0:T(8,128)S(1)}, u32[]{:S(2)}, u32[]{:S(2)}) collective-permute-start(f32[2,136,128]{2,1,0:T(8,128)S(1)} %pad_maximum_fusion.refs_2_), channel_id=1, source_target_pairs={{0,32},{32,0},{64,96},{96,64},{128,160},{160,128},{192,224},{224,1... | collective-permute-start | bytes 417800 | tf_op jit(solution)/shard_map/ppermute | solution.py:71
  6.9 12.9 %copy-start.2 = (f32[256,256]{1,0:T(8,128)S(1)}, f32[256,256]{1,0:T(8,128)}, u32[]{:S(2)}) copy-start(f32[256,256]{1,0:T(8,128)} %refs_3_.1) | copy-start | bytes 786436
  14.4 14.8 %copy-start.4 = (f32[2,256,256]{2,1,0:T(8,128)S(1)}, f32[2,256,256]{2,1,0:T(8,128)}, u32[]{:S(2)}) copy-start(f32[2,256,256]{2,1,0:T(8,128)} %refs_8_.3) | copy-start | bytes 1572868
  14.4 14.8 %copy-start.15 = (bf16[256,512]{1,0:T(8,128)(2,1)S(1)}, bf16[256,512]{1,0:T(8,128)(2,1)}, u32[]{:S(2)}) copy-start(bf16[256,512]{1,0:T(8,128)(2,1)} %constant.18.clone.refs_9_) | copy-start | bytes 786436
  14.4 14.8 %collective-permute-start.3 = (f32[2,408,128]{2,1,0:T(8,128)S(1)}, f32[2,408,128]{2,1,0:T(8,128)S(1)}, u32[]{:S(2)}, u32[]{:S(2)}) collective-permute-start(f32[2,408,128]{2,1,0:T(8,128)S(1)} %stack.22.refs_5_), channel_id=1, source_target_pairs={{1,2},{2,1},{3,4},{4,3},{5,6},{6,5},{7,8},{8,7},{9,10},{10,9},{11,... | collective-permute-start | bytes 1253384 | tf_op jit(solution)/shard_map/ppermute | solution.py:71
  19.7 9.4 %collective-permute-start.2 = (f32[2,408,128]{2,1,0:T(8,128)S(1)}, f32[2,408,128]{2,1,0:T(8,128)S(1)}, u32[]{:S(2)}, u32[]{:S(2)}) collective-permute-start(f32[2,408,128]{2,1,0:T(8,128)S(1)} %stack.22.refs_5_), channel_id=1, source_target_pairs={{0,1},{1,0},{2,3},{3,2},{4,5},{5,4},{6,7},{7,6},{8,9},{9,8},{10,11... | collective-permute-start | bytes 1253384 | tf_op jit(solution)/shard_map/ppermute | solution.py:71
  29.2 8.2 %copy-start.3 = (f32[2,408,128]{2,1,0:T(8,128)}, f32[2,408,128]{2,1,0:T(8,128)S(1)}, u32[]{:S(2)}) copy-start(f32[2,408,128]{2,1,0:T(8,128)S(1)} %collective-permute-done.2.refs_4_) | copy-start | bytes 1253380
  37.4 6.5 %collective-permute-start.6 = (f32[256,256]{1,0:T(8,128)S(1)}, f32[256,256]{1,0:T(8,128)S(1)}, u32[]{:S(2)}, u32[]{:S(2)}) collective-permute-start(f32[256,256]{1,0:T(8,128)S(1)} %get-tuple-element.24), channel_id=1, source_target_pairs={{0,1},{1,0},{2,3},{3,2},{4,5},{5,4},{6,7},{7,6},{8,9},{9,8},{10,11... | collective-permute-start | bytes 786440 | tf_op jit(solution)/shard_map/ppermute | solution.py:71
  37.5 13.7 %collective-permute-start.4 = (f32[2,384,128]{2,1,0:T(8,128)}, f32[2,384,128]{2,1,0:T(8,128)S(1)}, u32[]{:S(2)}, u32[]{:S(2)}) collective-permute-start(f32[2,384,128]{2,1,0:T(8,128)} %get-tuple-element.20), channel_id=1, source_target_pairs={{0,1},{1,0},{2,3},{3,2},{4,5},{5,4},{6,7},{7,6},{8,9},{9,8},{10,11... | collective-permute-start | bytes 1179656 | tf_op jit(solution)/shard_map/ppermute | solution.py:71
  38.0 17.8 %collective-permute-start.5 = (f32[2,384,128]{2,1,0:T(8,128)}, f32[2,384,128]{2,1,0:T(8,128)S(1)}, u32[]{:S(2)}, u32[]{:S(2)}) collective-permute-start(f32[2,384,128]{2,1,0:T(8,128)} %get-tuple-element.21), channel_id=1, source_target_pairs={{1,2},{2,1},{3,4},{4,3},{5,6},{6,5},{7,8},{8,7},{9,10},{10,9},{11,... | collective-permute-start | bytes 1179656 | tf_op jit(solution)/shard_map/ppermute | solution.py:71
  44.6 12.5 %all-to-all-start = ((f32[16,16,256]{2,1,0:T(8,128)}), f32[16,16,256]{2,1,0:T(8,128)S(1)}, u32[]{:S(2)}, u32[]{:S(2)}) async-start(f32[16,16,256]{2,1,0:T(8,128)} %bitcast.21), calls=%async_computation | async-start | bytes 524288 | tf_op jit(solution)/shard_map/all_to_all | solution.py:389
  56.4 0.7 copy-start.13
  57.0 13.1 %copy-start.5 = (f32[2,256,256]{2,1,0:T(8,128)S(1)}, f32[2,256,256]{2,1,0:T(8,128)}, u32[]{:S(2)}) copy-start(f32[2,256,256]{2,1,0:T(8,128)} %refs_8_.3) | copy-start | bytes 1572868
  57.8 8.3 %copy-start.14 = (f32[2,128,128]{2,1,0:T(8,128)S(1)}, f32[2,128,128]{2,1,0:T(8,128)}, u32[]{:S(2)}) copy-start(f32[2,128,128]{2,1,0:T(8,128)} %copy-done.13) | copy-start | bytes 393220
  57.8 22.7 %all-to-all-start.1 = ((f32[8,16,256]{2,1,0:T(8,128)}), f32[8,16,256]{2,1,0:T(8,128)S(1)}, u32[]{:S(2)}, u32[]{:S(2)}) async-start(f32[8,16,256]{2,1,0:T(8,128)} %sum_repeat.4.refs_0_), calls=%async_computation.1 | async-start | bytes 262144 | tf_op jit(solution)/shard_map/all_to_all | solution.py:393
  66.1 6.2 %collective-permute-start.7 = (f32[2,128,128]{2,1,0:T(8,128)S(1)}, f32[2,128,128]{2,1,0:T(8,128)S(1)}, u32[]{:S(2)}, u32[]{:S(2)}) collective-permute-start(f32[2,128,128]{2,1,0:T(8,128)S(1)} %copy-done.14), channel_id=1, source_target_pairs={{0,32},{32,0},{64,96},{96,64},{128,160},{160,128},{192,224},{224,1... | collective-permute-start | bytes 393224 | tf_op jit(solution)/shard_map/ppermute | solution.py:71
  67.9 7.8 %copy-start = (f32[2,128,128]{2,1,0:T(8,128)S(1)}, f32[2,128,128]{2,1,0:T(8,128)}, u32[]{:S(2)}) copy-start(f32[2,128,128]{2,1,0:T(8,128)} %refs_1_.1) | copy-start | bytes 393220
  67.9 7.8 %collective-permute-start.8 = (f32[2,128,128]{2,1,0:T(8,128)S(1)}, f32[2,128,128]{2,1,0:T(8,128)S(1)}, u32[]{:S(2)}, u32[]{:S(2)}) collective-permute-start(f32[2,128,128]{2,1,0:T(8,128)S(1)} %get-tuple-element.26), channel_id=1, source_target_pairs={{32,64},{64,32},{96,128},{128,96},{160,192},{192,160},{33,65},{65,... | collective-permute-start | bytes 393224 | tf_op jit(solution)/shard_map/ppermute | solution.py:71
  75.8 8.9 %collective-permute-start.11 = (f32[2,128,128]{2,1,0:T(8,128)S(1)}, f32[2,128,128]{2,1,0:T(8,128)S(1)}, u32[]{:S(2)}, u32[]{:S(2)}) collective-permute-start(f32[2,128,128]{2,1,0:T(8,128)S(1)} %renew.2.refs_0_.refs_3_), channel_id=1, source_target_pairs={{32,64},{64,32},{96,128},{128,96},{160,192},{192,160},{33,65},{65,... | collective-permute-start | bytes 393224 | tf_op jit(solution)/shard_map/ppermute | solution.py:71
  77.7 9.1 %collective-permute-start.10 = (f32[2,128,128]{2,1,0:T(8,128)S(1)}, f32[2,128,128]{2,1,0:T(8,128)S(1)}, u32[]{:S(2)}, u32[]{:S(2)}) collective-permute-start(f32[2,128,128]{2,1,0:T(8,128)S(1)} %renew.2.refs_0_.refs_3_), channel_id=1, source_target_pairs={{0,32},{32,0},{64,96},{96,64},{128,160},{160,128},{192,224},{224,1... | collective-permute-start | bytes 393224 | tf_op jit(solution)/shard_map/ppermute | solution.py:71
  81.2 12.3 %all-to-all-start.2 = ((f32[16,16,256]{2,1,0:T(8,128)}), f32[16,16,256]{2,1,0:T(8,128)S(1)}, u32[]{:S(2)}, u32[]{:S(2)}) async-start(f32[16,16,256]{2,1,0:T(8,128)} %sum_repeat.5.refs_0_), calls=%async_computation.2 | async-start | bytes 524288 | tf_op jit(solution)/shard_map/all_to_all | solution.py:399
  84.6 18.3 %copy-start.6 = (f32[2,256,256]{2,1,0:T(8,128)S(1)}, f32[2,256,256]{2,1,0:T(8,128)}, u32[]{:S(2)}) copy-start(f32[2,256,256]{2,1,0:T(8,128)} %refs_8_.3) | copy-start | bytes 1572868
  84.7 18.3 %copy-start.16 = (bf16[256,512]{1,0:T(8,128)(2,1)S(1)}, bf16[256,512]{1,0:T(8,128)(2,1)}, u32[]{:S(2)}) copy-start(bf16[256,512]{1,0:T(8,128)(2,1)} %constant.18.clone.refs_9_) | copy-start | bytes 786436
  87.3 14.1 %collective-permute-start.13 = (f32[2,384,128]{2,1,0:T(8,128)S(1)}, f32[2,384,128]{2,1,0:T(8,128)S(1)}, u32[]{:S(2)}, u32[]{:S(2)}) collective-permute-start(f32[2,384,128]{2,1,0:T(8,128)S(1)} %stack.23.refs_5_), channel_id=1, source_target_pairs={{1,2},{2,1},{3,4},{4,3},{5,6},{6,5},{7,8},{8,7},{9,10},{10,9},{11,... | collective-permute-start | bytes 1179656 | tf_op jit(solution)/shard_map/ppermute | solution.py:71
  93.4 8.8 %collective-permute-start.12 = (f32[2,384,128]{2,1,0:T(8,128)S(1)}, f32[2,384,128]{2,1,0:T(8,128)S(1)}, u32[]{:S(2)}, u32[]{:S(2)}) collective-permute-start(f32[2,384,128]{2,1,0:T(8,128)S(1)} %stack.23.refs_5_), channel_id=1, source_target_pairs={{0,1},{1,0},{2,3},{3,2},{4,5},{5,4},{6,7},{7,6},{8,9},{9,8},{10,11... | collective-permute-start | bytes 1179656 | tf_op jit(solution)/shard_map/ppermute | solution.py:71
  93.6 9.4 %collective-permute-start.9 = (f32[256,256]{1,0:T(8,128)S(1)}, f32[256,256]{1,0:T(8,128)S(1)}, u32[]{:S(2)}, u32[]{:S(2)}) collective-permute-start(f32[256,256]{1,0:T(8,128)S(1)} %bitcast.17), channel_id=1, source_target_pairs={{0,1},{1,0},{2,3},{3,2},{4,5},{5,4},{6,7},{7,6},{8,9},{9,8},{10,11... | collective-permute-start | bytes 786440 | tf_op jit(solution)/shard_map/ppermute | solution.py:71
  101.4 0.8 copy-start.9
  102.2 0.7 copy-start.11
  103.0 1.0 copy-start.10
  104.0 1.0 copy-start.12
  112.3 2.4 %copy-start.1 = (f32[2,384,128]{2,1,0:T(8,128)}, f32[2,384,128]{2,1,0:T(8,128)S(1)}, u32[]{:S(2)}) copy-start(f32[2,384,128]{2,1,0:T(8,128)S(1)} %get-tuple-element.30.refs_0_) | copy-start | bytes 1179652
  112.3 2.4 %copy-start.7 = (f32[2,384,128]{2,1,0:T(8,128)}, f32[2,384,128]{2,1,0:T(8,128)S(1)}, u32[]{:S(2)}) copy-start(f32[2,384,128]{2,1,0:T(8,128)S(1)} %get-tuple-element.29) | copy-start | bytes 1179652
  112.4 1.6 collective-permute-start.15
  114.7 8.5 %copy-start.8 = (f32[2,384,128]{2,1,0:T(8,128)S(1)}, f32[2,384,128]{2,1,0:T(8,128)}, u32[]{:S(2)}) copy-start(f32[2,384,128]{2,1,0:T(8,128)} %copy-done.7) | copy-start | bytes 1179652
  114.7 14.8 %all-to-all-start.3 = ((f32[16,16,256]{2,1,0:T(8,128)}), f32[16,16,256]{2,1,0:T(8,128)S(1)}, u32[]{:S(2)}, u32[]{:S(2)}) async-start(f32[16,16,256]{2,1,0:T(8,128)} %bitcast.7.refs_1_), calls=%async_computation.3 | async-start | bytes 524288 | tf_op jit(solution)/shard_map/all_to_all | solution.py:389
  123.2 12.5 %collective-permute-start.14 = (f32[2,384,128]{2,1,0:T(8,128)S(1)}, f32[2,384,128]{2,1,0:T(8,128)S(1)}, u32[]{:S(2)}, u32[]{:S(2)}) collective-permute-start(f32[2,384,128]{2,1,0:T(8,128)S(1)} %copy-done.8), channel_id=1, source_target_pairs={{0,1},{1,0},{2,3},{3,2},{4,5},{5,4},{6,7},{7,6},{8,9},{9,8},{10,11... | collective-permute-start | bytes 1179656 | tf_op jit(solution)/shard_map/ppermute | solution.py:71
  124.2 13.7 %collective-permute-start.16 = (f32[2,384,128]{2,1,0:T(8,128)}, f32[2,384,128]{2,1,0:T(8,128)S(1)}, u32[]{:S(2)}, u32[]{:S(2)}) collective-permute-start(f32[2,384,128]{2,1,0:T(8,128)} %hold.2), channel_id=1, source_target_pairs={{1,2},{2,1},{3,4},{4,3},{5,6},{6,5},{7,8},{8,7},{9,10},{10,9},{11,... | collective-permute-start | bytes 1179656 | tf_op jit(solution)/shard_map/ppermute | solution.py:71
  130.2 13.5 %all-to-all-start.4 = ((f32[8,16,256]{2,1,0:T(8,128)}), f32[8,16,256]{2,1,0:T(8,128)S(1)}, u32[]{:S(2)}, u32[]{:S(2)}) async-start(f32[8,16,256]{2,1,0:T(8,128)} %sum_repeat.6), calls=%async_computation.4 | async-start | bytes 262144 | tf_op jit(solution)/shard_map/all_to_all | solution.py:393
  144.5 15.1 %all-to-all-start.5 = ((f32[16,16,256]{2,1,0:T(8,128)}), f32[16,16,256]{2,1,0:T(8,128)S(1)}, u32[]{:S(2)}, u32[]{:S(2)}) async-start(f32[16,16,256]{2,1,0:T(8,128)} %sum_repeat.7), calls=%async_computation.5 | async-start | bytes 524288 | tf_op jit(solution)/shard_map/all_to_all | solution.py:399
  149.5 5.4 %collective-permute-start.17 = (f32[2,128,128]{2,1,0:T(8,128)S(1)}, f32[2,128,128]{2,1,0:T(8,128)S(1)}, u32[]{:S(2)}, u32[]{:S(2)}) collective-permute-start(f32[2,128,128]{2,1,0:T(8,128)S(1)} %get-tuple-element.33), channel_id=1, source_target_pairs={{0,32},{32,0},{64,96},{96,64},{128,160},{160,128},{192,224},{224,1... | collective-permute-start | bytes 393224 | tf_op jit(solution)/shard_map/ppermute | solution.py:71
  150.7 8.1 %collective-permute-start.18 = (f32[2,128,128]{2,1,0:T(8,128)S(1)}, f32[2,128,128]{2,1,0:T(8,128)S(1)}, u32[]{:S(2)}, u32[]{:S(2)}) collective-permute-start(f32[2,128,128]{2,1,0:T(8,128)S(1)} %get-tuple-element.35), channel_id=1, source_target_pairs={{32,64},{64,32},{96,128},{128,96},{160,192},{192,160},{33,65},{65,... | collective-permute-start | bytes 393224 | tf_op jit(solution)/shard_map/ppermute | solution.py:71
  160.2 4.9 %collective-permute-start.19 = (f32[256,256]{1,0:T(8,128)}, f32[256,256]{1,0:T(8,128)S(1)}, u32[]{:S(2)}, u32[]{:S(2)}) collective-permute-start(f32[256,256]{1,0:T(8,128)} %hold.3), channel_id=1, source_target_pairs={{0,1},{1,0},{2,3},{3,2},{4,5},{5,4},{6,7},{7,6},{8,9},{9,8},{10,11... | collective-permute-start | bytes 786440 | tf_op jit(solution)/shard_map/ppermute | solution.py:71

commit v4 on v3

--- a/solution.py
+++ b/solution.py
@@ -112,7 +112,9 @@
     moves[0].wait()
     if renew:
         renewed(probe, own, other, core, probe)
-    probe_out[...] = probe[...]
+        probe_out[...] = probe[...]
+    else:
+        probe_out[...] = jnp.zeros_like(probe_out)
     for move in moves[1:4]:
         move.wait()
     for p in range(count):
@@ -206,10 +208,12 @@
     rows, cols = side + side // 2, parts[0].shape[2]
     strip, square, wave = shape(2, rows, cols), shape(side, side), shape(2, side, side)
     count = amplitude.shape[0]
+    if not renew:
+        wave = shape(8, 128)
     return pl.pallas_call(
         lambda *refs: update_kernel(renew, *refs),
         out_shape=(strip, square, square, wave, strip, strip),
-        in_specs=[SMEM] * 2 + [VMEM] * 2 + [HBM] * 6,
+        in_specs=[SMEM] * 2 + [VMEM if renew else ANY] * 2 + [HBM] * 6,
         out_specs=[VMEM] * 4 + [HBM] * 2,
         scratch_shapes=(
             pltpu.VMEM((3, 2, rows, cols), f32),
@@ -227,6 +231,7 @@
             pltpu.SemaphoreType.DMA((8,)),
         ),
         compiler_params=pltpu.CompilerParams(vmem_limit_bytes=VMEM_LIMIT),
+        input_output_aliases={5: 0, 2: 1, 3: 2, 4: 4, 6: 5} if renew else {},
         cost_estimate=pl.CostEstimate(
             flops=count * 64 * side**3, bytes_accessed=0, transcendentals=0
         ),
@@ -243,6 +248,13 @@
         input_output_aliases={0: 0},
         name="hold",
     )(value, after)
+
+
+def relay(value, after):
+    def kernel(value, out):
+        out[...] = value[...]
+
+    return call(kernel, shape(*value.shape), (value,), "relay", scalars=0, after=after)
 
 
 def finish(ids, probe, own, other):
@@ -328,7 +340,7 @@
     )
 
 
-def split(ids, sib, mid, cross):
+def split(ids, sib, mid, cross, after):
     channels, tall, cols = mid.shape
     rows = tall // 3
 
@@ -345,7 +357,8 @@
 
     cross = pair_swap(cross, COL, 1)
     sib = pair_swap(sib, COL, 0)
-    near, own, far = call(kernel, [shape(channels, rows, cols)] * 3, (ids, mid, sib, cross), "split")
+    parts = [shape(channels, rows, cols)] * 3
+    near, own, far = call(kernel, parts, (ids, mid, sib, cross), "split", after=after)
     return pair_swap(near, ROW, 0), own, pair_swap(far, ROW, 1)
 
 
@@ -385,7 +398,7 @@
         ways, deep = part.shape[0], lax.axis_size("z")
         if last:
             cross = hold(cross, part)
-        near, centre, far = split(ids, sib, mid, cross)
+        near, centre, far = split(ids, sib, mid, cross, (bright,))
         part = lax.all_to_all(part, PLANE, 0, 0)
         part = sum_and_repeat(part, deep, () if last else (centre,))
         if not last:
@@ -397,7 +410,9 @@
         else:
             parts = widen(ids, tile, (part,))
         own = lax.all_to_all(part, PLANE, 0, 0).reshape(side, side)
-        other = pair_swap(hold(own, tile) if last else own, "core", 0)
+        if last:
+            own = relay(own, (tile,))
+        other = pair_swap(own, "core", 0)
     return tile, finish(ids, probe, own, other)
 
 

time: 168 us -> 167 us (level)
  waiting for transfers between devices: 45.9 us -> 42.2 us
  starting transfers between devices: 82.2 us -> 85.7 us
    ppermute x20, waiting for transfers between devices: 39.9 us -> 32.2 us  [pair_swap(): return lax.ppermute(value, axis, pairs)]
    all_to_all x2, waiting for transfers between devices: 0.87 us -> 4.79 us  [on_device(): part = lax.all_to_all(part, PLANE, 0, 0)]
    ppermute x20, starting transfers between devices: 45.7 us -> 48.7 us  [pair_swap(): return lax.ppermute(value, axis, pairs)]
    unnamed x37 -> x30, local copies, waits for them, and re-layouts: 5.56 us -> 3.35 us
    pallas_call x13 -> x14, Pallas kernels: 11.6 us -> 11.6 us  [call(): pl.pallas_call(body, out_shape=out_shape, in_specs=[ANY] * waits + [SMEM]...]
  transfers between devices with their start and end apart: 26 -> 26, of which waited for: 14 -> 13; matrix products, arithmetic and copies ran while one was open for 2% -> 3% of each run, Pallas kernels for 5% -> 5%
where the time goes in v4:
time: 167 us; the launch traced here: 166 us
  starting transfers between devices  85.7 us (51%)
  waiting for transfers between devices  42.2 us (25%)
  Pallas kernels  27 us (16%)
  other arithmetic  5.05 us (3%)
  local copies, waits for them, and re-layouts  4.79 us (3%)
    ppermute x20, starting transfers between devices, pair_swap(): return lax.ppermute(value, axis, pairs)  48.7 us
    ppermute x20, waiting for transfers between devices, pair_swap(): return lax.ppermute(value, axis, pairs)  32.2 us
    pallas_call x2, Pallas kernels, update(): pl.pallas_call(lambda *refs: update_kernel(renew, *refs), out_shape=(stri...  15.4 us
    all_to_all x2, starting transfers between devices, on_device(): part = lax.all_to_all(part, PLANE, 0, 0)  14.3 us
    all_to_all x2, starting transfers between devices, on_device(): part = lax.all_to_all(part, 'z', 0, 0)  12.8 us
    pallas_call x14, Pallas kernels, call(): pl.pallas_call(body, out_shape=out_shape, in_specs=[ANY] * waits + [SMEM]...  11.6 us
    all_to_all x2, starting transfers between devices, on_device(): own = lax.all_to_all(part, PLANE, 0, 0).reshape(side, side)  9.98 us
    all_to_all x2, waiting for transfers between devices, on_device(): part = lax.all_to_all(part, 'z', 0, 0)  5.18 us
  transfers between devices with their start and end apart: 26, of which 13 were waited for; matrix products, arithmetic and copies ran while one was open for 3% of the time, Pallas kernels for 5%

profile of v4, /device:TPU:3, one launch (start us, length us, event | category | flops | bytes accessed | tf_op | source)
XLA Modules:
  0.0 165.7 jit_solution(10763410291592532648)
XLA Ops:
  0.7 0.7 copy-done.14
  1.4 0.1 add.27
  1.5 0.9 pad_maximum_fusion.refs_2_
  2.4 3.2 %collective-permute-start.1 = (f32[2,136,128]{2,1,0:T(8,128)S(1)}, f32[2,136,128]{2,1,0:T(8,128)S(1)}, u32[]{:S(2)}, u32[]{:S(2)}) collective-permute-start(f32[2,136,128]{2,1,0:T(8,128)S(1)} %pad_maximum_fusion.refs_2_), channel_id=1, source_target_pairs={{32,64},{64,32},{96,128},{128,96},{160,192},{192,160},{33,65},{65,... | collective-permute-start | bytes 417800 | tf_op jit(solution)/shard_map/ppermute | solution.py:71
  5.6 1.2 collective-permute-start
  6.9 2.9 %collective-permute-done.1.refs_3_ = f32[2,136,128]{2,1,0:T(8,128)S(1)} collective-permute-done((f32[2,136,128]{2,1,0:T(8,128)S(1)}, f32[2,136,128]{2,1,0:T(8,128)S(1)}, u32[]{:S(2)}, u32[]{:S(2)}) %collective-permute-start.1) | collective-permute-done | bytes 139296 | tf_op jit(solution)/shard_map/ppermute | solution.py:71
  9.7 4.0 %collective-permute-done.refs_1_ = f32[2,136,128]{2,1,0:T(8,128)S(1)} collective-permute-done((f32[2,136,128]{2,1,0:T(8,128)S(1)}, f32[2,136,128]{2,1,0:T(8,128)S(1)}, u32[]{:S(2)}, u32[]{:S(2)}) %collective-permute-start) | collective-permute-done | bytes 139296 | tf_op jit(solution)/shard_map/ppermute | solution.py:71
  13.8 0.6 stack.22.refs_5_
  14.4 5.3 %collective-permute-start.3 = (f32[2,408,128]{2,1,0:T(8,128)S(1)}, f32[2,408,128]{2,1,0:T(8,128)S(1)}, u32[]{:S(2)}, u32[]{:S(2)}) collective-permute-start(f32[2,408,128]{2,1,0:T(8,128)S(1)} %stack.22.refs_5_), channel_id=1, source_target_pairs={{1,2},{2,1},{3,4},{4,3},{5,6},{6,5},{7,8},{8,7},{9,10},{10,9},{11,... | collective-permute-start | bytes 1253384 | tf_op jit(solution)/shard_map/ppermute | solution.py:71
  19.7 0.1 collective-permute-start.2
  19.8 1.5 fusion.1.refs_7_
  21.4 7.8 %collective-permute-done.3.refs_6_ = f32[2,408,128]{2,1,0:T(8,128)S(1)} collective-permute-done((f32[2,408,128]{2,1,0:T(8,128)S(1)}, f32[2,408,128]{2,1,0:T(8,128)S(1)}, u32[]{:S(2)}, u32[]{:S(2)}) %collective-permute-start.3) | collective-permute-done | bytes 417824 | tf_op jit(solution)/shard_map/ppermute | solution.py:71
  29.2 8.0 %update.2 = (f32[2,384,128]{2,1,0:T(8,128)S(1)}, f32[256,256]{1,0:T(8,128)S(1)}, f32[256,256]{1,0:T(8,128)}, f32[8,128]{1,0:T(8,128)}, f32[2,384,128]{2,1,0:T(8,128)}, /*index=5*/f32[2,384,128]{2,1,0:T(8,128)}) custom-call(s32[2]{0:T(128)S(1)} %pad_add_fusion.refs_0_.refs_1_, s32[4,2]{1,0:T(4,128)S(1)} %bitcast.18, f32[256,256]{1,0:T(8,128)S(1)} %copy-done.3, ...), custom_call_target="tpu_custom_call" | custom-call | flops 4294967296 | tf_op jit(solution)/shard_map/update/pallas_call | solution.py:213
  37.2 0.1 collective-permute-start.6
  37.3 0.5 collective-permute-start.4
  37.8 5.9 %collective-permute-start.5 = (f32[2,384,128]{2,1,0:T(8,128)}, f32[2,384,128]{2,1,0:T(8,128)S(1)}, u32[]{:S(2)}, u32[]{:S(2)}) collective-permute-start(f32[2,384,128]{2,1,0:T(8,128)} %get-tuple-element.21), channel_id=1, source_target_pairs={{1,2},{2,1},{3,4},{4,3},{5,6},{6,5},{7,8},{8,7},{9,10},{10,9},{11,... | collective-permute-start | bytes 1179656 | tf_op jit(solution)/shard_map/ppermute | solution.py:71
  43.7 0.6 slice.10
  44.3 0.7 slice.9
  45.0 1.7 %add.28 = f32[256,256]{1,0:T(8,128)} add(f32[256,256]{1,0:T(8,128)S(1)} %get-tuple-element.23, f32[256,256]{1,0:T(8,128)} %collective-permute-done.6) | non-fusion elementwise | flops 65536 | bytes 786432 | tf_op jit(solution)/shard_map/add | solution.py:279
  46.7 5.9 %all-to-all-start = ((f32[16,16,256]{2,1,0:T(8,128)}), f32[16,16,256]{2,1,0:T(8,128)S(1)}, u32[]{:S(2)}, u32[]{:S(2)}) async-start(f32[16,16,256]{2,1,0:T(8,128)} %bitcast.5), calls=%async_computation | async-start | bytes 524288 | tf_op jit(solution)/shard_map/all_to_all | solution.py:402
  52.7 2.0 %light.2.refs_0_.refs_2_ = f32[128,128]{1,0:T(8,128)S(1)} custom-call(s32[2]{0:T(128)S(1)} %pad_add_fusion.refs_0_.refs_1_, s32[3,3,8]{2,1,0:T(4,128)S(1)} %maximum_convert_fusion.refs_1_, f32[2,256,256]{2,1,0:T(8,128)S(1)} %copy-done.6), custom_call_target="tpu_custom_call" | custom-call | flops 2000000000 | bytes 524584 | tf_op jit(solution)/shard_map/light/pallas_call | solution.py:48
  54.7 0.6 split.2
  55.3 4.0 %all-to-all-done.refs_1_ = f32[16,16,256]{2,1,0:T(8,128)S(1)} async-done(((f32[16,16,256]{2,1,0:T(8,128)}), f32[16,16,256]{2,1,0:T(8,128)S(1)}, u32[]{:S(2)}, u32[]{:S(2)}) %all-to-all-start) | async-done | bytes 262176 | tf_op jit(solution)/shard_map/all_to_all | solution.py:402
  59.3 0.7 sum_repeat.4.refs_0_
  60.0 7.3 %all-to-all-start.1 = ((f32[8,16,256]{2,1,0:T(8,128)}), f32[8,16,256]{2,1,0:T(8,128)S(1)}, u32[]{:S(2)}, u32[]{:S(2)}) async-start(f32[8,16,256]{2,1,0:T(8,128)} %sum_repeat.4.refs_0_), calls=%async_computation.1 | async-start | bytes 262144 | tf_op jit(solution)/shard_map/all_to_all | solution.py:406
  67.3 0.6 collective-permute-start.7
  67.9 4.3 %collective-permute-start.8 = (f32[2,128,128]{2,1,0:T(8,128)S(1)}, f32[2,128,128]{2,1,0:T(8,128)S(1)}, u32[]{:S(2)}, u32[]{:S(2)}) collective-permute-start(f32[2,128,128]{2,1,0:T(8,128)S(1)} %get-tuple-element.26), channel_id=1, source_target_pairs={{32,64},{64,32},{96,128},{128,96},{160,192},{192,160},{33,65},{65,... | collective-permute-start | bytes 393224 | tf_op jit(solution)/shard_map/ppermute | solution.py:71
  72.2 2.7 %collective-permute-done.8.refs_5_ = f32[2,128,128]{2,1,0:T(8,128)S(1)} collective-permute-done((f32[2,128,128]{2,1,0:T(8,128)S(1)}, f32[2,128,128]{2,1,0:T(8,128)S(1)}, u32[]{:S(2)}, u32[]{:S(2)}) %collective-permute-start.8) | collective-permute-done | bytes 131104 | tf_op jit(solution)/shard_map/ppermute | solution.py:71
  74.9 4.2 %collective-permute-start.11 = (f32[2,128,128]{2,1,0:T(8,128)S(1)}, f32[2,128,128]{2,1,0:T(8,128)S(1)}, u32[]{:S(2)}, u32[]{:S(2)}) collective-permute-start(f32[2,128,128]{2,1,0:T(8,128)S(1)} %renew.2.refs_0_.refs_3_), channel_id=1, source_target_pairs={{32,64},{64,32},{96,128},{128,96},{160,192},{192,160},{33,65},{65,... | collective-permute-start | bytes 393224 | tf_op jit(solution)/shard_map/ppermute | solution.py:71
  79.2 0.1 collective-permute-start.10
  79.3 0.7 sum_repeat.5.refs_0_
  80.0 4.9 %all-to-all-start.2 = ((f32[16,16,256]{2,1,0:T(8,128)}), f32[16,16,256]{2,1,0:T(8,128)S(1)}, u32[]{:S(2)}, u32[]{:S(2)}) async-start(f32[16,16,256]{2,1,0:T(8,128)} %sum_repeat.5.refs_0_), calls=%async_computation.2 | async-start | bytes 524288 | tf_op jit(solution)/shard_map/all_to_all | solution.py:412
  85.0 0.6 stack.23.refs_5_
  85.5 8.5 %collective-permute-start.13 = (f32[2,384,128]{2,1,0:T(8,128)S(1)}, f32[2,384,128]{2,1,0:T(8,128)S(1)}, u32[]{:S(2)}, u32[]{:S(2)}) collective-permute-start(f32[2,384,128]{2,1,0:T(8,128)S(1)} %stack.23.refs_5_), channel_id=1, source_target_pairs={{1,2},{2,1},{3,4},{4,3},{5,6},{6,5},{7,8},{8,7},{9,10},{10,9},{11,... | collective-permute-start | bytes 1179656 | tf_op jit(solution)/shard_map/ppermute | solution.py:71
  94.1 0.1 collective-permute-start.12
  94.2 1.9 %collective-permute-start.9 = (f32[256,256]{1,0:T(8,128)S(1)}, f32[256,256]{1,0:T(8,128)S(1)}, u32[]{:S(2)}, u32[]{:S(2)}) collective-permute-start(f32[256,256]{1,0:T(8,128)S(1)} %bitcast.15), channel_id=1, source_target_pairs={{0,1},{1,0},{2,3},{3,2},{4,5},{5,4},{6,7},{7,6},{8,9},{9,8},{10,11... | collective-permute-start | bytes 786440 | tf_op jit(solution)/shard_map/ppermute | solution.py:71
  96.0 6.0 %collective-permute-done.13.refs_6_ = f32[2,384,128]{2,1,0:T(8,128)S(1)} collective-permute-done((f32[2,384,128]{2,1,0:T(8,128)S(1)}, f32[2,384,128]{2,1,0:T(8,128)S(1)}, u32[]{:S(2)}, u32[]{:S(2)}) %collective-permute-start.13) | collective-permute-done | bytes 393248 | tf_op jit(solution)/shard_map/ppermute | solution.py:71
  102.0 0.7 copy-done.7
  102.8 1.0 copy-done.8
  103.8 7.4 %update.3 = (f32[2,384,128]{2,1,0:T(8,128)S(1)}, f32[256,256]{1,0:T(8,128)S(1)}, f32[256,256]{1,0:T(8,128)S(1)}, f32[2,256,256]{2,1,0:T(8,128)S(1)}, f32[2,384,1...) custom-call(s32[2]{0:T(128)S(1)} %pad_add_fusion.refs_0_.refs_1_, ...), custom_call_target="tpu_custom_call", output_to_operand_aliasing={{0}: (5, {}), {1}: (2, {}), {2}: (3, {}), {4}: (4, {}), {5}... | custom-call | flops 4294967296 | tf_op jit(solution)/shard_map/update/pallas_call | solution.py:213
  111.2 0.1 collective-permute-start.15
  111.3 1.5 collective-permute-done.15
  112.8 0.7 add.29
  113.6 8.4 %all-to-all-start.3 = ((f32[16,16,256]{2,1,0:T(8,128)}), f32[16,16,256]{2,1,0:T(8,128)S(1)}, u32[]{:S(2)}, u32[]{:S(2)}) async-start(f32[16,16,256]{2,1,0:T(8,128)} %bitcast.7.refs_1_), calls=%async_computation.3 | async-start | bytes 524288 | tf_op jit(solution)/shard_map/all_to_all | solution.py:402
  122.0 1.0 collective-permute-start.14
  123.0 4.5 %collective-permute-start.16 = (f32[2,384,128]{2,1,0:T(8,128)}, f32[2,384,128]{2,1,0:T(8,128)S(1)}, u32[]{:S(2)}, u32[]{:S(2)}) collective-permute-start(f32[2,384,128]{2,1,0:T(8,128)} %hold.1), channel_id=1, source_target_pairs={{1,2},{2,1},{3,4},{4,3},{5,6},{6,5},{7,8},{8,7},{9,10},{10,9},{11,... | collective-permute-start | bytes 1179656 | tf_op jit(solution)/shard_map/ppermute | solution.py:71
  127.5 0.8 all-to-all-done.3.refs_0_
  128.3 0.7 sum_repeat.6
  129.0 5.5 %all-to-all-start.4 = ((f32[8,16,256]{2,1,0:T(8,128)}), f32[8,16,256]{2,1,0:T(8,128)S(1)}, u32[]{:S(2)}, u32[]{:S(2)}) async-start(f32[8,16,256]{2,1,0:T(8,128)} %sum_repeat.6), calls=%async_computation.4 | async-start | bytes 262144 | tf_op jit(solution)/shard_map/all_to_all | solution.py:406
  134.5 2.0 %light.3.refs_0_.refs_1_ = f32[128,128]{1,0:T(8,128)S(1)} custom-call(s32[2]{0:T(128)S(1)} %pad_add_fusion.refs_0_.refs_1_, s32[3,3,8]{2,1,0:T(4,128)S(1)} %maximum_convert_fusion.refs_1_, f32[2,256,256]{2,1,0:T(8,128)S(1)} %get-tuple-element.27.refs_2_.refs_1_), custom_call_target="tpu_custom_call" | custom-call | flops 2000000000 | bytes 524584 | tf_op jit(solution)/shard_map/light/pallas_call | solution.py:48
  136.6 0.2 collective-permute-done.16.refs_4_
  136.8 0.6 split.3
  137.4 5.2 %all-to-all-done.4.refs_1_ = f32[8,16,256]{2,1,0:T(8,128)S(1)} async-done(((f32[8,16,256]{2,1,0:T(8,128)}), f32[8,16,256]{2,1,0:T(8,128)S(1)}, u32[]{:S(2)}, u32[]{:S(2)}) %all-to-all-start.4) | async-done | bytes 131104 | tf_op jit(solution)/shard_map/all_to_all | solution.py:406
  142.6 0.7 sum_repeat.7
  143.3 5.1 %all-to-all-start.5 = ((f32[16,16,256]{2,1,0:T(8,128)}), f32[16,16,256]{2,1,0:T(8,128)S(1)}, u32[]{:S(2)}, u32[]{:S(2)}) async-start(f32[16,16,256]{2,1,0:T(8,128)} %sum_repeat.7), calls=%async_computation.5 | async-start | bytes 524288 | tf_op jit(solution)/shard_map/all_to_all | solution.py:412
  148.4 1.2 collective-permute-start.17
  149.6 2.2 %collective-permute-start.18 = (f32[2,128,128]{2,1,0:T(8,128)S(1)}, f32[2,128,128]{2,1,0:T(8,128)S(1)}, u32[]{:S(2)}, u32[]{:S(2)}) collective-permute-start(f32[2,128,128]{2,1,0:T(8,128)S(1)} %get-tuple-element.35), channel_id=1, source_target_pairs={{32,64},{64,32},{96,128},{128,96},{160,192},{192,160},{33,65},{65,... | collective-permute-start | bytes 393224 | tf_op jit(solution)/shard_map/ppermute | solution.py:71
  151.7 1.9 %collective-permute-done.17.refs_2_ = f32[2,128,128]{2,1,0:T(8,128)S(1)} collective-permute-done((f32[2,128,128]{2,1,0:T(8,128)S(1)}, f32[2,128,128]{2,1,0:T(8,128)S(1)}, u32[]{:S(2)}, u32[]{:S(2)}) %collective-permute-start.17) | collective-permute-done | bytes 131104 | tf_op jit(solution)/shard_map/ppermute | solution.py:71
  153.6 4.1 %collective-permute-done.18.refs_4_ = f32[2,128,128]{2,1,0:T(8,128)S(1)} collective-permute-done((f32[2,128,128]{2,1,0:T(8,128)S(1)}, f32[2,128,128]{2,1,0:T(8,128)S(1)}, u32[]{:S(2)}, u32[]{:S(2)}) %collective-permute-start.18) | collective-permute-done | bytes 131104 | tf_op jit(solution)/shard_map/ppermute | solution.py:71
  157.7 0.7 renew.3.refs_0_
  158.4 0.9 copy-done
  159.3 3.6 %collective-permute-start.19 = (f32[256,256]{1,0:T(8,128)S(1)}, f32[256,256]{1,0:T(8,128)S(1)}, u32[]{:S(2)}, u32[]{:S(2)}) collective-permute-start(f32[256,256]{1,0:T(8,128)S(1)} %relay.1.refs_2_), channel_id=1, source_target_pairs={{0,1},{1,0},{2,3},{3,2},{4,5},{5,4},{6,7},{7,6},{8,9},{9,8},{10,11... | collective-permute-start | bytes 786440 | tf_op jit(solution)/shard_map/ppermute | solution.py:71
  162.9 1.2 collective-permute-done.19.refs_3_
  164.1 1.6 finish.1
  (50 shorter events, 0.3 us)
Async XLA Ops:
  0.6 0.7 copy-start.14
  2.4 7.3 %collective-permute-start.1 = (f32[2,136,128]{2,1,0:T(8,128)S(1)}, f32[2,136,128]{2,1,0:T(8,128)S(1)}, u32[]{:S(2)}, u32[]{:S(2)}) collective-permute-start(f32[2,136,128]{2,1,0:T(8,128)S(1)} %pad_maximum_fusion.refs_2_), channel_id=1, source_target_pairs={{32,64},{64,32},{96,128},{128,96},{160,192},{192,160},{33,65},{65,... | collective-permute-start | bytes 417800 | tf_op jit(solution)/shard_map/ppermute | solution.py:71
  5.6 8.2 %collective-permute-start = (f32[2,136,128]{2,1,0:T(8,128)S(1)}, f32[2,136,128]{2,1,0:T(8,128)S(1)}, u32[]{:S(2)}, u32[]{:S(2)}) collective-permute-start(f32[2,136,128]{2,1,0:T(8,128)S(1)} %pad_maximum_fusion.refs_2_), channel_id=1, source_target_pairs={{0,32},{32,0},{64,96},{96,64},{128,160},{160,128},{192,224},{224,1... | collective-permute-start | bytes 417800 | tf_op jit(solution)/shard_map/ppermute | solution.py:71
  6.9 12.9 %copy-start.3 = (f32[256,256]{1,0:T(8,128)S(1)}, f32[256,256]{1,0:T(8,128)}, u32[]{:S(2)}) copy-start(f32[256,256]{1,0:T(8,128)} %refs_3_.1) | copy-start | bytes 786436
  14.4 14.8 %copy-start.5 = (f32[2,256,256]{2,1,0:T(8,128)S(1)}, f32[2,256,256]{2,1,0:T(8,128)}, u32[]{:S(2)}) copy-start(f32[2,256,256]{2,1,0:T(8,128)} %refs_8_.3) | copy-start | bytes 1572868
  14.4 14.8 %copy-start.11 = (bf16[256,512]{1,0:T(8,128)(2,1)S(1)}, bf16[256,512]{1,0:T(8,128)(2,1)}, u32[]{:S(2)}) copy-start(bf16[256,512]{1,0:T(8,128)(2,1)} %constant.18.clone.refs_9_) | copy-start | bytes 786436
  14.4 14.8 %collective-permute-start.3 = (f32[2,408,128]{2,1,0:T(8,128)S(1)}, f32[2,408,128]{2,1,0:T(8,128)S(1)}, u32[]{:S(2)}, u32[]{:S(2)}) collective-permute-start(f32[2,408,128]{2,1,0:T(8,128)S(1)} %stack.22.refs_5_), channel_id=1, source_target_pairs={{1,2},{2,1},{3,4},{4,3},{5,6},{6,5},{7,8},{8,7},{9,10},{10,9},{11,... | collective-permute-start | bytes 1253384 | tf_op jit(solution)/shard_map/ppermute | solution.py:71
  19.7 9.4 %collective-permute-start.2 = (f32[2,408,128]{2,1,0:T(8,128)S(1)}, f32[2,408,128]{2,1,0:T(8,128)S(1)}, u32[]{:S(2)}, u32[]{:S(2)}) collective-permute-start(f32[2,408,128]{2,1,0:T(8,128)S(1)} %stack.22.refs_5_), channel_id=1, source_target_pairs={{0,1},{1,0},{2,3},{3,2},{4,5},{5,4},{6,7},{7,6},{8,9},{9,8},{10,11... | collective-permute-start | bytes 1253384 | tf_op jit(solution)/shard_map/ppermute | solution.py:71
  29.2 8.0 %copy-start.4 = (f32[2,408,128]{2,1,0:T(8,128)}, f32[2,408,128]{2,1,0:T(8,128)S(1)}, u32[]{:S(2)}) copy-start(f32[2,408,128]{2,1,0:T(8,128)S(1)} %collective-permute-done.2.refs_4_) | copy-start | bytes 1253380
  37.2 7.8 %collective-permute-start.6 = (f32[256,256]{1,0:T(8,128)}, f32[256,256]{1,0:T(8,128)}, u32[]{:S(2)}, u32[]{:S(2)}) collective-permute-start(f32[256,256]{1,0:T(8,128)} %get-tuple-element.24), channel_id=1, source_target_pairs={{0,1},{1,0},{2,3},{3,2},{4,5},{5,4},{6,7},{7,6},{8,9},{9,8},{10,11... | collective-permute-start | bytes 786440 | tf_op jit(solution)/shard_map/ppermute | solution.py:71
  37.3 17.4 %collective-permute-start.4 = (f32[2,384,128]{2,1,0:T(8,128)}, f32[2,384,128]{2,1,0:T(8,128)S(1)}, u32[]{:S(2)}, u32[]{:S(2)}) collective-permute-start(f32[2,384,128]{2,1,0:T(8,128)} %get-tuple-element.20), channel_id=1, source_target_pairs={{0,1},{1,0},{2,3},{3,2},{4,5},{5,4},{6,7},{7,6},{8,9},{9,8},{10,11... | collective-permute-start | bytes 1179656 | tf_op jit(solution)/shard_map/ppermute | solution.py:71
  37.8 16.9 %collective-permute-start.5 = (f32[2,384,128]{2,1,0:T(8,128)}, f32[2,384,128]{2,1,0:T(8,128)S(1)}, u32[]{:S(2)}, u32[]{:S(2)}) collective-permute-start(f32[2,384,128]{2,1,0:T(8,128)} %get-tuple-element.21), channel_id=1, source_target_pairs={{1,2},{2,1},{3,4},{4,3},{5,6},{6,5},{7,8},{8,7},{9,10},{10,9},{11,... | collective-permute-start | bytes 1179656 | tf_op jit(solution)/shard_map/ppermute | solution.py:71
  45.0 7.6 %copy-start.13 = (f32[1,3,8]{2,1,0:T(4,128)S(1)}, f32[1,3,8]{2,1,0:T(4,128)}, u32[]{:S(2)}) copy-start(f32[1,3,8]{2,1,0:T(4,128)} %slice.10) | copy-start | bytes 292
  46.7 5.9 %copy-start.6 = (f32[2,256,256]{2,1,0:T(8,128)S(1)}, f32[2,256,256]{2,1,0:T(8,128)}, u32[]{:S(2)}) copy-start(f32[2,256,256]{2,1,0:T(8,128)} %refs_8_.3) | copy-start | bytes 1572868
  46.7 12.6 %all-to-all-start = ((f32[16,16,256]{2,1,0:T(8,128)}), f32[16,16,256]{2,1,0:T(8,128)S(1)}, u32[]{:S(2)}, u32[]{:S(2)}) async-start(f32[16,16,256]{2,1,0:T(8,128)} %bitcast.5), calls=%async_computation | async-start | bytes 524288 | tf_op jit(solution)/shard_map/all_to_all | solution.py:402
  60.0 14.9 %copy-start.1 = (f32[2,128,128]{2,1,0:T(8,128)S(1)}, f32[2,128,128]{2,1,0:T(8,128)}, u32[]{:S(2)}) copy-start(f32[2,128,128]{2,1,0:T(8,128)} %refs_1_.1) | copy-start | bytes 393220
  60.0 19.3 %all-to-all-start.1 = ((f32[8,16,256]{2,1,0:T(8,128)}), f32[8,16,256]{2,1,0:T(8,128)S(1)}, u32[]{:S(2)}, u32[]{:S(2)}) async-start(f32[8,16,256]{2,1,0:T(8,128)} %sum_repeat.4.refs_0_), calls=%async_computation.1 | async-start | bytes 262144 | tf_op jit(solution)/shard_map/all_to_all | solution.py:406
  67.3 5.0 %collective-permute-start.7 = (f32[2,128,128]{2,1,0:T(8,128)S(1)}, f32[2,128,128]{2,1,0:T(8,128)S(1)}, u32[]{:S(2)}, u32[]{:S(2)}) collective-permute-start(f32[2,128,128]{2,1,0:T(8,128)S(1)} %get-tuple-element.25), channel_id=1, source_target_pairs={{0,32},{32,0},{64,96},{96,64},{128,160},{160,128},{192,224},{224,1... | collective-permute-start | bytes 393224 | tf_op jit(solution)/shard_map/ppermute | solution.py:71
  67.9 7.0 %collective-permute-start.8 = (f32[2,128,128]{2,1,0:T(8,128)S(1)}, f32[2,128,128]{2,1,0:T(8,128)S(1)}, u32[]{:S(2)}, u32[]{:S(2)}) collective-permute-start(f32[2,128,128]{2,1,0:T(8,128)S(1)} %get-tuple-element.26), channel_id=1, source_target_pairs={{32,64},{64,32},{96,128},{128,96},{160,192},{192,160},{33,65},{65,... | collective-permute-start | bytes 393224 | tf_op jit(solution)/shard_map/ppermute | solution.py:71
  74.9 10.0 %collective-permute-start.11 = (f32[2,128,128]{2,1,0:T(8,128)S(1)}, f32[2,128,128]{2,1,0:T(8,128)S(1)}, u32[]{:S(2)}, u32[]{:S(2)}) collective-permute-start(f32[2,128,128]{2,1,0:T(8,128)S(1)} %renew.2.refs_0_.refs_3_), channel_id=1, source_target_pairs={{32,64},{64,32},{96,128},{128,96},{160,192},{192,160},{33,65},{65,... | collective-permute-start | bytes 393224 | tf_op jit(solution)/shard_map/ppermute | solution.py:71
  79.2 5.8 %collective-permute-start.10 = (f32[2,128,128]{2,1,0:T(8,128)S(1)}, f32[2,128,128]{2,1,0:T(8,128)S(1)}, u32[]{:S(2)}, u32[]{:S(2)}) collective-permute-start(f32[2,128,128]{2,1,0:T(8,128)S(1)} %renew.2.refs_0_.refs_3_), channel_id=1, source_target_pairs={{0,32},{32,0},{64,96},{96,64},{128,160},{160,128},{192,224},{224,1... | collective-permute-start | bytes 393224 | tf_op jit(solution)/shard_map/ppermute | solution.py:71
  80.0 14.1 %all-to-all-start.2 = ((f32[16,16,256]{2,1,0:T(8,128)}), f32[16,16,256]{2,1,0:T(8,128)S(1)}, u32[]{:S(2)}, u32[]{:S(2)}) async-start(f32[16,16,256]{2,1,0:T(8,128)} %sum_repeat.5.refs_0_), calls=%async_computation.2 | async-start | bytes 524288 | tf_op jit(solution)/shard_map/all_to_all | solution.py:412
  84.9 17.9 %copy-start.12 = (bf16[256,512]{1,0:T(8,128)(2,1)S(1)}, bf16[256,512]{1,0:T(8,128)(2,1)}, u32[]{:S(2)}) copy-start(bf16[256,512]{1,0:T(8,128)(2,1)} %constant.18.clone.refs_9_) | copy-start | bytes 786436
  85.5 16.5 %collective-permute-start.13 = (f32[2,384,128]{2,1,0:T(8,128)S(1)}, f32[2,384,128]{2,1,0:T(8,128)S(1)}, u32[]{:S(2)}, u32[]{:S(2)}) collective-permute-start(f32[2,384,128]{2,1,0:T(8,128)S(1)} %stack.23.refs_5_), channel_id=1, source_target_pairs={{1,2},{2,1},{3,4},{4,3},{5,6},{6,5},{7,8},{8,7},{9,10},{10,9},{11,... | collective-permute-start | bytes 1179656 | tf_op jit(solution)/shard_map/ppermute | solution.py:71
  94.1 8.0 %collective-permute-start.12 = (f32[2,384,128]{2,1,0:T(8,128)S(1)}, f32[2,384,128]{2,1,0:T(8,128)S(1)}, u32[]{:S(2)}, u32[]{:S(2)}) collective-permute-start(f32[2,384,128]{2,1,0:T(8,128)S(1)} %stack.23.refs_5_), channel_id=1, source_target_pairs={{0,1},{1,0},{2,3},{3,2},{4,5},{5,4},{6,7},{7,6},{8,9},{9,8},{10,11... | collective-permute-start | bytes 1179656 | tf_op jit(solution)/shard_map/ppermute | solution.py:71
  94.2 8.6 %collective-permute-start.9 = (f32[256,256]{1,0:T(8,128)S(1)}, f32[256,256]{1,0:T(8,128)S(1)}, u32[]{:S(2)}, u32[]{:S(2)}) collective-permute-start(f32[256,256]{1,0:T(8,128)S(1)} %bitcast.15), channel_id=1, source_target_pairs={{0,1},{1,0},{2,3},{3,2},{4,5},{5,4},{6,7},{7,6},{8,9},{9,8},{10,11... | collective-permute-start | bytes 786440 | tf_op jit(solution)/shard_map/ppermute | solution.py:71
  102.0 0.7 copy-start.7
  102.8 1.0 copy-start.8
  111.2 2.4 %copy-start.2 = (f32[2,384,128]{2,1,0:T(8,128)}, f32[2,384,128]{2,1,0:T(8,128)S(1)}, u32[]{:S(2)}) copy-start(f32[2,384,128]{2,1,0:T(8,128)S(1)} %get-tuple-element.30.refs_0_) | copy-start | bytes 1179652
  111.2 2.4 %copy-start.9 = (f32[2,384,128]{2,1,0:T(8,128)}, f32[2,384,128]{2,1,0:T(8,128)S(1)}, u32[]{:S(2)}) copy-start(f32[2,384,128]{2,1,0:T(8,128)S(1)} %get-tuple-element.29) | copy-start | bytes 1179652
  111.2 1.6 collective-permute-start.15
  113.6 8.4 %copy-start.10 = (f32[2,384,128]{2,1,0:T(8,128)S(1)}, f32[2,384,128]{2,1,0:T(8,128)}, u32[]{:S(2)}) copy-start(f32[2,384,128]{2,1,0:T(8,128)} %copy-done.9) | copy-start | bytes 1179652
  113.6 14.7 %all-to-all-start.3 = ((f32[16,16,256]{2,1,0:T(8,128)}), f32[16,16,256]{2,1,0:T(8,128)S(1)}, u32[]{:S(2)}, u32[]{:S(2)}) async-start(f32[16,16,256]{2,1,0:T(8,128)} %bitcast.7.refs_1_), calls=%async_computation.3 | async-start | bytes 524288 | tf_op jit(solution)/shard_map/all_to_all | solution.py:402
  122.0 14.6 %collective-permute-start.14 = (f32[2,384,128]{2,1,0:T(8,128)S(1)}, f32[2,384,128]{2,1,0:T(8,128)S(1)}, u32[]{:S(2)}, u32[]{:S(2)}) collective-permute-start(f32[2,384,128]{2,1,0:T(8,128)S(1)} %copy-done.10), channel_id=1, source_target_pairs={{0,1},{1,0},{2,3},{3,2},{4,5},{5,4},{6,7},{7,6},{8,9},{9,8},{10,11... | collective-permute-start | bytes 1179656 | tf_op jit(solution)/shard_map/ppermute | solution.py:71
  123.0 13.7 %collective-permute-start.16 = (f32[2,384,128]{2,1,0:T(8,128)}, f32[2,384,128]{2,1,0:T(8,128)S(1)}, u32[]{:S(2)}, u32[]{:S(2)}) collective-permute-start(f32[2,384,128]{2,1,0:T(8,128)} %hold.1), channel_id=1, source_target_pairs={{1,2},{2,1},{3,4},{4,3},{5,6},{6,5},{7,8},{8,7},{9,10},{10,9},{11,... | collective-permute-start | bytes 1179656 | tf_op jit(solution)/shard_map/ppermute | solution.py:71
  129.0 13.5 %all-to-all-start.4 = ((f32[8,16,256]{2,1,0:T(8,128)}), f32[8,16,256]{2,1,0:T(8,128)S(1)}, u32[]{:S(2)}, u32[]{:S(2)}) async-start(f32[8,16,256]{2,1,0:T(8,128)} %sum_repeat.6), calls=%async_computation.4 | async-start | bytes 262144 | tf_op jit(solution)/shard_map/all_to_all | solution.py:406
  143.3 15.1 %all-to-all-start.5 = ((f32[16,16,256]{2,1,0:T(8,128)}), f32[16,16,256]{2,1,0:T(8,128)S(1)}, u32[]{:S(2)}, u32[]{:S(2)}) async-start(f32[16,16,256]{2,1,0:T(8,128)} %sum_repeat.7), calls=%async_computation.5 | async-start | bytes 524288 | tf_op jit(solution)/shard_map/all_to_all | solution.py:412
  148.4 5.2 %collective-permute-start.17 = (f32[2,128,128]{2,1,0:T(8,128)S(1)}, f32[2,128,128]{2,1,0:T(8,128)S(1)}, u32[]{:S(2)}, u32[]{:S(2)}) collective-permute-start(f32[2,128,128]{2,1,0:T(8,128)S(1)} %get-tuple-element.33), channel_id=1, source_target_pairs={{0,32},{32,0},{64,96},{96,64},{128,160},{160,128},{192,224},{224,1... | collective-permute-start | bytes 393224 | tf_op jit(solution)/shard_map/ppermute | solution.py:71
  149.6 8.1 %collective-permute-start.18 = (f32[2,128,128]{2,1,0:T(8,128)S(1)}, f32[2,128,128]{2,1,0:T(8,128)S(1)}, u32[]{:S(2)}, u32[]{:S(2)}) collective-permute-start(f32[2,128,128]{2,1,0:T(8,128)S(1)} %get-tuple-element.35), channel_id=1, source_target_pairs={{32,64},{64,32},{96,128},{128,96},{160,192},{192,160},{33,65},{65,... | collective-permute-start | bytes 393224 | tf_op jit(solution)/shard_map/ppermute | solution.py:71
  158.4 0.9 copy-start
  159.3 4.8 %collective-permute-start.19 = (f32[256,256]{1,0:T(8,128)S(1)}, f32[256,256]{1,0:T(8,128)S(1)}, u32[]{:S(2)}, u32[]{:S(2)}) collective-permute-start(f32[256,256]{1,0:T(8,128)S(1)} %relay.1.refs_2_), channel_id=1, source_target_pairs={{0,1},{1,0},{2,3},{3,2},{4,5},{5,4},{6,7},{7,6},{8,9},{9,8},{10,11... | collective-permute-start | bytes 786440 | tf_op jit(solution)/shard_map/ppermute | solution.py:71

commit v5 on v4

--- a/solution.py
+++ b/solution.py
@@ -276,7 +276,10 @@
 
 
 def add_into_ways(a, b, ways):
-    return (a + b).reshape(ways, -1, a.shape[-1])
+    def kernel(a, b, out):
+        out[...] = a[...] + b[...]
+
+    return call(kernel, shape(*a.shape), (a, b), "add", scalars=0).reshape(ways, -1, a.shape[-1])
 
 
 def spread_over(keep, give):
@@ -384,20 +387,22 @@
     tags = jnp.pad(tags, ((0, 0), (0, 7), (0, tile.shape[2] - tags.shape[2])))
     tags = jnp.broadcast_to(tags, (2,) + tags.shape[1:])
     parts = widen(ids, jnp.concatenate([tile, tags], axis=1))
-    tall = side + side // 2
-    spots = jnp.stack([v[0, tall::8, : 2 * rows * cols] for v in parts]).astype(jnp.int32)
     for step in range(ITERS):
         mid, keep, give, new_probe, sib, cross = update(
             step > 0, ids, starts, parts, amplitude, probe, own, other, table
         )
         if step > 0:
             probe = new_probe
-        bright = light(ids, spots, probe)
         last = step == ITERS - 1
         part = spread_over(keep, give)
         ways, deep = part.shape[0], lax.axis_size("z")
         if last:
             cross = hold(cross, part)
+        else:
+            tall, width = side + side // 2, 2 * rows * cols
+            spots = (parts[0], parts[1], hold(parts[2], part))
+            spots = jnp.stack([v[0, tall::8, :width] for v in spots]).astype(jnp.int32)
+        bright = light(ids, spots, probe)
         near, centre, far = split(ids, sib, mid, cross, (bright,))
         part = lax.all_to_all(part, PLANE, 0, 0)
         part = sum_and_repeat(part, deep, () if last else (centre,))

time: 167 us -> 165 us (0.988)
  other arithmetic: 5.05 us -> 2.62 us
    ppermute x20, waiting for transfers between devices: 32.2 us -> 34.7 us  [pair_swap(): return lax.ppermute(value, axis, pairs)]
    add x2 -> x0, other arithmetic: 2.43 us -> none  [add_into_ways(): return (a + b).reshape(ways, -1, a.shape[-1])]
    all_to_all x2, waiting for transfers between devices: 4.79 us -> 2.39 us  [on_device(): part = lax.all_to_all(part, PLANE, 0, 0)]
    pallas_call x14 -> x16, Pallas kernels: 11.6 us -> 13.1 us  [call(): pl.pallas_call(body, out_shape=out_shape, in_specs=[ANY] * waits + [SMEM]...]
  transfers between devices with their start and end apart: 26 -> 26, of which waited for: 13 -> 14; matrix products, arithmetic and copies ran while one was open for 3% -> 2% of each run, Pallas kernels for 5% -> 5%
where the time goes in v5:
time: 165 us; the launch traced here: 164 us
  starting transfers between devices  84.5 us (51%)
  waiting for transfers between devices  42.2 us (26%)
  Pallas kernels  28.4 us (17%)
  local copies, waits for them, and re-layouts  5.22 us (3%)
  other arithmetic  2.62 us (2%)
    ppermute x20, starting transfers between devices, pair_swap(): return lax.ppermute(value, axis, pairs)  47.6 us
    ppermute x20, waiting for transfers between devices, pair_swap(): return lax.ppermute(value, axis, pairs)  34.7 us
    pallas_call x2, Pallas kernels, update(): pl.pallas_call(lambda *refs: update_kernel(renew, *refs), out_shape=(stri...  15.3 us
    all_to_all x2, starting transfers between devices, on_device(): part = lax.all_to_all(part, PLANE, 0, 0)  14.2 us
    pallas_call x16, Pallas kernels, call(): pl.pallas_call(body, out_shape=out_shape, in_specs=[ANY] * waits + [SMEM]...  13.1 us
    all_to_all x2, starting transfers between devices, on_device(): part = lax.all_to_all(part, 'z', 0, 0)  12.7 us
    all_to_all x2, starting transfers between devices, on_device(): own = lax.all_to_all(part, PLANE, 0, 0).reshape(side, side)  9.97 us
    all_to_all x2, waiting for transfers between devices, on_device(): part = lax.all_to_all(part, 'z', 0, 0)  5.12 us
  transfers between devices with their start and end apart: 26, of which 14 were waited for; matrix products, arithmetic and copies ran while one was open for 2% of the time, Pallas kernels for 5%

profile of v5, /device:TPU:3, one launch (start us, length us, event | category | flops | bytes accessed | tf_op | source)
XLA Modules:
  0.0 163.9 jit_solution(9103109400739617479)
XLA Ops:
  0.7 0.7 copy-done.14
  1.5 0.9 pad_maximum_fusion.refs_2_
  2.4 3.2 %collective-permute-start.1 = (f32[2,136,128]{2,1,0:T(8,128)S(1)}, f32[2,136,128]{2,1,0:T(8,128)S(1)}, u32[]{:S(2)}, u32[]{:S(2)}) collective-permute-start(f32[2,136,128]{2,1,0:T(8,128)S(1)} %pad_maximum_fusion.refs_2_), channel_id=1, source_target_pairs={{32,64},{64,32},{96,128},{128,96},{160,192},{192,160},{33,65},{65,... | collective-permute-start | bytes 417800 | tf_op jit(solution)/shard_map/ppermute | solution.py:71
  5.6 1.2 collective-permute-start
  6.9 2.9 %collective-permute-done.1.refs_3_ = f32[2,136,128]{2,1,0:T(8,128)S(1)} collective-permute-done((f32[2,136,128]{2,1,0:T(8,128)S(1)}, f32[2,136,128]{2,1,0:T(8,128)S(1)}, u32[]{:S(2)}, u32[]{:S(2)}) %collective-permute-start.1) | collective-permute-done | bytes 139296 | tf_op jit(solution)/shard_map/ppermute | solution.py:71
  9.7 4.0 %collective-permute-done.refs_1_ = f32[2,136,128]{2,1,0:T(8,128)S(1)} collective-permute-done((f32[2,136,128]{2,1,0:T(8,128)S(1)}, f32[2,136,128]{2,1,0:T(8,128)S(1)}, u32[]{:S(2)}, u32[]{:S(2)}) %collective-permute-start) | collective-permute-done | bytes 139296 | tf_op jit(solution)/shard_map/ppermute | solution.py:71
  13.8 0.6 stack.22.refs_5_
  14.4 5.3 %collective-permute-start.3 = (f32[2,408,128]{2,1,0:T(8,128)S(1)}, f32[2,408,128]{2,1,0:T(8,128)S(1)}, u32[]{:S(2)}, u32[]{:S(2)}) collective-permute-start(f32[2,408,128]{2,1,0:T(8,128)S(1)} %stack.22.refs_5_), channel_id=1, source_target_pairs={{1,2},{2,1},{3,4},{4,3},{5,6},{6,5},{7,8},{8,7},{9,10},{10,9},{11,... | collective-permute-start | bytes 1253384 | tf_op jit(solution)/shard_map/ppermute | solution.py:71
  19.7 0.1 collective-permute-start.2
  19.8 1.5 fusion.1.refs_7_
  21.4 7.8 %collective-permute-done.3.refs_6_.refs_0_ = f32[2,408,128]{2,1,0:T(8,128)S(1)} collective-permute-done((f32[2,408,128]{2,1,0:T(8,128)S(1)}, f32[2,408,128]{2,1,0:T(8,128)S(1)}, u32[]{:S(2)}, u32[]{:S(2)}) %collective-permute-start.3) | collective-permute-done | bytes 417824 | tf_op jit(solution)/shard_map/ppermute | solution.py:71
  29.2 7.9 %update.2 = (f32[2,384,128]{2,1,0:T(8,128)S(1)}, f32[256,256]{1,0:T(8,128)S(1)}, f32[256,256]{1,0:T(8,128)S(1)}, f32[8,128]{1,0:T(8,128)}, f32[2,384,128]{2,1,0:T(8,128)}, /*index=5*/f32[2,384,128]{2,1,0:T(8,128)}) custom-call(s32[2]{0:T(128)S(1)} %pad_add_fusion.refs_0_.refs_1_, s32[4,2]{1,0:T(4,128)S(1)} %bitcast.18, f32[256,256]{1,0:T(8,128)S(1)} %copy-done.4, ...), custom_call_target="tpu_custom_call" | custom-call | flops 4294967296 | tf_op jit(solution)/shard_map/update/pallas_call | solution.py:213
  37.1 0.1 collective-permute-start.4
  37.2 0.5 collective-permute-start.5
  37.7 5.8 %collective-permute-start.6 = (f32[2,384,128]{2,1,0:T(8,128)}, f32[2,384,128]{2,1,0:T(8,128)S(1)}, u32[]{:S(2)}, u32[]{:S(2)}) collective-permute-start(f32[2,384,128]{2,1,0:T(8,128)} %get-tuple-element.23), channel_id=1, source_target_pairs={{1,2},{2,1},{3,4},{4,3},{5,6},{6,5},{7,8},{8,7},{9,10},{10,9},{11,... | collective-permute-start | bytes 1179656 | tf_op jit(solution)/shard_map/ppermute | solution.py:71
  43.6 0.7 slice.9
  44.3 0.7 add.34
  45.0 5.7 %all-to-all-start = ((f32[16,16,256]{2,1,0:T(8,128)}), f32[16,16,256]{2,1,0:T(8,128)S(1)}, u32[]{:S(2)}, u32[]{:S(2)}) async-start(f32[16,16,256]{2,1,0:T(8,128)} %bitcast.5.refs_1_), calls=%async_computation | async-start | bytes 524288 | tf_op jit(solution)/shard_map/all_to_all | solution.py:407
  50.8 0.8 slice.11
  51.6 0.2 copy-done.7
  51.8 2.0 %light.2.refs_0_.refs_2_ = f32[128,128]{1,0:T(8,128)S(1)} custom-call(s32[2]{0:T(128)S(1)} %pad_add_fusion.refs_0_.refs_1_, s32[3,3,8]{2,1,0:T(4,128)S(1)} %maximum_convert_fusion.refs_1_, f32[2,256,256]{2,1,0:T(8,128)S(1)} %copy-done.7), custom_call_target="tpu_custom_call" | custom-call | flops 2000000000 | bytes 524584 | tf_op jit(solution)/shard_map/light/pallas_call | solution.py:48
  53.9 1.5 collective-permute-done.6.refs_4_
  55.4 0.6 split.2
  56.0 1.6 all-to-all-done.refs_1_
  57.6 0.7 sum_repeat.4.refs_0_
  58.2 7.3 %all-to-all-start.1 = ((f32[8,16,256]{2,1,0:T(8,128)}), f32[8,16,256]{2,1,0:T(8,128)S(1)}, u32[]{:S(2)}, u32[]{:S(2)}) async-start(f32[8,16,256]{2,1,0:T(8,128)} %sum_repeat.4.refs_0_), calls=%async_computation.1 | async-start | bytes 262144 | tf_op jit(solution)/shard_map/all_to_all | solution.py:411
  65.5 1.5 collective-permute-start.7
  67.0 3.2 %collective-permute-start.8 = (f32[2,128,128]{2,1,0:T(8,128)S(1)}, f32[2,128,128]{2,1,0:T(8,128)S(1)}, u32[]{:S(2)}, u32[]{:S(2)}) collective-permute-start(f32[2,128,128]{2,1,0:T(8,128)S(1)} %get-tuple-element.26), channel_id=1, source_target_pairs={{32,64},{64,32},{96,128},{128,96},{160,192},{192,160},{33,65},{65,... | collective-permute-start | bytes 393224 | tf_op jit(solution)/shard_map/ppermute | solution.py:71
  70.3 3.6 %collective-permute-done.8.refs_5_ = f32[2,128,128]{2,1,0:T(8,128)S(1)} collective-permute-done((f32[2,128,128]{2,1,0:T(8,128)S(1)}, f32[2,128,128]{2,1,0:T(8,128)S(1)}, u32[]{:S(2)}, u32[]{:S(2)}) %collective-permute-start.8) | collective-permute-done | bytes 131104 | tf_op jit(solution)/shard_map/ppermute | solution.py:71
  73.9 3.3 %collective-permute-start.11 = (f32[2,128,128]{2,1,0:T(8,128)S(1)}, f32[2,128,128]{2,1,0:T(8,128)S(1)}, u32[]{:S(2)}, u32[]{:S(2)}) collective-permute-start(f32[2,128,128]{2,1,0:T(8,128)S(1)} %renew.2.refs_0_.refs_3_), channel_id=1, source_target_pairs={{32,64},{64,32},{96,128},{128,96},{160,192},{192,160},{33,65},{65,... | collective-permute-start | bytes 393224 | tf_op jit(solution)/shard_map/ppermute | solution.py:71
  77.2 1.1 collective-permute-start.10
  78.3 0.7 sum_repeat.5.refs_0_
  79.0 4.9 %all-to-all-start.2 = ((f32[16,16,256]{2,1,0:T(8,128)}), f32[16,16,256]{2,1,0:T(8,128)S(1)}, u32[]{:S(2)}, u32[]{:S(2)}) async-start(f32[16,16,256]{2,1,0:T(8,128)} %sum_repeat.5.refs_0_), calls=%async_computation.2 | async-start | bytes 524288 | tf_op jit(solution)/shard_map/all_to_all | solution.py:417
  83.9 0.6 stack.23.refs_5_
  84.5 7.8 %collective-permute-start.13 = (f32[2,384,128]{2,1,0:T(8,128)S(1)}, f32[2,384,128]{2,1,0:T(8,128)S(1)}, u32[]{:S(2)}, u32[]{:S(2)}) collective-permute-start(f32[2,384,128]{2,1,0:T(8,128)S(1)} %stack.23.refs_5_), channel_id=1, source_target_pairs={{1,2},{2,1},{3,4},{4,3},{5,6},{6,5},{7,8},{8,7},{9,10},{10,9},{11,... | collective-permute-start | bytes 1179656 | tf_op jit(solution)/shard_map/ppermute | solution.py:71
  92.3 0.1 collective-permute-start.12
  92.4 1.9 %collective-permute-start.9 = (f32[256,256]{1,0:T(8,128)S(1)}, f32[256,256]{1,0:T(8,128)S(1)}, u32[]{:S(2)}, u32[]{:S(2)}) collective-permute-start(f32[256,256]{1,0:T(8,128)S(1)} %bitcast.15), channel_id=1, source_target_pairs={{0,1},{1,0},{2,3},{3,2},{4,5},{5,4},{6,7},{7,6},{8,9},{9,8},{10,11... | collective-permute-start | bytes 786440 | tf_op jit(solution)/shard_map/ppermute | solution.py:71
  94.3 6.0 %collective-permute-done.13.refs_6_ = f32[2,384,128]{2,1,0:T(8,128)S(1)} collective-permute-done((f32[2,384,128]{2,1,0:T(8,128)S(1)}, f32[2,384,128]{2,1,0:T(8,128)S(1)}, u32[]{:S(2)}, u32[]{:S(2)}) %collective-permute-start.13) | collective-permute-done | bytes 393248 | tf_op jit(solution)/shard_map/ppermute | solution.py:71
  100.3 0.7 copy-done.8
  101.0 1.0 copy-done.9
  102.0 7.4 %update.3 = (f32[2,384,128]{2,1,0:T(8,128)S(1)}, f32[256,256]{1,0:T(8,128)S(1)}, f32[256,256]{1,0:T(8,128)S(1)}, f32[2,256,256]{2,1,0:T(8,128)S(1)}, f32[2,384,1...) custom-call(s32[2]{0:T(128)S(1)} %pad_add_fusion.refs_0_.refs_1_, ...), custom_call_target="tpu_custom_call", output_to_operand_aliasing={{0}: (5, {}), {1}: (2, {}), {2}: (3, {}), {4}: (4, {}), {5}... | custom-call | flops 4294967296 | tf_op jit(solution)/shard_map/update/pallas_call | solution.py:213
  109.6 1.5 collective-permute-done.15.refs_1_
  111.1 0.7 add.35
  111.9 8.4 %all-to-all-start.3 = ((f32[16,16,256]{2,1,0:T(8,128)}), f32[16,16,256]{2,1,0:T(8,128)S(1)}, u32[]{:S(2)}, u32[]{:S(2)}) async-start(f32[16,16,256]{2,1,0:T(8,128)} %bitcast.7.refs_1_), calls=%async_computation.3 | async-start | bytes 524288 | tf_op jit(solution)/shard_map/all_to_all | solution.py:407
  120.3 1.0 collective-permute-start.14
  121.3 4.5 %collective-permute-start.16 = (f32[2,384,128]{2,1,0:T(8,128)}, f32[2,384,128]{2,1,0:T(8,128)S(1)}, u32[]{:S(2)}, u32[]{:S(2)}) collective-permute-start(f32[2,384,128]{2,1,0:T(8,128)} %hold.3), channel_id=1, source_target_pairs={{1,2},{2,1},{3,4},{4,3},{5,6},{6,5},{7,8},{8,7},{9,10},{10,9},{11,... | collective-permute-start | bytes 1179656 | tf_op jit(solution)/shard_map/ppermute | solution.py:71
  125.8 0.8 all-to-all-done.3.refs_0_
  126.6 0.7 sum_repeat.6
  127.3 5.5 %all-to-all-start.4 = ((f32[8,16,256]{2,1,0:T(8,128)}), f32[8,16,256]{2,1,0:T(8,128)S(1)}, u32[]{:S(2)}, u32[]{:S(2)}) async-start(f32[8,16,256]{2,1,0:T(8,128)} %sum_repeat.6), calls=%async_computation.4 | async-start | bytes 262144 | tf_op jit(solution)/shard_map/all_to_all | solution.py:411
  132.7 2.0 %light.3.refs_0_.refs_1_ = f32[128,128]{1,0:T(8,128)S(1)} custom-call(s32[2]{0:T(128)S(1)} %pad_add_fusion.refs_0_.refs_1_, s32[3,3,8]{2,1,0:T(4,128)S(1)} %maximum_convert_fusion.refs_1_, f32[2,256,256]{2,1,0:T(8,128)S(1)} %get-tuple-element.27.refs_2_.refs_1_), custom_call_target="tpu_custom_call" | custom-call | flops 2000000000 | bytes 524584 | tf_op jit(solution)/shard_map/light/pallas_call | solution.py:48
  134.8 0.3 collective-permute-done.16.refs_4_
  135.0 0.6 split.3
  135.7 5.1 %all-to-all-done.4.refs_1_ = f32[8,16,256]{2,1,0:T(8,128)S(1)} async-done(((f32[8,16,256]{2,1,0:T(8,128)}), f32[8,16,256]{2,1,0:T(8,128)S(1)}, u32[]{:S(2)}, u32[]{:S(2)}) %all-to-all-start.4) | async-done | bytes 131104 | tf_op jit(solution)/shard_map/all_to_all | solution.py:411
  140.8 0.7 sum_repeat.7
  141.5 5.1 %all-to-all-start.5 = ((f32[16,16,256]{2,1,0:T(8,128)}), f32[16,16,256]{2,1,0:T(8,128)S(1)}, u32[]{:S(2)}, u32[]{:S(2)}) async-start(f32[16,16,256]{2,1,0:T(8,128)} %sum_repeat.7), calls=%async_computation.5 | async-start | bytes 524288 | tf_op jit(solution)/shard_map/all_to_all | solution.py:417
  146.6 1.2 collective-permute-start.17
  147.8 2.2 %collective-permute-start.18 = (f32[2,128,128]{2,1,0:T(8,128)S(1)}, f32[2,128,128]{2,1,0:T(8,128)S(1)}, u32[]{:S(2)}, u32[]{:S(2)}) collective-permute-start(f32[2,128,128]{2,1,0:T(8,128)S(1)} %get-tuple-element.35), channel_id=1, source_target_pairs={{32,64},{64,32},{96,128},{128,96},{160,192},{192,160},{33,65},{65,... | collective-permute-start | bytes 393224 | tf_op jit(solution)/shard_map/ppermute | solution.py:71
  150.0 1.9 %collective-permute-done.17.refs_2_ = f32[2,128,128]{2,1,0:T(8,128)S(1)} collective-permute-done((f32[2,128,128]{2,1,0:T(8,128)S(1)}, f32[2,128,128]{2,1,0:T(8,128)S(1)}, u32[]{:S(2)}, u32[]{:S(2)}) %collective-permute-start.17) | collective-permute-done | bytes 131104 | tf_op jit(solution)/shard_map/ppermute | solution.py:71
  151.8 4.1 %collective-permute-done.18.refs_4_ = f32[2,128,128]{2,1,0:T(8,128)S(1)} collective-permute-done((f32[2,128,128]{2,1,0:T(8,128)S(1)}, f32[2,128,128]{2,1,0:T(8,128)S(1)}, u32[]{:S(2)}, u32[]{:S(2)}) %collective-permute-start.18) | collective-permute-done | bytes 131104 | tf_op jit(solution)/shard_map/ppermute | solution.py:71
  155.9 0.7 renew.3.refs_0_
  156.6 0.9 copy-done
  157.5 3.6 %collective-permute-start.19 = (f32[256,256]{1,0:T(8,128)S(1)}, f32[256,256]{1,0:T(8,128)S(1)}, u32[]{:S(2)}, u32[]{:S(2)}) collective-permute-start(f32[256,256]{1,0:T(8,128)S(1)} %relay.1.refs_2_), channel_id=1, source_target_pairs={{0,1},{1,0},{2,3},{3,2},{4,5},{5,4},{6,7},{7,6},{8,9},{9,8},{10,11... | collective-permute-start | bytes 786440 | tf_op jit(solution)/shard_map/ppermute | solution.py:71
  161.1 1.2 collective-permute-done.19.refs_3_
  162.3 1.6 finish.1
  (51 shorter events, 0.5 us)
Async XLA Ops:
  0.6 0.7 copy-start.14
  2.4 7.3 %collective-permute-start.1 = (f32[2,136,128]{2,1,0:T(8,128)S(1)}, f32[2,136,128]{2,1,0:T(8,128)S(1)}, u32[]{:S(2)}, u32[]{:S(2)}) collective-permute-start(f32[2,136,128]{2,1,0:T(8,128)S(1)} %pad_maximum_fusion.refs_2_), channel_id=1, source_target_pairs={{32,64},{64,32},{96,128},{128,96},{160,192},{192,160},{33,65},{65,... | collective-permute-start | bytes 417800 | tf_op jit(solution)/shard_map/ppermute | solution.py:71
  5.6 8.2 %collective-permute-start = (f32[2,136,128]{2,1,0:T(8,128)S(1)}, f32[2,136,128]{2,1,0:T(8,128)S(1)}, u32[]{:S(2)}, u32[]{:S(2)}) collective-permute-start(f32[2,136,128]{2,1,0:T(8,128)S(1)} %pad_maximum_fusion.refs_2_), channel_id=1, source_target_pairs={{0,32},{32,0},{64,96},{96,64},{128,160},{160,128},{192,224},{224,1... | collective-permute-start | bytes 417800 | tf_op jit(solution)/shard_map/ppermute | solution.py:71
  6.9 12.9 %copy-start.4 = (f32[256,256]{1,0:T(8,128)S(1)}, f32[256,256]{1,0:T(8,128)}, u32[]{:S(2)}) copy-start(f32[256,256]{1,0:T(8,128)} %refs_3_.1) | copy-start | bytes 786436
  14.4 14.8 %copy-start.6 = (f32[2,256,256]{2,1,0:T(8,128)S(1)}, f32[2,256,256]{2,1,0:T(8,128)}, u32[]{:S(2)}) copy-start(f32[2,256,256]{2,1,0:T(8,128)} %refs_8_.3) | copy-start | bytes 1572868
  14.4 14.8 %copy-start.12 = (bf16[256,512]{1,0:T(8,128)(2,1)S(1)}, bf16[256,512]{1,0:T(8,128)(2,1)}, u32[]{:S(2)}) copy-start(bf16[256,512]{1,0:T(8,128)(2,1)} %constant.18.clone.refs_9_) | copy-start | bytes 786436
  14.4 14.8 %collective-permute-start.3 = (f32[2,408,128]{2,1,0:T(8,128)S(1)}, f32[2,408,128]{2,1,0:T(8,128)S(1)}, u32[]{:S(2)}, u32[]{:S(2)}) collective-permute-start(f32[2,408,128]{2,1,0:T(8,128)S(1)} %stack.22.refs_5_), channel_id=1, source_target_pairs={{1,2},{2,1},{3,4},{4,3},{5,6},{6,5},{7,8},{8,7},{9,10},{10,9},{11,... | collective-permute-start | bytes 1253384 | tf_op jit(solution)/shard_map/ppermute | solution.py:71
  19.7 9.4 %collective-permute-start.2 = (f32[2,408,128]{2,1,0:T(8,128)S(1)}, f32[2,408,128]{2,1,0:T(8,128)S(1)}, u32[]{:S(2)}, u32[]{:S(2)}) collective-permute-start(f32[2,408,128]{2,1,0:T(8,128)S(1)} %stack.22.refs_5_), channel_id=1, source_target_pairs={{0,1},{1,0},{2,3},{3,2},{4,5},{5,4},{6,7},{7,6},{8,9},{9,8},{10,11... | collective-permute-start | bytes 1253384 | tf_op jit(solution)/shard_map/ppermute | solution.py:71
  29.2 7.9 %copy-start.2 = (f32[2,408,128]{2,1,0:T(8,128)}, f32[2,408,128]{2,1,0:T(8,128)S(1)}, u32[]{:S(2)}) copy-start(f32[2,408,128]{2,1,0:T(8,128)S(1)} %collective-permute-done.3.refs_6_.refs_0_) | copy-start | bytes 1253380
  29.2 7.9 %copy-start.5 = (f32[2,408,128]{2,1,0:T(8,128)}, f32[2,408,128]{2,1,0:T(8,128)S(1)}, u32[]{:S(2)}) copy-start(f32[2,408,128]{2,1,0:T(8,128)S(1)} %collective-permute-done.2.refs_4_) | copy-start | bytes 1253380
  37.1 7.2 %collective-permute-start.4 = (f32[256,256]{1,0:T(8,128)S(1)}, f32[256,256]{1,0:T(8,128)S(1)}, u32[]{:S(2)}, u32[]{:S(2)}) collective-permute-start(f32[256,256]{1,0:T(8,128)S(1)} %get-tuple-element.20), channel_id=1, source_target_pairs={{0,1},{1,0},{2,3},{3,2},{4,5},{5,4},{6,7},{7,6},{8,9},{9,8},{10,11... | collective-permute-start | bytes 786440 | tf_op jit(solution)/shard_map/ppermute | solution.py:71
  37.2 16.6 %collective-permute-start.5 = (f32[2,384,128]{2,1,0:T(8,128)}, f32[2,384,128]{2,1,0:T(8,128)S(1)}, u32[]{:S(2)}, u32[]{:S(2)}) collective-permute-start(f32[2,384,128]{2,1,0:T(8,128)} %get-tuple-element.22), channel_id=1, source_target_pairs={{0,1},{1,0},{2,3},{3,2},{4,5},{5,4},{6,7},{7,6},{8,9},{9,8},{10,11... | collective-permute-start | bytes 1179656 | tf_op jit(solution)/shard_map/ppermute | solution.py:71
  37.7 17.6 %collective-permute-start.6 = (f32[2,384,128]{2,1,0:T(8,128)}, f32[2,384,128]{2,1,0:T(8,128)S(1)}, u32[]{:S(2)}, u32[]{:S(2)}) collective-permute-start(f32[2,384,128]{2,1,0:T(8,128)} %get-tuple-element.23), channel_id=1, source_target_pairs={{1,2},{2,1},{3,4},{4,3},{5,6},{6,5},{7,8},{8,7},{9,10},{10,9},{11,... | collective-permute-start | bytes 1179656 | tf_op jit(solution)/shard_map/ppermute | solution.py:71
  45.0 12.5 %all-to-all-start = ((f32[16,16,256]{2,1,0:T(8,128)}), f32[16,16,256]{2,1,0:T(8,128)S(1)}, u32[]{:S(2)}, u32[]{:S(2)}) async-start(f32[16,16,256]{2,1,0:T(8,128)} %bitcast.5.refs_1_), calls=%async_computation | async-start | bytes 524288 | tf_op jit(solution)/shard_map/all_to_all | solution.py:407
  50.8 1.1 copy-start.7
  58.2 15.7 %copy-start.1 = (f32[2,128,128]{2,1,0:T(8,128)S(1)}, f32[2,128,128]{2,1,0:T(8,128)}, u32[]{:S(2)}) copy-start(f32[2,128,128]{2,1,0:T(8,128)} %refs_1_.1) | copy-start | bytes 393220
  58.2 20.0 %all-to-all-start.1 = ((f32[8,16,256]{2,1,0:T(8,128)}), f32[8,16,256]{2,1,0:T(8,128)S(1)}, u32[]{:S(2)}, u32[]{:S(2)}) async-start(f32[8,16,256]{2,1,0:T(8,128)} %sum_repeat.4.refs_0_), calls=%async_computation.1 | async-start | bytes 262144 | tf_op jit(solution)/shard_map/all_to_all | solution.py:411
  65.5 4.7 %collective-permute-start.7 = (f32[2,128,128]{2,1,0:T(8,128)S(1)}, f32[2,128,128]{2,1,0:T(8,128)S(1)}, u32[]{:S(2)}, u32[]{:S(2)}) collective-permute-start(f32[2,128,128]{2,1,0:T(8,128)S(1)} %get-tuple-element.25), channel_id=1, source_target_pairs={{0,32},{32,0},{64,96},{96,64},{128,160},{160,128},{192,224},{224,1... | collective-permute-start | bytes 393224 | tf_op jit(solution)/shard_map/ppermute | solution.py:71
  67.0 6.9 %collective-permute-start.8 = (f32[2,128,128]{2,1,0:T(8,128)S(1)}, f32[2,128,128]{2,1,0:T(8,128)S(1)}, u32[]{:S(2)}, u32[]{:S(2)}) collective-permute-start(f32[2,128,128]{2,1,0:T(8,128)S(1)} %get-tuple-element.26), channel_id=1, source_target_pairs={{32,64},{64,32},{96,128},{128,96},{160,192},{192,160},{33,65},{65,... | collective-permute-start | bytes 393224 | tf_op jit(solution)/shard_map/ppermute | solution.py:71
  73.9 10.0 %collective-permute-start.11 = (f32[2,128,128]{2,1,0:T(8,128)S(1)}, f32[2,128,128]{2,1,0:T(8,128)S(1)}, u32[]{:S(2)}, u32[]{:S(2)}) collective-permute-start(f32[2,128,128]{2,1,0:T(8,128)S(1)} %renew.2.refs_0_.refs_3_), channel_id=1, source_target_pairs={{32,64},{64,32},{96,128},{128,96},{160,192},{192,160},{33,65},{65,... | collective-permute-start | bytes 393224 | tf_op jit(solution)/shard_map/ppermute | solution.py:71
  77.2 6.7 %collective-permute-start.10 = (f32[2,128,128]{2,1,0:T(8,128)S(1)}, f32[2,128,128]{2,1,0:T(8,128)S(1)}, u32[]{:S(2)}, u32[]{:S(2)}) collective-permute-start(f32[2,128,128]{2,1,0:T(8,128)S(1)} %renew.2.refs_0_.refs_3_), channel_id=1, source_target_pairs={{0,32},{32,0},{64,96},{96,64},{128,160},{160,128},{192,224},{224,1... | collective-permute-start | bytes 393224 | tf_op jit(solution)/shard_map/ppermute | solution.py:71
  79.0 13.4 %all-to-all-start.2 = ((f32[16,16,256]{2,1,0:T(8,128)}), f32[16,16,256]{2,1,0:T(8,128)S(1)}, u32[]{:S(2)}, u32[]{:S(2)}) async-start(f32[16,16,256]{2,1,0:T(8,128)} %sum_repeat.5.refs_0_), calls=%async_computation.2 | async-start | bytes 524288 | tf_op jit(solution)/shard_map/all_to_all | solution.py:417
  83.9 17.1 %copy-start.13 = (bf16[256,512]{1,0:T(8,128)(2,1)S(1)}, bf16[256,512]{1,0:T(8,128)(2,1)}, u32[]{:S(2)}) copy-start(bf16[256,512]{1,0:T(8,128)(2,1)} %constant.18.clone.refs_9_) | copy-start | bytes 786436
  84.5 15.8 %collective-permute-start.13 = (f32[2,384,128]{2,1,0:T(8,128)S(1)}, f32[2,384,128]{2,1,0:T(8,128)S(1)}, u32[]{:S(2)}, u32[]{:S(2)}) collective-permute-start(f32[2,384,128]{2,1,0:T(8,128)S(1)} %stack.23.refs_5_), channel_id=1, source_target_pairs={{1,2},{2,1},{3,4},{4,3},{5,6},{6,5},{7,8},{8,7},{9,10},{10,9},{11,... | collective-permute-start | bytes 1179656 | tf_op jit(solution)/shard_map/ppermute | solution.py:71
  92.3 8.0 %collective-permute-start.12 = (f32[2,384,128]{2,1,0:T(8,128)S(1)}, f32[2,384,128]{2,1,0:T(8,128)S(1)}, u32[]{:S(2)}, u32[]{:S(2)}) collective-permute-start(f32[2,384,128]{2,1,0:T(8,128)S(1)} %stack.23.refs_5_), channel_id=1, source_target_pairs={{0,1},{1,0},{2,3},{3,2},{4,5},{5,4},{6,7},{7,6},{8,9},{9,8},{10,11... | collective-permute-start | bytes 1179656 | tf_op jit(solution)/shard_map/ppermute | solution.py:71
  92.4 8.6 %collective-permute-start.9 = (f32[256,256]{1,0:T(8,128)S(1)}, f32[256,256]{1,0:T(8,128)S(1)}, u32[]{:S(2)}, u32[]{:S(2)}) collective-permute-start(f32[256,256]{1,0:T(8,128)S(1)} %bitcast.15), channel_id=1, source_target_pairs={{0,1},{1,0},{2,3},{3,2},{4,5},{5,4},{6,7},{7,6},{8,9},{9,8},{10,11... | collective-permute-start | bytes 786440 | tf_op jit(solution)/shard_map/ppermute | solution.py:71
  100.3 0.7 copy-start.8
  101.0 1.0 copy-start.9
  109.5 2.4 %copy-start.3 = (f32[2,384,128]{2,1,0:T(8,128)}, f32[2,384,128]{2,1,0:T(8,128)S(1)}, u32[]{:S(2)}) copy-start(f32[2,384,128]{2,1,0:T(8,128)S(1)} %get-tuple-element.30.refs_0_) | copy-start | bytes 1179652
  109.5 2.4 %copy-start.10 = (f32[2,384,128]{2,1,0:T(8,128)}, f32[2,384,128]{2,1,0:T(8,128)S(1)}, u32[]{:S(2)}) copy-start(f32[2,384,128]{2,1,0:T(8,128)S(1)} %get-tuple-element.29) | copy-start | bytes 1179652
  109.5 1.6 collective-permute-start.15
  111.8 8.4 %copy-start.11 = (f32[2,384,128]{2,1,0:T(8,128)S(1)}, f32[2,384,128]{2,1,0:T(8,128)}, u32[]{:S(2)}) copy-start(f32[2,384,128]{2,1,0:T(8,128)} %copy-done.10) | copy-start | bytes 1179652
  111.9 14.8 %all-to-all-start.3 = ((f32[16,16,256]{2,1,0:T(8,128)}), f32[16,16,256]{2,1,0:T(8,128)S(1)}, u32[]{:S(2)}, u32[]{:S(2)}) async-start(f32[16,16,256]{2,1,0:T(8,128)} %bitcast.7.refs_1_), calls=%async_computation.3 | async-start | bytes 524288 | tf_op jit(solution)/shard_map/all_to_all | solution.py:407
  120.3 14.5 %collective-permute-start.14 = (f32[2,384,128]{2,1,0:T(8,128)S(1)}, f32[2,384,128]{2,1,0:T(8,128)S(1)}, u32[]{:S(2)}, u32[]{:S(2)}) collective-permute-start(f32[2,384,128]{2,1,0:T(8,128)S(1)} %copy-done.11), channel_id=1, source_target_pairs={{0,1},{1,0},{2,3},{3,2},{4,5},{5,4},{6,7},{7,6},{8,9},{9,8},{10,11... | collective-permute-start | bytes 1179656 | tf_op jit(solution)/shard_map/ppermute | solution.py:71
  121.3 13.7 %collective-permute-start.16 = (f32[2,384,128]{2,1,0:T(8,128)}, f32[2,384,128]{2,1,0:T(8,128)S(1)}, u32[]{:S(2)}, u32[]{:S(2)}) collective-permute-start(f32[2,384,128]{2,1,0:T(8,128)} %hold.3), channel_id=1, source_target_pairs={{1,2},{2,1},{3,4},{4,3},{5,6},{6,5},{7,8},{8,7},{9,10},{10,9},{11,... | collective-permute-start | bytes 1179656 | tf_op jit(solution)/shard_map/ppermute | solution.py:71
  127.3 13.5 %all-to-all-start.4 = ((f32[8,16,256]{2,1,0:T(8,128)}), f32[8,16,256]{2,1,0:T(8,128)S(1)}, u32[]{:S(2)}, u32[]{:S(2)}) async-start(f32[8,16,256]{2,1,0:T(8,128)} %sum_repeat.6), calls=%async_computation.4 | async-start | bytes 262144 | tf_op jit(solution)/shard_map/all_to_all | solution.py:411
  141.5 15.1 %all-to-all-start.5 = ((f32[16,16,256]{2,1,0:T(8,128)}), f32[16,16,256]{2,1,0:T(8,128)S(1)}, u32[]{:S(2)}, u32[]{:S(2)}) async-start(f32[16,16,256]{2,1,0:T(8,128)} %sum_repeat.7), calls=%async_computation.5 | async-start | bytes 524288 | tf_op jit(solution)/shard_map/all_to_all | solution.py:417
  146.6 5.2 %collective-permute-start.17 = (f32[2,128,128]{2,1,0:T(8,128)S(1)}, f32[2,128,128]{2,1,0:T(8,128)S(1)}, u32[]{:S(2)}, u32[]{:S(2)}) collective-permute-start(f32[2,128,128]{2,1,0:T(8,128)S(1)} %get-tuple-element.33), channel_id=1, source_target_pairs={{0,32},{32,0},{64,96},{96,64},{128,160},{160,128},{192,224},{224,1... | collective-permute-start | bytes 393224 | tf_op jit(solution)/shard_map/ppermute | solution.py:71
  147.8 8.1 %collective-permute-start.18 = (f32[2,128,128]{2,1,0:T(8,128)S(1)}, f32[2,128,128]{2,1,0:T(8,128)S(1)}, u32[]{:S(2)}, u32[]{:S(2)}) collective-permute-start(f32[2,128,128]{2,1,0:T(8,128)S(1)} %get-tuple-element.35), channel_id=1, source_target_pairs={{32,64},{64,32},{96,128},{128,96},{160,192},{192,160},{33,65},{65,... | collective-permute-start | bytes 393224 | tf_op jit(solution)/shard_map/ppermute | solution.py:71
  156.6 0.9 copy-start
  157.5 4.8 %collective-permute-start.19 = (f32[256,256]{1,0:T(8,128)S(1)}, f32[256,256]{1,0:T(8,128)S(1)}, u32[]{:S(2)}, u32[]{:S(2)}) collective-permute-start(f32[256,256]{1,0:T(8,128)S(1)} %relay.1.refs_2_), channel_id=1, source_target_pairs={{0,1},{1,0},{2,3},{3,2},{4,5},{5,4},{6,7},{7,6},{8,9},{9,8},{10,11... | collective-permute-start | bytes 786440 | tf_op jit(solution)/shard_map/ppermute | solution.py:71

commit v6 on v5

--- a/solution.py
+++ b/solution.py
@@ -405,11 +405,11 @@
         bright = light(ids, spots, probe)
         near, centre, far = split(ids, sib, mid, cross, (bright,))
         part = lax.all_to_all(part, PLANE, 0, 0)
-        part = sum_and_repeat(part, deep, () if last else (centre,))
+        part = sum_and_repeat(part, deep, () if last else (near,))
         if not last:
             tile = renew(tile, bright, near, centre, far, (part,))
         part = lax.all_to_all(part, "z", 0, 0)
-        part = sum_and_repeat(part, ways, (centre,) if last else (tile,))
+        part = sum_and_repeat(part, ways, (near,) if last else (tile,))
         if last:
             tile = renew(tile, bright, near, centre, far, ())
         else:

time: 165 us -> 170 us (1.030)
  waiting for transfers between devices: 42.2 us -> 45.1 us
    ppermute x20, waiting for transfers between devices: 34.7 us -> 38.4 us  [pair_swap(): return lax.ppermute(value, axis, pairs)]
  transfers between devices with their start and end apart: 26 -> 26, of which waited for: 14 -> 15; matrix products, arithmetic and copies ran while one was open for 2% -> 2% of each run, Pallas kernels for 5% -> 5%
where the time goes in v6:
time: 170 us; the launch traced here: 168 us
  starting transfers between devices  85.4 us (50%)
  waiting for transfers between devices  45.1 us (27%)
  Pallas kernels  28.4 us (17%)
  local copies, waits for them, and re-layouts  5.22 us (3%)
  other arithmetic  2.62 us (2%)
    ppermute x20, starting transfers between devices, pair_swap(): return lax.ppermute(value, axis, pairs)  48.2 us
    ppermute x20, waiting for transfers between devices, pair_swap(): return lax.ppermute(value, axis, pairs)  38.4 us
    pallas_call x2, Pallas kernels, update(): pl.pallas_call(lambda *refs: update_kernel(renew, *refs), out_shape=(stri...  15.4 us
    all_to_all x2, starting transfers between devices, on_device(): part = lax.all_to_all(part, 'z', 0, 0)  13.8 us
    all_to_all x2, starting transfers between devices, on_device(): part = lax.all_to_all(part, PLANE, 0, 0)  13.8 us
    pallas_call x16, Pallas kernels, call(): pl.pallas_call(body, out_shape=out_shape, in_specs=[ANY] * waits + [SMEM]...  13.1 us
    all_to_all x2, starting transfers between devices, on_device(): own = lax.all_to_all(part, PLANE, 0, 0).reshape(side, side)  9.61 us
    all_to_all x2, waiting for transfers between devices, on_device(): part = lax.all_to_all(part, 'z', 0, 0)  4.68 us
  transfers between devices with their start and end apart: 26, of which 15 were waited for; matrix products, arithmetic and copies ran while one was open for 2% of the time, Pallas kernels for 5%

profile of v6, /device:TPU:3, one launch (start us, length us, event | category | flops | bytes accessed | tf_op | source)
XLA Modules:
  0.0 167.8 jit_solution(9700568207292234720)
XLA Ops:
  0.7 0.7 copy-done.14
  1.5 0.9 pad_maximum_fusion.refs_2_
  2.4 3.2 %collective-permute-start.1 = (f32[2,136,128]{2,1,0:T(8,128)S(1)}, f32[2,136,128]{2,1,0:T(8,128)S(1)}, u32[]{:S(2)}, u32[]{:S(2)}) collective-permute-start(f32[2,136,128]{2,1,0:T(8,128)S(1)} %pad_maximum_fusion.refs_2_), channel_id=1, source_target_pairs={{32,64},{64,32},{96,128},{128,96},{160,192},{192,160},{33,65},{65,... | collective-permute-start | bytes 417800 | tf_op jit(solution)/shard_map/ppermute | solution.py:71
  5.6 1.2 collective-permute-start
  6.9 2.9 %collective-permute-done.1.refs_3_ = f32[2,136,128]{2,1,0:T(8,128)S(1)} collective-permute-done((f32[2,136,128]{2,1,0:T(8,128)S(1)}, f32[2,136,128]{2,1,0:T(8,128)S(1)}, u32[]{:S(2)}, u32[]{:S(2)}) %collective-permute-start.1) | collective-permute-done | bytes 139296 | tf_op jit(solution)/shard_map/ppermute | solution.py:71
  9.7 4.0 %collective-permute-done.refs_1_ = f32[2,136,128]{2,1,0:T(8,128)S(1)} collective-permute-done((f32[2,136,128]{2,1,0:T(8,128)S(1)}, f32[2,136,128]{2,1,0:T(8,128)S(1)}, u32[]{:S(2)}, u32[]{:S(2)}) %collective-permute-start) | collective-permute-done | bytes 139296 | tf_op jit(solution)/shard_map/ppermute | solution.py:71
  13.8 0.6 stack.22.refs_5_
  14.4 5.3 %collective-permute-start.3 = (f32[2,408,128]{2,1,0:T(8,128)S(1)}, f32[2,408,128]{2,1,0:T(8,128)S(1)}, u32[]{:S(2)}, u32[]{:S(2)}) collective-permute-start(f32[2,408,128]{2,1,0:T(8,128)S(1)} %stack.22.refs_5_), channel_id=1, source_target_pairs={{1,2},{2,1},{3,4},{4,3},{5,6},{6,5},{7,8},{8,7},{9,10},{10,9},{11,... | collective-permute-start | bytes 1253384 | tf_op jit(solution)/shard_map/ppermute | solution.py:71
  19.7 0.1 collective-permute-start.2
  19.8 1.5 fusion.1.refs_7_
  21.4 7.8 %collective-permute-done.3.refs_6_.refs_0_ = f32[2,408,128]{2,1,0:T(8,128)S(1)} collective-permute-done((f32[2,408,128]{2,1,0:T(8,128)S(1)}, f32[2,408,128]{2,1,0:T(8,128)S(1)}, u32[]{:S(2)}, u32[]{:S(2)}) %collective-permute-start.3) | collective-permute-done | bytes 417824 | tf_op jit(solution)/shard_map/ppermute | solution.py:71
  29.2 7.9 %update.2 = (f32[2,384,128]{2,1,0:T(8,128)S(1)}, f32[256,256]{1,0:T(8,128)S(1)}, f32[256,256]{1,0:T(8,128)S(1)}, f32[8,128]{1,0:T(8,128)}, f32[2,384,128]{2,1,0:T(8,128)}, /*index=5*/f32[2,384,128]{2,1,0:T(8,128)}) custom-call(s32[2]{0:T(128)S(1)} %pad_add_fusion.refs_0_.refs_1_, s32[4,2]{1,0:T(4,128)S(1)} %bitcast.18, f32[256,256]{1,0:T(8,128)S(1)} %copy-done.4, ...), custom_call_target="tpu_custom_call" | custom-call | flops 4294967296 | tf_op jit(solution)/shard_map/update/pallas_call | solution.py:213
  37.1 0.1 collective-permute-start.4
  37.2 0.5 collective-permute-start.5
  37.7 5.8 %collective-permute-start.6 = (f32[2,384,128]{2,1,0:T(8,128)}, f32[2,384,128]{2,1,0:T(8,128)S(1)}, u32[]{:S(2)}, u32[]{:S(2)}) collective-permute-start(f32[2,384,128]{2,1,0:T(8,128)} %get-tuple-element.23), channel_id=1, source_target_pairs={{1,2},{2,1},{3,4},{4,3},{5,6},{6,5},{7,8},{8,7},{9,10},{10,9},{11,... | collective-permute-start | bytes 1179656 | tf_op jit(solution)/shard_map/ppermute | solution.py:71
  43.6 0.7 slice.9
  44.3 0.7 add.34
  45.0 5.8 %all-to-all-start = ((f32[16,16,256]{2,1,0:T(8,128)}), f32[16,16,256]{2,1,0:T(8,128)S(1)}, u32[]{:S(2)}, u32[]{:S(2)}) async-start(f32[16,16,256]{2,1,0:T(8,128)} %bitcast.5.refs_1_), calls=%async_computation | async-start | bytes 524288 | tf_op jit(solution)/shard_map/all_to_all | solution.py:407
  50.8 0.8 slice.11
  51.6 0.2 copy-done.7
  51.9 2.0 %light.2.refs_0_.refs_2_ = f32[128,128]{1,0:T(8,128)S(1)} custom-call(s32[2]{0:T(128)S(1)} %pad_add_fusion.refs_0_.refs_1_, s32[3,3,8]{2,1,0:T(4,128)S(1)} %maximum_convert_fusion.refs_1_, f32[2,256,256]{2,1,0:T(8,128)S(1)} %copy-done.7), custom_call_target="tpu_custom_call" | custom-call | flops 2000000000 | bytes 524584 | tf_op jit(solution)/shard_map/light/pallas_call | solution.py:48
  53.9 1.4 collective-permute-done.6.refs_4_
  55.3 0.6 split.2
  55.9 0.4 collective-permute-start.7
  56.3 1.3 all-to-all-done.refs_1_
  57.6 2.3 %collective-permute-done.7.refs_0_.refs_3_ = f32[2,128,128]{2,1,0:T(8,128)S(1)} collective-permute-done((f32[2,128,128]{2,1,0:T(8,128)S(1)}, f32[2,128,128]{2,1,0:T(8,128)S(1)}, u32[]{:S(2)}, u32[]{:S(2)}) %collective-permute-start.7) | collective-permute-done | bytes 131104 | tf_op jit(solution)/shard_map/ppermute | solution.py:71
  59.8 0.7 sum_repeat.4.refs_0_
  60.5 8.4 %all-to-all-start.1 = ((f32[8,16,256]{2,1,0:T(8,128)}), f32[8,16,256]{2,1,0:T(8,128)S(1)}, u32[]{:S(2)}, u32[]{:S(2)}) async-start(f32[8,16,256]{2,1,0:T(8,128)} %sum_repeat.4.refs_0_), calls=%async_computation.1 | async-start | bytes 262144 | tf_op jit(solution)/shard_map/all_to_all | solution.py:411
  68.9 3.3 %collective-permute-start.8 = (f32[2,128,128]{2,1,0:T(8,128)S(1)}, f32[2,128,128]{2,1,0:T(8,128)S(1)}, u32[]{:S(2)}, u32[]{:S(2)}) collective-permute-start(f32[2,128,128]{2,1,0:T(8,128)S(1)} %get-tuple-element.26), channel_id=1, source_target_pairs={{32,64},{64,32},{96,128},{128,96},{160,192},{192,160},{33,65},{65,... | collective-permute-start | bytes 393224 | tf_op jit(solution)/shard_map/ppermute | solution.py:71
  72.2 5.0 %collective-permute-done.8.refs_5_ = f32[2,128,128]{2,1,0:T(8,128)S(1)} collective-permute-done((f32[2,128,128]{2,1,0:T(8,128)S(1)}, f32[2,128,128]{2,1,0:T(8,128)S(1)}, u32[]{:S(2)}, u32[]{:S(2)}) %collective-permute-start.8) | collective-permute-done | bytes 131104 | tf_op jit(solution)/shard_map/ppermute | solution.py:71
  77.2 2.1 %collective-permute-start.11 = (f32[2,128,128]{2,1,0:T(8,128)S(1)}, f32[2,128,128]{2,1,0:T(8,128)S(1)}, u32[]{:S(2)}, u32[]{:S(2)}) collective-permute-start(f32[2,128,128]{2,1,0:T(8,128)S(1)} %renew.2.refs_0_.refs_3_), channel_id=1, source_target_pairs={{32,64},{64,32},{96,128},{128,96},{160,192},{192,160},{33,65},{65,... | collective-permute-start | bytes 393224 | tf_op jit(solution)/shard_map/ppermute | solution.py:71
  79.4 2.2 %collective-permute-start.10 = (f32[2,128,128]{2,1,0:T(8,128)S(1)}, f32[2,128,128]{2,1,0:T(8,128)S(1)}, u32[]{:S(2)}, u32[]{:S(2)}) collective-permute-start(f32[2,128,128]{2,1,0:T(8,128)S(1)} %renew.2.refs_0_.refs_3_), channel_id=1, source_target_pairs={{0,32},{32,0},{64,96},{96,64},{128,160},{160,128},{192,224},{224,1... | collective-permute-start | bytes 393224 | tf_op jit(solution)/shard_map/ppermute | solution.py:71
  81.6 0.7 sum_repeat.5.refs_0_
  82.3 4.5 %all-to-all-start.2 = ((f32[16,16,256]{2,1,0:T(8,128)}), f32[16,16,256]{2,1,0:T(8,128)S(1)}, u32[]{:S(2)}, u32[]{:S(2)}) async-start(f32[16,16,256]{2,1,0:T(8,128)} %sum_repeat.5.refs_0_), calls=%async_computation.2 | async-start | bytes 524288 | tf_op jit(solution)/shard_map/all_to_all | solution.py:417
  86.9 1.3 collective-permute-done.10.refs_2_
  88.2 0.6 stack.23.refs_5_
  88.8 8.9 %collective-permute-start.13 = (f32[2,384,128]{2,1,0:T(8,128)S(1)}, f32[2,384,128]{2,1,0:T(8,128)S(1)}, u32[]{:S(2)}, u32[]{:S(2)}) collective-permute-start(f32[2,384,128]{2,1,0:T(8,128)S(1)} %stack.23.refs_5_), channel_id=1, source_target_pairs={{1,2},{2,1},{3,4},{4,3},{5,6},{6,5},{7,8},{8,7},{9,10},{10,9},{11,... | collective-permute-start | bytes 1179656 | tf_op jit(solution)/shard_map/ppermute | solution.py:71
  97.9 1.9 %collective-permute-start.9 = (f32[256,256]{1,0:T(8,128)S(1)}, f32[256,256]{1,0:T(8,128)S(1)}, u32[]{:S(2)}, u32[]{:S(2)}) collective-permute-start(f32[256,256]{1,0:T(8,128)S(1)} %bitcast.15), channel_id=1, source_target_pairs={{0,1},{1,0},{2,3},{3,2},{4,5},{5,4},{6,7},{7,6},{8,9},{9,8},{10,11... | collective-permute-start | bytes 786440 | tf_op jit(solution)/shard_map/ppermute | solution.py:71
  99.7 6.4 %collective-permute-done.13.refs_6_ = f32[2,384,128]{2,1,0:T(8,128)S(1)} collective-permute-done((f32[2,384,128]{2,1,0:T(8,128)S(1)}, f32[2,384,128]{2,1,0:T(8,128)S(1)}, u32[]{:S(2)}, u32[]{:S(2)}) %collective-permute-start.13) | collective-permute-done | bytes 393248 | tf_op jit(solution)/shard_map/ppermute | solution.py:71
  106.1 0.7 copy-done.8
  106.9 1.0 copy-done.9
  107.9 7.4 %update.3 = (f32[2,384,128]{2,1,0:T(8,128)S(1)}, f32[256,256]{1,0:T(8,128)S(1)}, f32[256,256]{1,0:T(8,128)S(1)}, f32[2,256,256]{2,1,0:T(8,128)S(1)}, f32[2,384,1...) custom-call(s32[2]{0:T(128)S(1)} %pad_add_fusion.refs_0_.refs_1_, ...), custom_call_target="tpu_custom_call", output_to_operand_aliasing={{0}: (5, {}), {1}: (2, {}), {2}: (3, {}), {4}: (4, {}), {5}... | custom-call | flops 4294967296 | tf_op jit(solution)/shard_map/update/pallas_call | solution.py:213
  115.4 1.5 collective-permute-done.15.refs_1_
  116.9 0.7 add.35
  117.7 8.0 %all-to-all-start.3 = ((f32[16,16,256]{2,1,0:T(8,128)}), f32[16,16,256]{2,1,0:T(8,128)S(1)}, u32[]{:S(2)}, u32[]{:S(2)}) async-start(f32[16,16,256]{2,1,0:T(8,128)} %bitcast.7.refs_1_), calls=%async_computation.3 | async-start | bytes 524288 | tf_op jit(solution)/shard_map/all_to_all | solution.py:407
  125.7 1.0 collective-permute-start.14
  126.7 4.5 %collective-permute-start.16 = (f32[2,384,128]{2,1,0:T(8,128)}, f32[2,384,128]{2,1,0:T(8,128)S(1)}, u32[]{:S(2)}, u32[]{:S(2)}) collective-permute-start(f32[2,384,128]{2,1,0:T(8,128)} %hold.3), channel_id=1, source_target_pairs={{1,2},{2,1},{3,4},{4,3},{5,6},{6,5},{7,8},{8,7},{9,10},{10,9},{11,... | collective-permute-start | bytes 1179656 | tf_op jit(solution)/shard_map/ppermute | solution.py:71
  131.3 0.8 all-to-all-done.3.refs_0_
  132.0 0.7 sum_repeat.6
  132.7 5.4 %all-to-all-start.4 = ((f32[8,16,256]{2,1,0:T(8,128)}), f32[8,16,256]{2,1,0:T(8,128)S(1)}, u32[]{:S(2)}, u32[]{:S(2)}) async-start(f32[8,16,256]{2,1,0:T(8,128)} %sum_repeat.6), calls=%async_computation.4 | async-start | bytes 262144 | tf_op jit(solution)/shard_map/all_to_all | solution.py:411
  138.1 2.0 %light.3.refs_0_.refs_1_ = f32[128,128]{1,0:T(8,128)S(1)} custom-call(s32[2]{0:T(128)S(1)} %pad_add_fusion.refs_0_.refs_1_, s32[3,3,8]{2,1,0:T(4,128)S(1)} %maximum_convert_fusion.refs_1_, f32[2,256,256]{2,1,0:T(8,128)S(1)} %get-tuple-element.27.refs_2_.refs_1_), custom_call_target="tpu_custom_call" | custom-call | flops 2000000000 | bytes 524584 | tf_op jit(solution)/shard_map/light/pallas_call | solution.py:48
  140.2 0.3 collective-permute-done.16.refs_4_
  140.5 0.6 split.3
  141.1 0.4 collective-permute-start.17
  141.5 4.7 %all-to-all-done.4.refs_1_ = f32[8,16,256]{2,1,0:T(8,128)S(1)} async-done(((f32[8,16,256]{2,1,0:T(8,128)}), f32[8,16,256]{2,1,0:T(8,128)S(1)}, u32[]{:S(2)}, u32[]{:S(2)}) %all-to-all-start.4) | async-done | bytes 131104 | tf_op jit(solution)/shard_map/all_to_all | solution.py:411
  146.2 0.7 sum_repeat.7
  146.9 5.1 %all-to-all-start.5 = ((f32[16,16,256]{2,1,0:T(8,128)}), f32[16,16,256]{2,1,0:T(8,128)S(1)}, u32[]{:S(2)}, u32[]{:S(2)}) async-start(f32[16,16,256]{2,1,0:T(8,128)} %sum_repeat.7), calls=%async_computation.5 | async-start | bytes 524288 | tf_op jit(solution)/shard_map/all_to_all | solution.py:417
  152.0 3.1 %collective-permute-start.18 = (f32[2,128,128]{2,1,0:T(8,128)S(1)}, f32[2,128,128]{2,1,0:T(8,128)S(1)}, u32[]{:S(2)}, u32[]{:S(2)}) collective-permute-start(f32[2,128,128]{2,1,0:T(8,128)S(1)} %get-tuple-element.35), channel_id=1, source_target_pairs={{32,64},{64,32},{96,128},{128,96},{160,192},{192,160},{33,65},{65,... | collective-permute-start | bytes 393224 | tf_op jit(solution)/shard_map/ppermute | solution.py:71
  155.0 4.3 %collective-permute-done.18.refs_4_ = f32[2,128,128]{2,1,0:T(8,128)S(1)} collective-permute-done((f32[2,128,128]{2,1,0:T(8,128)S(1)}, f32[2,128,128]{2,1,0:T(8,128)S(1)}, u32[]{:S(2)}, u32[]{:S(2)}) %collective-permute-start.18) | collective-permute-done | bytes 131104 | tf_op jit(solution)/shard_map/ppermute | solution.py:71
  159.3 0.7 renew.3.refs_0_
  160.0 0.9 copy-done
  161.0 4.1 %collective-permute-start.19 = (f32[256,256]{1,0:T(8,128)S(1)}, f32[256,256]{1,0:T(8,128)S(1)}, u32[]{:S(2)}, u32[]{:S(2)}) collective-permute-start(f32[256,256]{1,0:T(8,128)S(1)} %relay.1.refs_2_), channel_id=1, source_target_pairs={{0,1},{1,0},{2,3},{3,2},{4,5},{5,4},{6,7},{7,6},{8,9},{9,8},{10,11... | collective-permute-start | bytes 786440 | tf_op jit(solution)/shard_map/ppermute | solution.py:71
  165.0 1.2 collective-permute-done.19.refs_3_
  166.2 1.6 finish.1
  (51 shorter events, 0.6 us)
Async XLA Ops:
  0.6 0.7 copy-start.14
  2.4 7.3 %collective-permute-start.1 = (f32[2,136,128]{2,1,0:T(8,128)S(1)}, f32[2,136,128]{2,1,0:T(8,128)S(1)}, u32[]{:S(2)}, u32[]{:S(2)}) collective-permute-start(f32[2,136,128]{2,1,0:T(8,128)S(1)} %pad_maximum_fusion.refs_2_), channel_id=1, source_target_pairs={{32,64},{64,32},{96,128},{128,96},{160,192},{192,160},{33,65},{65,... | collective-permute-start | bytes 417800 | tf_op jit(solution)/shard_map/ppermute | solution.py:71
  5.6 8.2 %collective-permute-start = (f32[2,136,128]{2,1,0:T(8,128)S(1)}, f32[2,136,128]{2,1,0:T(8,128)S(1)}, u32[]{:S(2)}, u32[]{:S(2)}) collective-permute-start(f32[2,136,128]{2,1,0:T(8,128)S(1)} %pad_maximum_fusion.refs_2_), channel_id=1, source_target_pairs={{0,32},{32,0},{64,96},{96,64},{128,160},{160,128},{192,224},{224,1... | collective-permute-start | bytes 417800 | tf_op jit(solution)/shard_map/ppermute | solution.py:71
  6.9 12.9 %copy-start.4 = (f32[256,256]{1,0:T(8,128)S(1)}, f32[256,256]{1,0:T(8,128)}, u32[]{:S(2)}) copy-start(f32[256,256]{1,0:T(8,128)} %refs_3_.1) | copy-start | bytes 786436
  14.4 14.8 %copy-start.6 = (f32[2,256,256]{2,1,0:T(8,128)S(1)}, f32[2,256,256]{2,1,0:T(8,128)}, u32[]{:S(2)}) copy-start(f32[2,256,256]{2,1,0:T(8,128)} %refs_8_.3) | copy-start | bytes 1572868
  14.4 14.8 %copy-start.12 = (bf16[256,512]{1,0:T(8,128)(2,1)S(1)}, bf16[256,512]{1,0:T(8,128)(2,1)}, u32[]{:S(2)}) copy-start(bf16[256,512]{1,0:T(8,128)(2,1)} %constant.18.clone.refs_9_) | copy-start | bytes 786436
  14.4 14.8 %collective-permute-start.3 = (f32[2,408,128]{2,1,0:T(8,128)S(1)}, f32[2,408,128]{2,1,0:T(8,128)S(1)}, u32[]{:S(2)}, u32[]{:S(2)}) collective-permute-start(f32[2,408,128]{2,1,0:T(8,128)S(1)} %stack.22.refs_5_), channel_id=1, source_target_pairs={{1,2},{2,1},{3,4},{4,3},{5,6},{6,5},{7,8},{8,7},{9,10},{10,9},{11,... | collective-permute-start | bytes 1253384 | tf_op jit(solution)/shard_map/ppermute | solution.py:71
  19.7 9.4 %collective-permute-start.2 = (f32[2,408,128]{2,1,0:T(8,128)S(1)}, f32[2,408,128]{2,1,0:T(8,128)S(1)}, u32[]{:S(2)}, u32[]{:S(2)}) collective-permute-start(f32[2,408,128]{2,1,0:T(8,128)S(1)} %stack.22.refs_5_), channel_id=1, source_target_pairs={{0,1},{1,0},{2,3},{3,2},{4,5},{5,4},{6,7},{7,6},{8,9},{9,8},{10,11... | collective-permute-start | bytes 1253384 | tf_op jit(solution)/shard_map/ppermute | solution.py:71
  29.2 8.0 %copy-start.2 = (f32[2,408,128]{2,1,0:T(8,128)}, f32[2,408,128]{2,1,0:T(8,128)S(1)}, u32[]{:S(2)}) copy-start(f32[2,408,128]{2,1,0:T(8,128)S(1)} %collective-permute-done.3.refs_6_.refs_0_) | copy-start | bytes 1253380
  29.2 8.0 %copy-start.5 = (f32[2,408,128]{2,1,0:T(8,128)}, f32[2,408,128]{2,1,0:T(8,128)S(1)}, u32[]{:S(2)}) copy-start(f32[2,408,128]{2,1,0:T(8,128)S(1)} %collective-permute-done.2.refs_4_) | copy-start | bytes 1253380
  37.1 7.1 %collective-permute-start.4 = (f32[256,256]{1,0:T(8,128)S(1)}, f32[256,256]{1,0:T(8,128)S(1)}, u32[]{:S(2)}, u32[]{:S(2)}) collective-permute-start(f32[256,256]{1,0:T(8,128)S(1)} %get-tuple-element.20), channel_id=1, source_target_pairs={{0,1},{1,0},{2,3},{3,2},{4,5},{5,4},{6,7},{7,6},{8,9},{9,8},{10,11... | collective-permute-start | bytes 786440 | tf_op jit(solution)/shard_map/ppermute | solution.py:71
  37.2 16.6 %collective-permute-start.5 = (f32[2,384,128]{2,1,0:T(8,128)}, f32[2,384,128]{2,1,0:T(8,128)S(1)}, u32[]{:S(2)}, u32[]{:S(2)}) collective-permute-start(f32[2,384,128]{2,1,0:T(8,128)} %get-tuple-element.22), channel_id=1, source_target_pairs={{0,1},{1,0},{2,3},{3,2},{4,5},{5,4},{6,7},{7,6},{8,9},{9,8},{10,11... | collective-permute-start | bytes 1179656 | tf_op jit(solution)/shard_map/ppermute | solution.py:71
  37.7 17.6 %collective-permute-start.6 = (f32[2,384,128]{2,1,0:T(8,128)}, f32[2,384,128]{2,1,0:T(8,128)S(1)}, u32[]{:S(2)}, u32[]{:S(2)}) collective-permute-start(f32[2,384,128]{2,1,0:T(8,128)} %get-tuple-element.23), channel_id=1, source_target_pairs={{1,2},{2,1},{3,4},{4,3},{5,6},{6,5},{7,8},{8,7},{9,10},{10,9},{11,... | collective-permute-start | bytes 1179656 | tf_op jit(solution)/shard_map/ppermute | solution.py:71
  45.0 12.5 %all-to-all-start = ((f32[16,16,256]{2,1,0:T(8,128)}), f32[16,16,256]{2,1,0:T(8,128)S(1)}, u32[]{:S(2)}, u32[]{:S(2)}) async-start(f32[16,16,256]{2,1,0:T(8,128)} %bitcast.5.refs_1_), calls=%async_computation | async-start | bytes 524288 | tf_op jit(solution)/shard_map/all_to_all | solution.py:407
  50.8 1.1 copy-start.7
  55.9 3.9 %collective-permute-start.7 = (f32[2,128,128]{2,1,0:T(8,128)S(1)}, f32[2,128,128]{2,1,0:T(8,128)S(1)}, u32[]{:S(2)}, u32[]{:S(2)}) collective-permute-start(f32[2,128,128]{2,1,0:T(8,128)S(1)} %get-tuple-element.24), channel_id=1, source_target_pairs={{0,32},{32,0},{64,96},{96,64},{128,160},{160,128},{192,224},{224,1... | collective-permute-start | bytes 393224 | tf_op jit(solution)/shard_map/ppermute | solution.py:71
  60.5 16.7 %copy-start.1 = (f32[2,128,128]{2,1,0:T(8,128)S(1)}, f32[2,128,128]{2,1,0:T(8,128)}, u32[]{:S(2)}) copy-start(f32[2,128,128]{2,1,0:T(8,128)} %refs_1_.1) | copy-start | bytes 393220
  60.5 21.1 %all-to-all-start.1 = ((f32[8,16,256]{2,1,0:T(8,128)}), f32[8,16,256]{2,1,0:T(8,128)S(1)}, u32[]{:S(2)}, u32[]{:S(2)}) async-start(f32[8,16,256]{2,1,0:T(8,128)} %sum_repeat.4.refs_0_), calls=%async_computation.1 | async-start | bytes 262144 | tf_op jit(solution)/shard_map/all_to_all | solution.py:411
  68.9 8.3 %collective-permute-start.8 = (f32[2,128,128]{2,1,0:T(8,128)S(1)}, f32[2,128,128]{2,1,0:T(8,128)S(1)}, u32[]{:S(2)}, u32[]{:S(2)}) collective-permute-start(f32[2,128,128]{2,1,0:T(8,128)S(1)} %get-tuple-element.26), channel_id=1, source_target_pairs={{32,64},{64,32},{96,128},{128,96},{160,192},{192,160},{33,65},{65,... | collective-permute-start | bytes 393224 | tf_op jit(solution)/shard_map/ppermute | solution.py:71
  77.2 9.7 %collective-permute-start.11 = (f32[2,128,128]{2,1,0:T(8,128)S(1)}, f32[2,128,128]{2,1,0:T(8,128)S(1)}, u32[]{:S(2)}, u32[]{:S(2)}) collective-permute-start(f32[2,128,128]{2,1,0:T(8,128)S(1)} %renew.2.refs_0_.refs_3_), channel_id=1, source_target_pairs={{32,64},{64,32},{96,128},{128,96},{160,192},{192,160},{33,65},{65,... | collective-permute-start | bytes 393224 | tf_op jit(solution)/shard_map/ppermute | solution.py:71
  79.4 8.9 %collective-permute-start.10 = (f32[2,128,128]{2,1,0:T(8,128)S(1)}, f32[2,128,128]{2,1,0:T(8,128)S(1)}, u32[]{:S(2)}, u32[]{:S(2)}) collective-permute-start(f32[2,128,128]{2,1,0:T(8,128)S(1)} %renew.2.refs_0_.refs_3_), channel_id=1, source_target_pairs={{0,32},{32,0},{64,96},{96,64},{128,160},{160,128},{192,224},{224,1... | collective-permute-start | bytes 393224 | tf_op jit(solution)/shard_map/ppermute | solution.py:71
  82.3 15.5 %all-to-all-start.2 = ((f32[16,16,256]{2,1,0:T(8,128)}), f32[16,16,256]{2,1,0:T(8,128)S(1)}, u32[]{:S(2)}, u32[]{:S(2)}) async-start(f32[16,16,256]{2,1,0:T(8,128)} %sum_repeat.5.refs_0_), calls=%async_computation.2 | async-start | bytes 524288 | tf_op jit(solution)/shard_map/all_to_all | solution.py:417
  86.9 20.0 %copy-start.13 = (bf16[256,512]{1,0:T(8,128)(2,1)S(1)}, bf16[256,512]{1,0:T(8,128)(2,1)}, u32[]{:S(2)}) copy-start(bf16[256,512]{1,0:T(8,128)(2,1)} %constant.18.clone.refs_9_) | copy-start | bytes 786436
  88.8 17.3 %collective-permute-start.13 = (f32[2,384,128]{2,1,0:T(8,128)S(1)}, f32[2,384,128]{2,1,0:T(8,128)S(1)}, u32[]{:S(2)}, u32[]{:S(2)}) collective-permute-start(f32[2,384,128]{2,1,0:T(8,128)S(1)} %stack.23.refs_5_), channel_id=1, source_target_pairs={{1,2},{2,1},{3,4},{4,3},{5,6},{6,5},{7,8},{8,7},{9,10},{10,9},{11,... | collective-permute-start | bytes 1179656 | tf_op jit(solution)/shard_map/ppermute | solution.py:71
  97.8 8.4 %collective-permute-start.12 = (f32[2,384,128]{2,1,0:T(8,128)S(1)}, f32[2,384,128]{2,1,0:T(8,128)S(1)}, u32[]{:S(2)}, u32[]{:S(2)}) collective-permute-start(f32[2,384,128]{2,1,0:T(8,128)S(1)} %stack.23.refs_5_), channel_id=1, source_target_pairs={{0,1},{1,0},{2,3},{3,2},{4,5},{5,4},{6,7},{7,6},{8,9},{9,8},{10,11... | collective-permute-start | bytes 1179656 | tf_op jit(solution)/shard_map/ppermute | solution.py:71
  97.9 9.0 %collective-permute-start.9 = (f32[256,256]{1,0:T(8,128)S(1)}, f32[256,256]{1,0:T(8,128)S(1)}, u32[]{:S(2)}, u32[]{:S(2)}) collective-permute-start(f32[256,256]{1,0:T(8,128)S(1)} %bitcast.15), channel_id=1, source_target_pairs={{0,1},{1,0},{2,3},{3,2},{4,5},{5,4},{6,7},{7,6},{8,9},{9,8},{10,11... | collective-permute-start | bytes 786440 | tf_op jit(solution)/shard_map/ppermute | solution.py:71
  106.1 0.7 copy-start.8
  106.9 1.0 copy-start.9
  115.3 2.4 %copy-start.3 = (f32[2,384,128]{2,1,0:T(8,128)}, f32[2,384,128]{2,1,0:T(8,128)S(1)}, u32[]{:S(2)}) copy-start(f32[2,384,128]{2,1,0:T(8,128)S(1)} %get-tuple-element.30.refs_0_) | copy-start | bytes 1179652
  115.3 2.4 %copy-start.10 = (f32[2,384,128]{2,1,0:T(8,128)}, f32[2,384,128]{2,1,0:T(8,128)S(1)}, u32[]{:S(2)}) copy-start(f32[2,384,128]{2,1,0:T(8,128)S(1)} %get-tuple-element.29) | copy-start | bytes 1179652
  115.3 1.6 collective-permute-start.15
  117.7 8.0 %copy-start.11 = (f32[2,384,128]{2,1,0:T(8,128)S(1)}, f32[2,384,128]{2,1,0:T(8,128)}, u32[]{:S(2)}) copy-start(f32[2,384,128]{2,1,0:T(8,128)} %copy-done.10) | copy-start | bytes 1179652
  117.7 14.3 %all-to-all-start.3 = ((f32[16,16,256]{2,1,0:T(8,128)}), f32[16,16,256]{2,1,0:T(8,128)S(1)}, u32[]{:S(2)}, u32[]{:S(2)}) async-start(f32[16,16,256]{2,1,0:T(8,128)} %bitcast.7.refs_1_), calls=%async_computation.3 | async-start | bytes 524288 | tf_op jit(solution)/shard_map/all_to_all | solution.py:407
  125.7 14.4 %collective-permute-start.14 = (f32[2,384,128]{2,1,0:T(8,128)S(1)}, f32[2,384,128]{2,1,0:T(8,128)S(1)}, u32[]{:S(2)}, u32[]{:S(2)}) collective-permute-start(f32[2,384,128]{2,1,0:T(8,128)S(1)} %copy-done.11), channel_id=1, source_target_pairs={{0,1},{1,0},{2,3},{3,2},{4,5},{5,4},{6,7},{7,6},{8,9},{9,8},{10,11... | collective-permute-start | bytes 1179656 | tf_op jit(solution)/shard_map/ppermute | solution.py:71
  126.7 13.7 %collective-permute-start.16 = (f32[2,384,128]{2,1,0:T(8,128)}, f32[2,384,128]{2,1,0:T(8,128)S(1)}, u32[]{:S(2)}, u32[]{:S(2)}) collective-permute-start(f32[2,384,128]{2,1,0:T(8,128)} %hold.3), channel_id=1, source_target_pairs={{1,2},{2,1},{3,4},{4,3},{5,6},{6,5},{7,8},{8,7},{9,10},{10,9},{11,... | collective-permute-start | bytes 1179656 | tf_op jit(solution)/shard_map/ppermute | solution.py:71
  132.7 13.4 %all-to-all-start.4 = ((f32[8,16,256]{2,1,0:T(8,128)}), f32[8,16,256]{2,1,0:T(8,128)S(1)}, u32[]{:S(2)}, u32[]{:S(2)}) async-start(f32[8,16,256]{2,1,0:T(8,128)} %sum_repeat.6), calls=%async_computation.4 | async-start | bytes 262144 | tf_op jit(solution)/shard_map/all_to_all | solution.py:411
  141.1 5.1 %collective-permute-start.17 = (f32[2,128,128]{2,1,0:T(8,128)S(1)}, f32[2,128,128]{2,1,0:T(8,128)S(1)}, u32[]{:S(2)}, u32[]{:S(2)}) collective-permute-start(f32[2,128,128]{2,1,0:T(8,128)S(1)} %get-tuple-element.33), channel_id=1, source_target_pairs={{0,32},{32,0},{64,96},{96,64},{128,160},{160,128},{192,224},{224,1... | collective-permute-start | bytes 393224 | tf_op jit(solution)/shard_map/ppermute | solution.py:71
  146.9 13.1 %all-to-all-start.5 = ((f32[16,16,256]{2,1,0:T(8,128)}), f32[16,16,256]{2,1,0:T(8,128)S(1)}, u32[]{:S(2)}, u32[]{:S(2)}) async-start(f32[16,16,256]{2,1,0:T(8,128)} %sum_repeat.7), calls=%async_computation.5 | async-start | bytes 524288 | tf_op jit(solution)/shard_map/all_to_all | solution.py:417
  152.0 7.4 %collective-permute-start.18 = (f32[2,128,128]{2,1,0:T(8,128)S(1)}, f32[2,128,128]{2,1,0:T(8,128)S(1)}, u32[]{:S(2)}, u32[]{:S(2)}) collective-permute-start(f32[2,128,128]{2,1,0:T(8,128)S(1)} %get-tuple-element.35), channel_id=1, source_target_pairs={{32,64},{64,32},{96,128},{128,96},{160,192},{192,160},{33,65},{65,... | collective-permute-start | bytes 393224 | tf_op jit(solution)/shard_map/ppermute | solution.py:71
  160.0 0.9 copy-start
  161.0 5.2 %collective-permute-start.19 = (f32[256,256]{1,0:T(8,128)S(1)}, f32[256,256]{1,0:T(8,128)S(1)}, u32[]{:S(2)}, u32[]{:S(2)}) collective-permute-start(f32[256,256]{1,0:T(8,128)S(1)} %relay.1.refs_2_), channel_id=1, source_target_pairs={{0,1},{1,0},{2,3},{3,2},{4,5},{5,4},{6,7},{7,6},{8,9},{9,8},{10,11... | collective-permute-start | bytes 786440 | tf_op jit(solution)/shard_map/ppermute | solution.py:71
